TPU v7x, 32 devices: a whole 2x2x4 slice. The times are simulated.
32 devices in a mesh: tgt: 4 (over y, core), src: 8 (over z, x).
Axes of the slice: x: 2, y: 2, z: 4, core: 2. Of those that a mesh axis runs over, the one named last changes fastest.
Arguments:
- shear_leaves: bfloat16 [8, 8, 128, 128], P('tgt', 'src'), may hold values from -2 to 2, as said below
- normal_leaves: bfloat16 [8, 8, 128, 128], P('tgt', 'src'), may hold values from -2 to 2, as said below
- near_flags: int32 [8, 8], P('tgt', 'src'), may hold values from 0 to 1, as said below
- ranks: int32 [8, 8], P('tgt', 'src'), may hold values from 16 to 64
- shear_traction: float32 [1024, 128], P(('tgt', 'src')), may hold values from -1 to 1
- normal_traction: float32 [1024, 128], P(('tgt', 'src')), may hold values from 0.5 to 4
- state: float32 [1024, 128], P(('tgt', 'src')), may hold values from -0.5 to 0.5
- friction_a: float32 [1024, 128], P(('tgt', 'src')), may hold values from 1 to 2
- heal_rate: float32 [1024, 128], P(('tgt', 'src')), may hold values from 0.1 to 0.5
Outputs:
- shear_out: float32 [1024, 128], P(('tgt', 'src'))
- normal_out: float32 [1024, 128], P(('tgt', 'src'))
- state_out: float32 [1024, 128], P(('tgt', 'src'))
Inputs may be any that keep to these rules, and one draw needn't show every extreme that they name: `near_flags`: every leaf with equal leaf row and leaf column is 1, and a 1 stands only where the leaf row and the leaf column differ by at most 1. `shear_leaves`: columns 0 to 63 of an admissible leaf hold its factor U, columns 64 onward its factor V. `normal_leaves`: columns 0 to 63 of an admissible leaf hold its factor U, columns 64 onward its factor V.
All inputs are finite; a program needn't handle non-finite values.
Results may differ from a plain program's by a relative error of at most 0.002.
Values may be sent and summed in bfloat16 or wider, within the bound.
No kernel may reach another device: no remote copies, remote signals or barrier semaphores. Data moves between devices by JAX's collectives and lax.ppermute only.
A program may use at most 64 MiB of HBM per device.

v0:
```python
import jax
import jax.numpy as jnp
from jax import lax
from jax.sharding import PartitionSpec as P

RMAX = 64
BLK = 128


time_step = 0.25


def spread(block, axis, owner):
    block = jnp.where(lax.axis_index(axis) == owner, block, jnp.zeros_like(block))
    return lax.psum(block, axis)


def kernel_terms(leaves, near_flags, ranks, source):
    leaf_rows, leaf_cols = near_flags.shape
    members = source.shape[-1]
    blocks = source.reshape(leaf_cols, BLK, members)
    factor_u = leaves[:, :, :, :RMAX]
    factor_v = leaves[:, :, :, RMAX:]
    inner = jnp.einsum("rcjk,cjn->rckn", factor_v, blocks, preferred_element_type=jnp.float32)
    keep_mask = (jnp.arange(RMAX, dtype=jnp.int32)[None, None, :] < ranks[:, :, None]) & (
        near_flags[:, :, None] == 0
    )
    inner = jnp.where(keep_mask[:, :, :, None], inner, 0.0).astype(jnp.bfloat16)
    lowrank = jnp.einsum("rcik,rckn->rin", factor_u, inner, preferred_element_type=jnp.float32)
    masked = jnp.where((near_flags == 1)[:, :, None, None], leaves, jnp.zeros((), leaves.dtype))
    dense_sum = jnp.einsum("rcij,cjn->rin", masked, blocks, preferred_element_type=jnp.float32)
    return (lowrank + dense_sum).reshape(leaf_rows * BLK, members)


def to_source(block_rows, leaf_rows, leaf_cols, src_index):
    first_leaf = src_index * leaf_cols
    offset = first_leaf % leaf_rows * BLK
    owner = first_leaf // leaf_rows
    piece = lax.dynamic_slice_in_dim(block_rows, offset, leaf_cols * BLK, 0)
    return spread(piece, "tgt", owner)


def friction(shear_now, normal_now, state_now, friction_a):
    effective = jnp.maximum(normal_now, 1.0)
    slip_rate = (
        2.0 * jnp.exp(-state_now / friction_a) * jnp.sinh(shear_now / (friction_a * effective))
    )
    return (slip_rate, (slip_rate - 1.0).astype(jnp.bfloat16))


def advance(rates, start):
    first_rates = rates(*start)
    first = tuple((value + time_step * change for value, change in zip(start, first_rates)))
    second_rates = rates(*first)
    second = tuple(
        (
            0.75 * begin + 0.25 * (value + time_step * change)
            for begin, value, change in zip(start, first, second_rates)
        )
    )
    third_rates = rates(*second)
    return tuple(
        (
            begin / 3.0 + 2.0 / 3.0 * (value + time_step * change)
            for begin, value, change in zip(start, second, third_rates)
        )
    )


def per_device(
    shear_leaves,
    normal_leaves,
    near_flags,
    ranks,
    shear_traction,
    normal_traction,
    state,
    friction_a,
    heal_rate,
):
    leaf_rows, leaf_cols = near_flags.shape
    src_index = lax.axis_index("src")
    own_count = shear_traction.shape[0]

    def both_kernels(block_rows):
        source = to_source(block_rows, leaf_rows, leaf_cols, src_index)
        shear_part = kernel_terms(shear_leaves, near_flags, ranks, source)
        normal_part = kernel_terms(normal_leaves, near_flags, ranks, source)
        return (shear_part, normal_part)

    block_shear, block_normal, block_state, block_a, block_heal = (
        lax.all_gather(shear_traction, "src", axis=0, tiled=True),
        lax.all_gather(normal_traction, "src", axis=0, tiled=True),
        lax.all_gather(state, "src", axis=0, tiled=True),
        lax.all_gather(friction_a, "src", axis=0, tiled=True),
        lax.all_gather(heal_rate, "src", axis=0, tiled=True),
    )

    def block_rates(shear_now, normal_now, state_now):
        slip_rate, deviation = friction(shear_now, normal_now, state_now, block_a)
        shear_part, normal_part = both_kernels(deviation)
        shear_rate, normal_rate = lax.psum((shear_part, normal_part), "src")
        return (shear_rate, normal_rate, block_heal * (jnp.exp(-state_now) - slip_rate))

    result = advance(block_rates, (block_shear, block_normal, block_state))
    start_row = src_index * own_count
    outputs = tuple((lax.dynamic_slice_in_dim(value, start_row, own_count, 0) for value in result))
    return (outputs[0], outputs[1], outputs[2])


def solution(mesh):
    in_specs = (
        P("tgt", "src", None, None),
        P("tgt", "src", None, None),
        P("tgt", "src"),
        P("tgt", "src"),
        P(("tgt", "src"), None),
        P(("tgt", "src"), None),
        P(("tgt", "src"), None),
        P(("tgt", "src"), None),
        P(("tgt", "src"), None),
    )
    out_specs = (P(("tgt", "src"), None), P(("tgt", "src"), None), P(("tgt", "src"), None))
    return jax.shard_map(
        per_device, mesh=mesh, in_specs=in_specs, out_specs=out_specs, check_vma=False
    )
```

profile of v0, /device:TPU:0, one launch (start us, length us, event | category | flops | bytes accessed | tf_op | source)
XLA Modules:
  0.0 397.3 jit_solution(17154584748902754204)
XLA Ops:
  7.2 0.6 copy-done.9
  7.9 1.0 slice.8
  9.0 0.6 copy-done.4
  9.6 32.4 %all_gather.15 = f32[256,128]{1,0:T(8,128)S(1)} all-gather(f32[32,128]{1,0:T(8,128)S(1)} %copy-done.4), channel_id=1, replica_groups=mesh['tgt'=4,'src'=8] {'src'}, dimensions={0}, use_global_device_ids=true | all-gather | bytes 147456 | tf_op jit(solution)/shard_map/all_gather | solution.py:92
  42.0 30.6 %all_gather.18 = f32[256,128]{1,0:T(8,128)S(1)} all-gather(f32[32,128]{1,0:T(8,128)S(1)} %copy-done.5), channel_id=1, replica_groups=mesh['tgt'=4,'src'=8] {'src'}, dimensions={0}, use_global_device_ids=true | all-gather | bytes 147456 | tf_op jit(solution)/shard_map/all_gather | solution.py:93
  72.7 30.6 %all_gather.16 = f32[256,128]{1,0:T(8,128)S(1)} all-gather(f32[32,128]{1,0:T(8,128)S(1)} %copy-done.6), channel_id=1, replica_groups=mesh['tgt'=4,'src'=8] {'src'}, dimensions={0}, use_global_device_ids=true | all-gather | bytes 147456 | tf_op jit(solution)/shard_map/all_gather | solution.py:94
  103.3 30.5 %all_gather.17 = f32[256,128]{1,0:T(8,128)S(1)} all-gather(f32[32,128]{1,0:T(8,128)S(1)} %copy-done.7), channel_id=1, replica_groups=mesh['tgt'=4,'src'=8] {'src'}, dimensions={0}, use_global_device_ids=true | all-gather | bytes 147456 | tf_op jit(solution)/shard_map/all_gather | solution.py:95
  134.0 10.3 %psum.63 = bf16[128,128]{1,0:T(8,128)(2,1)S(1)} all-reduce(bf16[128,128]{1,0:T(8,128)(2,1)S(1)} %fusion.54), channel_id=1, replica_groups=mesh['tgt'=4,'src'=8] {'tgt'}, use_global_device_ids=true, to_apply=%region_0.1 | all-reduce | flops 16384 | bytes 65536 | tf_op jit(solution)/shard_map/psum | solution.py:15
  144.3 0.2 fusion.28
  144.5 0.6 copy-done.1
  145.8 0.7 copy-done.10
  146.6 0.9 fusion.1
  147.5 0.9 fusion
  148.4 0.6 copy-done.8
  149.0 30.5 %all_gather.19 = f32[256,128]{1,0:T(8,128)S(1)} all-gather(f32[32,128]{1,0:T(8,128)S(1)} %copy-done.8), channel_id=1, replica_groups=mesh['tgt'=4,'src'=8] {'src'}, dimensions={0}, use_global_device_ids=true | all-gather | bytes 147456 | tf_op jit(solution)/shard_map/all_gather | solution.py:96
  179.6 40.9 %all-reduce.11.cloned.1.call-done = (f32[256,128]{1,0:T(8,128)}, f32[256,128]{1,0:T(8,128)}) async-done(((f32[256,128]{1,0:T(8,128)}, f32[256,128]{1,0:T(8,128)}), (f32[256,128]{1,0:T(8,128)}, f32[256,128]{1,0:T(8,128)})) %all-reduce.11.cloned.1.call-update) | async-done | bytes 262160 | tf_op jit(solution)/shard_map/psum | solution.py:102
  220.5 1.2 negate_exponential_fusion
  221.8 10.3 %psum.66 = bf16[128,128]{1,0:T(8,128)(2,1)S(1)} all-reduce(bf16[128,128]{1,0:T(8,128)(2,1)S(1)} %fusion.55), channel_id=1, replica_groups=mesh['tgt'=4,'src'=8] {'tgt'}, use_global_device_ids=true, to_apply=%region_3.4 | all-reduce | flops 16384 | bytes 65536 | tf_op jit(solution)/shard_map/psum | solution.py:15
  232.3 0.2 fusion.26
  232.5 0.2 fusion.32
  232.7 0.9 fusion.3
  233.6 0.9 fusion.2
  234.6 70.4 %all-reduce.9.cloned.1.call-done = (f32[256,128]{1,0:T(8,128)}, f32[256,128]{1,0:T(8,128)}) async-done(((f32[256,128]{1,0:T(8,128)}, f32[256,128]{1,0:T(8,128)}), (f32[256,128]{1,0:T(8,128)}, f32[256,128]{1,0:T(8,128)})) %all-reduce.9.cloned.1.call-update) | async-done | bytes 262160 | tf_op jit(solution)/shard_map/psum | solution.py:102
  305.0 1.2 fusion.14
  306.2 10.3 %psum.69 = bf16[128,128]{1,0:T(8,128)(2,1)S(1)} all-reduce(bf16[128,128]{1,0:T(8,128)(2,1)S(1)} %fusion.56), channel_id=1, replica_groups=mesh['tgt'=4,'src'=8] {'tgt'}, use_global_device_ids=true, to_apply=%region_6.7 | all-reduce | flops 16384 | bytes 65536 | tf_op jit(solution)/shard_map/psum | solution.py:15
  316.8 0.2 fusion.24
  317.0 0.2 fusion.30
  317.2 0.9 fusion.5
  318.1 0.9 fusion.4
  319.0 0.6 fusion.75
  319.6 69.8 %all-reduce.7.cloned.1.call-done = (f32[256,128]{1,0:T(8,128)}, f32[256,128]{1,0:T(8,128)}) async-done(((f32[256,128]{1,0:T(8,128)}, f32[256,128]{1,0:T(8,128)}), (f32[256,128]{1,0:T(8,128)}, f32[256,128]{1,0:T(8,128)})) %all-reduce.7.cloned.1.call-update) | async-done | bytes 262160 | tf_op jit(solution)/shard_map/psum | solution.py:102
  389.4 1.4 fusion.78
  (39 shorter events, 1.8 us)
Async XLA Ops:
  7.2 213.4 %all-reduce.11.cloned.1.call-start = ((), (), s32[]{:S(2)}) async-start(), calls=%async_computation.2 | async-start | bytes 524288 | tf_op jit(solution)/shard_map/psum | solution.py:102
  7.2 0.7 copy-start.9
  7.9 1.0 copy-start
  8.9 0.7 copy-start.4
  9.6 32.4 %copy-start.5 = (f32[32,128]{1,0:T(8,128)S(1)}, f32[32,128]{1,0:T(8,128)}, u32[]{:S(2)}) copy-start(f32[32,128]{1,0:T(8,128)} %param.14) | copy-start | bytes 49156
  42.0 30.6 %copy-start.6 = (f32[32,128]{1,0:T(8,128)S(1)}, f32[32,128]{1,0:T(8,128)}, u32[]{:S(2)}) copy-start(f32[32,128]{1,0:T(8,128)} %param.15) | copy-start | bytes 49156
  72.7 30.6 %copy-start.7 = (f32[32,128]{1,0:T(8,128)S(1)}, f32[32,128]{1,0:T(8,128)}, u32[]{:S(2)}) copy-start(f32[32,128]{1,0:T(8,128)} %param.16) | copy-start | bytes 49156
  144.3 0.8 copy-start.1
  145.8 0.7 copy-start.10
  148.3 0.7 copy-start.8
  148.4 156.6 %all-reduce.9.cloned.1.call-start = ((), (), s32[]{:S(2)}) async-start(), calls=%async_computation.1 | async-start | bytes 524288 | tf_op jit(solution)/shard_map/psum | solution.py:102
  234.5 70.5 %copy-start.2 = (f32[256,128]{1,0:T(8,128)S(1)}, f32[256,128]{1,0:T(8,128)}, u32[]{:S(2)}) copy-start(f32[256,128]{1,0:T(8,128)} %get-tuple-element.7) | copy-start | bytes 393220
  234.5 70.5 %copy-start.3 = (f32[256,128]{1,0:T(8,128)S(1)}, f32[256,128]{1,0:T(8,128)}, u32[]{:S(2)}) copy-start(f32[256,128]{1,0:T(8,128)} %get-tuple-element.8) | copy-start | bytes 393220
  234.5 154.9 %all-reduce.7.cloned.1.call-start = ((), (), s32[]{:S(2)}) async-start(), calls=%async_computation | async-start | bytes 524288 | tf_op jit(solution)/shard_map/psum | solution.py:102
Sparse Core Ops, SparseCore 0:
  148.5 72.0 all-reduce.10
  234.6 70.3 all-reduce.8
  319.1 70.2 all-reduce.6
where the time goes:
time: 398 us; the launch traced here: 397 us
  blocking collectives  186 us (47%)
  waiting for transfers between devices  181 us (45%)
  between operations  13.9 us (3%)
  matrix products  7.3 us (2%)
  other arithmetic  4.69 us (1%)
  local copies, waits for them, and re-layouts  4.47 us (1%)
    psum x3, waiting for transfers between devices, block_rates(): shear_rate, normal_rate = lax.psum((shear_part, normal_part), 'src')  181 us
    all_gather x1, blocking collectives, per_device(): lax.all_gather(shear_traction, 'src', axis=0, tiled=True)  32.4 us
    psum x3, blocking collectives, spread(): return lax.psum(block, axis)  30.8 us
    all_gather x1, blocking collectives, per_device(): lax.all_gather(normal_traction, 'src', axis=0, tiled=True)  30.6 us
    all_gather x1, blocking collectives, per_device(): lax.all_gather(state, 'src', axis=0, tiled=True)  30.6 us
    all_gather x1, blocking collectives, per_device(): lax.all_gather(heal_rate, 'src', axis=0, tiled=True)  30.5 us
    all_gather x1, blocking collectives, per_device(): lax.all_gather(friction_a, 'src', axis=0, tiled=True)  30.5 us
  transfers between devices with their start and end apart: 3, of which 3 were waited for; matrix products, arithmetic and copies ran while one was open for 0% of the time, Pallas kernels for 0%

commit v1 on v0

v1 whole, which is shorter than its diff:
```python
import functools

import jax
import jax.numpy as jnp
from jax import lax
from jax.experimental import pallas as pl
from jax.experimental.pallas import tpu as pltpu
from jax.sharding import PartitionSpec as P

time_step = 0.25
VMEM = pl.BlockSpec(memory_space=pltpu.VMEM)


def friction(shear_now, normal_now, state_now, friction_a):
    drive = shear_now / (friction_a * jnp.maximum(normal_now, 1.0))
    decay = state_now / friction_a
    return jnp.exp(drive - decay) - jnp.exp(-drive - decay)


def send_copies(dev_ref, slip_rate):
    deviation = (slip_rate - 1.0).astype(jnp.bfloat16)
    dev_ref[...] = jnp.broadcast_to(deviation[None], dev_ref.shape)


def prepare_kernel(near_ref, rank_ref, shear_ref, normal_ref, s_ref, n_ref, p_ref, a_ref, strips_ref, dev_ref):
    leaf_rows, leaf_cols, block, _ = shear_ref.shape
    half = block // 2
    own = s_ref.shape[0]
    rank_ids = lax.broadcasted_iota(jnp.int32, (block, half), 1)
    per_leaf = block // own
    for row in range(leaf_rows):
        for col in range(leaf_cols):
            near = near_ref[row : row + 1, col : col + 1] == 1
            for which, leaves in enumerate((shear_ref, normal_ref)):
                leaf = leaves[row, col]
                factor_u = jnp.where(rank_ids < rank_ref[row : row + 1, col : col + 1], leaf[:, :half].astype(jnp.float32), 0.0)
                product = lax.dot_general(
                    factor_u.astype(jnp.bfloat16),
                    leaf[:, half:],
                    (((1,), (1,)), ((), ())),
                    preferred_element_type=jnp.float32,
                )
                dense = jnp.where(near, leaf.astype(jnp.float32), product).astype(jnp.bfloat16)
                for part in range(per_leaf):
                    strips_ref[row * per_leaf + part, which * own : (which + 1) * own, col * block : (col + 1) * block] = (
                        dense[part * own : (part + 1) * own]
                    )
    send_copies(dev_ref, friction(s_ref[...], n_ref[...], p_ref[...], a_ref[...]))


def stage_kernel(stage, strips_ref, all_dev_ref, *refs):
    if stage == 0:
        s0_ref, n0_ref, p0_ref, a_ref, h_ref = refs[:5]
        begin = now = (s0_ref[...], n0_ref[...], p0_ref[...])
        outs = refs[5:]
    else:
        s0_ref, n0_ref, p0_ref, a_ref, h_ref, s_ref, n_ref, p_ref = refs[:8]
        begin = (s0_ref[...], n0_ref[...], p0_ref[...])
        now = (s_ref[...], n_ref[...], p_ref[...])
        outs = refs[8:]
    friction_a = a_ref[...]
    own = friction_a.shape[0]
    pieces, _, width = strips_ref.shape
    total = jnp.zeros((2 * own, friction_a.shape[1]), jnp.float32)
    for piece in range(pieces):
        total += jnp.dot(
            strips_ref[piece], all_dev_ref[piece * width : (piece + 1) * width], preferred_element_type=jnp.float32
        )
    slip_rate = friction(*now, friction_a)
    rates = (total[:own], total[own:], h_ref[...] * (jnp.exp(-now[2]) - slip_rate))
    moved = tuple(value + time_step * change for value, change in zip(now, rates))
    if stage == 1:
        moved = tuple(0.75 * start + 0.25 * value for start, value in zip(begin, moved))
    elif stage == 2:
        moved = tuple(start / 3.0 + (2.0 / 3.0) * value for start, value in zip(begin, moved))
    for out, value in zip(outs, moved):
        out[...] = value
    if stage < 2:
        send_copies(outs[3], friction(*moved, friction_a))


def per_device(
    shear_leaves, normal_leaves, near_flags, ranks, shear_traction, normal_traction, state, friction_a, heal_rate
):
    leaf_rows, leaf_cols, block, _ = shear_leaves.shape
    own, members = state.shape
    sources = lax.axis_size("src")
    devices = sources * lax.axis_size("tgt")
    row_type = jax.ShapeDtypeStruct((own, members), jnp.float32)
    copies_type = jax.ShapeDtypeStruct((devices, own, members), jnp.bfloat16)

    strips, copies = pl.pallas_call(
        prepare_kernel,
        out_shape=(jax.ShapeDtypeStruct((sources, 2 * own, leaf_cols * block), jnp.bfloat16), copies_type),
        in_specs=[VMEM] * 8,
        out_specs=(VMEM, VMEM),
    )(near_flags, ranks, shear_leaves, normal_leaves, shear_traction, normal_traction, state, friction_a)
    strips = lax.all_to_all(strips, "src", 0, 0, tiled=True)

    begin = (shear_traction, normal_traction, state)
    now = ()
    for stage in range(3):
        all_dev = lax.all_to_all(copies, ("tgt", "src"), 0, 0, tiled=True).reshape(devices * own, members)
        given = (strips, all_dev, *begin, friction_a, heal_rate, *now)
        outs = pl.pallas_call(
            functools.partial(stage_kernel, stage),
            out_shape=(row_type,) * 3 + ((copies_type,) if stage < 2 else ()),
            in_specs=[VMEM] * len(given),
            out_specs=(VMEM,) * (4 if stage < 2 else 3),
        )(*given)
        now = outs[:3]
        if stage < 2:
            copies = outs[3]
    return tuple(now)


def solution(mesh):
    rows = P(("tgt", "src"), None)
    leaves = P("tgt", "src", None, None)
    flags = P("tgt", "src")
    return jax.shard_map(
        per_device,
        mesh=mesh,
        in_specs=(leaves, leaves, flags, flags) + (rows,) * 5,
        out_specs=(rows,) * 3,
        check_vma=False,
    )
```

time: 398 us -> 66.6 us (0.17)
  waiting for transfers between devices: 181 us -> 0 us
  blocking collectives: 186 us -> 55.7 us
  between operations: 13.9 us -> 0.64 us
  Pallas kernels: 0 us -> 7.72 us
  matrix products: 7.3 us -> 0 us
  other arithmetic: 4.69 us -> 0 us
    psum x3 -> x0, waiting for transfers between devices: 181 us -> none  [block_rates(): shear_rate, normal_rate = lax.psum((shear_part, normal_part), 'src')]
    all_gather x5 -> x0, blocking collectives: 155 us -> none  [the longest x1 32.4 us: per_device(): lax.all_gather(shear_traction, 'src', axis=0, tiled=True)]
    all_to_all x0 -> x4, blocking collectives: none -> 55.7 us  [the longest x3 40.9 us: per_device(): lax.all_to_all(copies, ('tgt', 'src'), 0, 0, tiled=True)]
    psum x3 -> x0, blocking collectives: 30.8 us -> none  [spread(): return lax.psum(block, axis)]
    pallas_call x0 -> x4, Pallas kernels: none -> 7.72 us  [the longest x3 5.83 us: per_device(): pl.pallas_call(functools.partial(stage_kernel, stage), out_shape=(row_typ...]
    dot_general x12 -> x0, matrix products: 6.51 us -> none  [the longest x6 5.25 us: kernel_terms(): jnp.einsum('rcik,rckn->rin', factor_u, inner, preferred_element_type=jnp....]
  transfers between devices with their start and end apart: 3 -> 0, of which waited for: 3 -> 0; matrix products, arithmetic and copies ran while one was open for 0% -> 0% of each run, Pallas kernels for 0% -> 0%
where the time goes in v1:
time: 66.6 us; the launch traced here: 66 us
  blocking collectives  55.7 us (84%)
  Pallas kernels  7.72 us (12%)
  local copies, waits for them, and re-layouts  1.96 us (3%)
    all_to_all x3, blocking collectives, per_device(): lax.all_to_all(copies, ('tgt', 'src'), 0, 0, tiled=True)  40.9 us
    all_to_all x1, blocking collectives, per_device(): strips = lax.all_to_all(strips, 'src', 0, 0, tiled=True)  14.8 us
    pallas_call x3, Pallas kernels, per_device(): pl.pallas_call(functools.partial(stage_kernel, stage), out_shape=(row_typ...  5.83 us
    unnamed x6, local copies, waits for them, and re-layouts  1.96 us
    pallas_call x1, Pallas kernels, per_device(): pl.pallas_call(prepare_kernel, out_shape=(jax.ShapeDtypeStruct((sources,...  1.88 us

profile of v1, /device:TPU:0, one launch (start us, length us, event | category | flops | bytes accessed | tf_op | source)
XLA Modules:
  0.0 66.0 jit_solution(1274713706642971164)
XLA Ops:
  0.6 0.0 copy-start.1
  0.6 1.3 %copy.12.near_ref = s32[2,1]{1,0:T(2,128)} copy(s32[2,1]{0,1:T(1,128)} %param.11) | data formatting | bytes 16 | tf_op args[2]
  1.9 0.0 copy-done.1
  1.9 0.6 copy.13.rank_ref
  2.6 1.9 %shard_map.112 = (bf16[8,64,128]{2,1,0:T(8,128)(2,1)}, bf16[32,32,128]{2,1,0:T(8,128)(2,1)}) custom-call(s32[2,1]{1,0:T(2,128)} %copy.12.near_ref, s32[2,1]{1,0:T(2,128)} %copy.13.rank_ref, bf16[2,1,128,128]{3,2,1,0:T(8,128)(2,1)} %shear_ref.1, bf16[2,1,128,128]{3,2,1,0:T(8,128)(2,1)} %normal_ref.1, f32[32,128]{1,0:T(8,128)} %refs_0_.5, f32[32,128]{1,0:T(8,128)} %refs_1_.5, ...), custom_call_target="tpu_custom_call" | custom-call | tf_op jit(solution)/shard_map/pallas_call | solution.py:92
  4.5 0.0 copy-start
  4.5 14.8 %all_to_all.20.strips_ref = bf16[8,64,128]{2,1,0:T(8,128)(2,1)} all-to-all(bf16[8,64,128]{2,1,0:T(8,128)(2,1)} %get-tuple-element.13), channel_id=1, replica_groups=mesh['tgt'=4,'src'=8] {'src'}, dimensions={0} | all-to-all | bytes 262144 | tf_op jit(solution)/shard_map/all_to_all | solution.py:98
  19.3 0.0 copy-done
  19.3 13.0 %all_to_all.21 = bf16[32,32,128]{2,1,0:T(8,128)(2,1)} all-to-all(bf16[32,32,128]{2,1,0:T(8,128)(2,1)S(1)} %copy-done), channel_id=1, replica_groups=mesh['tgt'=4,'src'=8] {'tgt','src'}, dimensions={0} | all-to-all | bytes 524288 | tf_op jit(solution)/shard_map/all_to_all | solution.py:103
  32.3 2.0 %shard_map.113 = (f32[32,128]{1,0:T(8,128)}, f32[32,128]{1,0:T(8,128)}, f32[32,128]{1,0:T(8,128)}, bf16[32,32,128]{2,1,0:T(8,128)(2,1)}) custom-call(bf16[8,64,128]{2,1,0:T(8,128)(2,1)} %all_to_all.20.strips_ref, bf16[1024,128]{1,0:T(8,128)(2,1)} %bitcast.5, f32[32,128]{1,0:T(8,128)} %refs_0_.5, f32[32,128]{1,0:T(8,128)} %refs_1_.5, f32[32,128]{1,0:T(8,128)} %refs_2_.5, ...), custom_call_target="tpu_custom_call" | custom-call | tf_op jit(solution)/shard_map/pallas_call | solution.py:105
  34.3 13.9 %all_to_all.22 = bf16[32,32,128]{2,1,0:T(8,128)(2,1)} all-to-all(bf16[32,32,128]{2,1,0:T(8,128)(2,1)} %get-tuple-element.15), channel_id=1, replica_groups=mesh['tgt'=4,'src'=8] {'tgt','src'}, dimensions={0} | all-to-all | bytes 524288 | tf_op jit(solution)/shard_map/all_to_all | solution.py:103
  48.2 2.0 %shard_map.114 = (f32[32,128]{1,0:T(8,128)}, f32[32,128]{1,0:T(8,128)}, f32[32,128]{1,0:T(8,128)}, bf16[32,32,128]{2,1,0:T(8,128)(2,1)}) custom-call(bf16[8,64,128]{2,1,0:T(8,128)(2,1)} %all_to_all.20.strips_ref, bf16[1024,128]{1,0:T(8,128)(2,1)} %bitcast.3, f32[32,128]{1,0:T(8,128)} %refs_0_.5, f32[32,128]{1,0:T(8,128)} %refs_1_.5, f32[32,128]{1,0:T(8,128)} %refs_2_.5, ...), custom_call_target="tpu_custom_call" | custom-call | tf_op jit(solution)/shard_map/pallas_call | solution.py:105
  50.2 13.9 %all_to_all.23 = bf16[32,32,128]{2,1,0:T(8,128)(2,1)} all-to-all(bf16[32,32,128]{2,1,0:T(8,128)(2,1)} %get-tuple-element.19), channel_id=1, replica_groups=mesh['tgt'=4,'src'=8] {'tgt','src'}, dimensions={0} | all-to-all | bytes 524288 | tf_op jit(solution)/shard_map/all_to_all | solution.py:103
  64.2 1.9 %shard_map.115 = (f32[32,128]{1,0:T(8,128)}, f32[32,128]{1,0:T(8,128)}, f32[32,128]{1,0:T(8,128)}) custom-call(bf16[8,64,128]{2,1,0:T(8,128)(2,1)} %all_to_all.20.strips_ref, bf16[1024,128]{1,0:T(8,128)(2,1)} %bitcast.4, f32[32,128]{1,0:T(8,128)} %refs_0_.5, f32[32,128]{1,0:T(8,128)} %refs_1_.5, f32[32,128]{1,0:T(8,128)} %refs_2_.5, f32[32,128]{1,0:T(8,128)} %refs_3_.5, ...), custom_call_target="tpu_custom_call" | custom-call | tf_op jit(solution)/shard_map/pallas_call | solution.py:105
Async XLA Ops:
  0.6 1.3 %copy-start.1 = (s32[2,1]{0,1:T(1,128)S(1)}, s32[2,1]{0,1:T(1,128)}, u32[]{:S(2)}) copy-start(s32[2,1]{0,1:T(1,128)} %param.12) | copy-start | bytes 28
  4.5 14.8 %copy-start = (bf16[32,32,128]{2,1,0:T(8,128)(2,1)S(1)}, bf16[32,32,128]{2,1,0:T(8,128)(2,1)}, u32[]{:S(2)}) copy-start(bf16[32,32,128]{2,1,0:T(8,128)(2,1)} %get-tuple-element.14) | copy-start | bytes 786436

commit v2 on v1

v2 whole, which is shorter than its diff:
```python
import functools

import jax
import jax.numpy as jnp
from jax import lax
from jax.experimental import pallas as pl
from jax.experimental.pallas import tpu as pltpu
from jax.sharding import PartitionSpec as P

time_step = 0.25
VMEM = pl.BlockSpec(memory_space=pltpu.VMEM)


def partner(index, step, count):
    return index ^ step if count & (count - 1) == 0 else (index + step) % count


def origin(index, step, count):
    return index ^ step if count & (count - 1) == 0 else (index + count - step) % count


def pair_of(sources):
    return 2 if sources % 2 == 0 else 1


def block_order(me, sources):
    pair = pair_of(sources)
    line = sources // pair
    far, near = me // pair, me % pair
    return [
        origin(far, step, line) * pair + origin(near, side, pair) for side in range(pair) for step in range(line)
    ]


def along_line(block, step):
    sources = lax.axis_size("src")
    pair = pair_of(sources)
    line = sources // pair
    moves = [(i, partner(i // pair, step, line) * pair + i % pair) for i in range(sources)]
    return lax.ppermute(block, "src", moves)


def across_pair(block):
    return lax.ppermute(block, "src", [(i, i ^ 1) for i in range(lax.axis_size("src"))])


def gather_source(block):
    sources = lax.axis_size("src")
    pair = pair_of(sources)
    blocks = [block] + [along_line(block, step) for step in range(1, sources // pair)]
    return blocks + ([across_pair(held) for held in blocks] if pair == 2 else [])


def gather_target(block):
    targets = lax.axis_size("tgt")
    return [block] + [
        lax.ppermute(block, "tgt", [(i, partner(i, step, targets)) for i in range(targets)])
        for step in range(1, targets)
    ]


def friction(shear_now, normal_now, state_now, friction_a):
    drive = shear_now / (friction_a * jnp.maximum(normal_now, 1.0))
    decay = state_now / friction_a
    return jnp.exp(drive - decay) - jnp.exp(-drive - decay)


def deviation_of(slip_rate):
    return (slip_rate - 1.0).astype(jnp.bfloat16)


def lane_side(shape, half):
    return lax.broadcasted_iota(jnp.int32, shape, len(shape) - 1) // half


def pack_kernel(*refs):
    packed_ref = refs[-1]
    own = refs[0].shape[0]
    for i, ref in enumerate(refs[:-1]):
        packed_ref[i * own : (i + 1) * own] = ref[...]


def dense_kernel(near_ref, rank_ref, shear_ref, normal_ref, dense_ref):
    leaf_rows, leaf_cols, block, _ = shear_ref.shape
    half = block // 2
    rank_ids = lax.broadcasted_iota(jnp.int32, (block, half), 1)
    for which, leaves in enumerate((shear_ref, normal_ref)):
        for row in range(leaf_rows):
            for col in range(leaf_cols):
                near = near_ref[col : col + 1, row : row + 1] == 1
                leaf = leaves[row, col]
                kept = rank_ids < rank_ref[col : col + 1, row : row + 1]
                factor_u = jnp.where(kept, leaf[:, :half].astype(jnp.float32), 0.0).astype(jnp.bfloat16)
                product = lax.dot_general(
                    factor_u, leaf[:, half:], (((1,), (1,)), ((), ())), preferred_element_type=jnp.float32
                )
                dense = jnp.where(near, leaf.astype(jnp.float32), product).astype(jnp.bfloat16)
                start = (which * leaf_rows + row) * block
                dense_ref[start : start + block, col * block : (col + 1) * block] = dense


def join_kernel(mine_ref, theirs_ref, *outs):
    half = mine_ref.shape[1] // 2
    side = lax.axis_index("src") % 2
    theirs = pltpu.roll(theirs_ref[...], half, 1)
    joined = jnp.where(lane_side(theirs.shape, half) == side, mine_ref[...], theirs)
    each = joined.shape[0] // len(outs)
    for i, out in enumerate(outs):
        out[...] = joined[i * each : (i + 1) * each]


def unpack_kernel(count, *refs):
    blocks, outs, dev_ref = refs[: -count - 1], refs[-count - 1 : -1], refs[-1]
    own = blocks[0].shape[0] // count
    far = lax.axis_index("src") // 2
    for step, block in enumerate(blocks):
        start = pl.multiple_of(origin(far, step, len(blocks)) * own, own)
        for i, out in enumerate(outs):
            out[pl.ds(start, own)] = block[i * own : (i + 1) * own]
    dev_ref[...] = deviation_of(friction(*(out[...] for out in outs[:4])))


def stage_kernel(stage, own, dense_count, targets, *refs):
    refs, all_dev = refs[:-1], refs[-1]
    dense_in, refs = refs[:dense_count], refs[dense_count:]
    dev_in, refs = refs[:targets], refs[targets:]
    begin_in, (a_ref, h_ref), refs = refs[:3], refs[3:5], refs[5:]
    now_in, outs = (refs[:3], refs[3:]) if stage else (begin_in, refs)

    joined, members = dev_in[0].shape
    half = members // 2
    rows, line = 2 * joined, joined // own
    for step, dev_ref in enumerate(dev_in):
        place = origin(lax.axis_index("tgt"), step, targets) * rows
        dev = dev_ref[...].astype(jnp.float32)
        for side, part in enumerate((dev, pltpu.roll(dev, half, 1))):
            for far in range(line):
                start = pl.multiple_of(place + (2 * far + side) * own, own)
                all_dev[pl.ds(start, own)] = part[far * own : (far + 1) * own]
    deviations = all_dev[...].astype(jnp.bfloat16)
    if stage == 0:
        dense_ref, outs = outs[-1], outs[:-1]
        width = dense_in[0].shape[1]
        for place, dense in zip(block_order(lax.axis_index("src"), dense_count), dense_in):
            dense_ref[:, pl.ds(pl.multiple_of(place * width, width), width)] = dense[...]
    else:
        dense_ref = dense_in[0]

    if stage < 2:
        mine, kept = slice(None), line
        total = jnp.dot(dense_ref[...], deviations, preferred_element_type=jnp.float32)
        totals = [total[:rows], total[rows:]]
    else:
        kept = 1
        far = lax.axis_index("src") // 2
        mine = pl.ds(pl.multiple_of(far * own, own), own)
        start = pl.multiple_of(far * 2 * own, 2 * own)
        totals = [
            jnp.dot(dense_ref[pl.ds(first + start, 2 * own)], deviations, preferred_element_type=jnp.float32)
            for first in (0, rows)
        ]
    change = []
    for total in totals:
        sides = [
            jnp.concatenate([total[(2 * far + side) * own : (2 * far + side + 1) * own] for far in range(kept)])
            for side in range(2)
        ]
        change.append(
            jnp.where(lane_side(sides[0].shape, half) == 0, sides[0], pltpu.roll(sides[1], half, 1))
        )
    now = tuple(ref[mine] for ref in now_in)
    friction_a = a_ref[mine]
    change.append(h_ref[mine] * (jnp.exp(-now[2]) - friction(*now, friction_a)))
    moved = tuple(value + time_step * rate for value, rate in zip(now, change))
    if stage:
        begin = tuple(ref[mine] for ref in begin_in)
    if stage == 1:
        moved = tuple(0.75 * first + 0.25 * value for first, value in zip(begin, moved))
    elif stage == 2:
        moved = tuple(first / 3.0 + (2.0 / 3.0) * value for first, value in zip(begin, moved))
        for i, value in enumerate(moved):
            outs[0][i * own : (i + 1) * own] = value
        return
    for out, value in zip(outs, moved):
        out[...] = value
    outs[3][...] = deviation_of(friction(*moved, friction_a))


def call(kernel, outs, given, scratch=(), limit=48 << 20):
    return pl.pallas_call(
        kernel,
        out_shape=tuple(outs),
        in_specs=[VMEM] * len(given),
        out_specs=(VMEM,) * len(outs),
        scratch_shapes=list(scratch),
        compiler_params=pltpu.CompilerParams(vmem_limit_bytes=limit),
    )(*given)


def per_device(
    shear_leaves, normal_leaves, near_flags, ranks, shear_traction, normal_traction, state, friction_a, heal_rate
):
    leaf_rows, leaf_cols, block, _ = shear_leaves.shape
    own, members = state.shape
    sources, targets = lax.axis_size("src"), lax.axis_size("tgt")
    rows = own * sources
    arrays = (shear_traction, normal_traction, state, friction_a, heal_rate)

    def floats(count):
        return jax.ShapeDtypeStruct((count, members), jnp.float32)

    wide = floats(rows // 2)
    dev_type = jax.ShapeDtypeStruct((rows // 2, members), jnp.bfloat16)

    (packed,) = call(pack_kernel, (floats(len(arrays) * own),), arrays, limit=60 << 20)
    (dense,) = call(
        dense_kernel,
        (jax.ShapeDtypeStruct((2 * rows, leaf_cols * block), jnp.bfloat16),),
        (near_flags.T, ranks.T, shear_leaves, normal_leaves),
        limit=60 << 20,
    )
    (joined,) = call(join_kernel, (floats(len(arrays) * own),), (packed, across_pair(packed)))
    joined_blocks = [joined] + [along_line(joined, step) for step in range(1, sources // 2)]
    dense_blocks = gather_source(dense)
    *begin, all_a, all_h, dev = call(
        functools.partial(unpack_kernel, len(arrays)), (wide,) * len(arrays) + (dev_type,), joined_blocks
    )
    now = ()
    matrix_type = jax.ShapeDtypeStruct((2 * rows, sources * leaf_cols * block), jnp.bfloat16)
    for stage in range(3):
        given = (*dense_blocks, *gather_target(dev), *begin, all_a, all_h, *now)
        outs = ((wide,) * 3 + (dev_type,)) if stage < 2 else (floats(3 * own),)
        outs = outs + ((matrix_type,) if stage == 0 else ())
        results = call(
            functools.partial(stage_kernel, stage, own, len(dense_blocks), targets),
            outs,
            given,
            [pltpu.VMEM((rows * targets, members), jnp.float32)],
        )
        now = results[:3]
        if stage < 2:
            dev = results[3]
        if stage == 0:
            dense_blocks = [results[4]]
    return call(join_kernel, (floats(own),) * 3, (results[0], across_pair(results[0])))


def solution(mesh):
    rows = P(("tgt", "src"), None)
    leaves = P("tgt", "src", None, None)
    flags = P("tgt", "src")
    return jax.shard_map(
        per_device,
        mesh=mesh,
        in_specs=(leaves, leaves, flags, flags) + (rows,) * 5,
        out_specs=(rows,) * 3,
        check_vma=False,
    )
```

time: 66.6 us -> 48.9 us (0.73)
  blocking collectives: 55.7 us -> 0 us
  starting transfers between devices: 0 us -> 21 us
  waiting for transfers between devices: 0 us -> 20 us
  Pallas kernels: 7.72 us -> 6.02 us
  local copies, waits for them, and re-layouts: 1.96 us -> 0.89 us
    all_to_all x4 -> x0, blocking collectives: 55.7 us -> none  [the longest x3 40.9 us: per_device(): lax.all_to_all(copies, ('tgt', 'src'), 0, 0, tiled=True)]
    ppermute x0 -> x21, starting transfers between devices: none -> 21 us  [the longest x6 8.12 us: across_pair(): lax.ppermute(block, 'src', [(i, i ^ 1) for i in range(lax.axis_size('src'...]
    ppermute x0 -> x21, waiting for transfers between devices: none -> 20 us  [the longest x9 8.45 us: gather_target(): lax.ppermute(block, 'tgt', [(i, partner(i, step, targets)) for i in range...]
    pallas_call x4 -> x8, Pallas kernels: 7.72 us -> 6.02 us  [call(): pl.pallas_call(kernel, out_shape=tuple(outs), in_specs=[VMEM] * len(given...]
    unnamed x6 -> x4, local copies, waits for them, and re-layouts: 1.96 us -> 0.89 us
  transfers between devices with their start and end apart: 0 -> 21, of which waited for: 0 -> 12; matrix products, arithmetic and copies ran while one was open for 0% -> 0% of each run, Pallas kernels for 0% -> 3%
where the time goes in v2:
time: 48.9 us; the launch traced here: 48.6 us
  starting transfers between devices  21 us (43%)
  waiting for transfers between devices  20 us (41%)
  Pallas kernels  6.02 us (12%)
  local copies, waits for them, and re-layouts  0.89 us (2%)
  between operations  0.71 us (1%)
    ppermute x9, waiting for transfers between devices, gather_target(): lax.ppermute(block, 'tgt', [(i, partner(i, step, targets)) for i in range...  8.45 us
    ppermute x6, starting transfers between devices, across_pair(): lax.ppermute(block, 'src', [(i, i ^ 1) for i in range(lax.axis_size('src'...  8.12 us
    ppermute x6, starting transfers between devices, along_line(): return lax.ppermute(block, 'src', moves)  7.14 us
    ppermute x6, waiting for transfers between devices, along_line(): return lax.ppermute(block, 'src', moves)  6.92 us
    pallas_call x8, Pallas kernels, call(): pl.pallas_call(kernel, out_shape=tuple(outs), in_specs=[VMEM] * len(given...  6.02 us
    ppermute x9, starting transfers between devices, gather_target(): lax.ppermute(block, 'tgt', [(i, partner(i, step, targets)) for i in range...  5.69 us
    ppermute x6, waiting for transfers between devices, across_pair(): lax.ppermute(block, 'src', [(i, i ^ 1) for i in range(lax.axis_size('src'...  4.67 us
  transfers between devices with their start and end apart: 21, of which 12 were waited for; matrix products, arithmetic and copies ran while one was open for 0% of the time, Pallas kernels for 3%

profile of v2, /device:TPU:0, one launch (start us, length us, event | category | flops | bytes accessed | tf_op | source)
XLA Modules:
  0.0 48.6 jit_solution(15309455549138112518)
XLA Ops:
  0.6 1.8 %shard_map.112.refs_0_ = bf16[512,128]{1,0:T(8,128)(2,1)} custom-call(s32[1,2]{1,0:T(1,128)} %bitcast.2, s32[1,2]{1,0:T(1,128)} %bitcast.3, bf16[2,1,128,128]{3,2,1,0:T(8,128)(2,1)} %shear_ref.1, bf16[2,1,128,128]{3,2,1,0:T(8,128)(2,1)} %normal_ref.1), custom_call_target="tpu_custom_call" | custom-call | tf_op jit(solution)/shard_map/pallas_call | solution.py:190
  2.5 5.0 %collective-permute-start.2 = (bf16[512,128]{1,0:T(8,128)(2,1)}, bf16[512,128]{1,0:T(8,128)(2,1)S(1)}, u32[]{:S(2)}, u32[]{:S(2)}) collective-permute-start(bf16[512,128]{1,0:T(8,128)(2,1)} %shard_map.112.refs_0_), channel_id=1, source_target_pairs={{0,6},{1,7},{2,4},{3,5},{4,2},{5,3},{6,0},{7,1},{8,14},{9,15},{10,... | collective-permute-start | bytes 393224 | tf_op jit(solution)/shard_map/ppermute | solution.py:40
  7.5 1.4 %shard_map.113.mine_ref = f32[160,128]{1,0:T(8,128)} custom-call(f32[32,128]{1,0:T(8,128)} %refs_0_.1, f32[32,128]{1,0:T(8,128)} %refs_1_.1, f32[32,128]{1,0:T(8,128)} %refs_2_.1, f32[32,128]{1,0:T(8,128)} %refs_3_.1, f32[32,128]{1,0:T(8,128)} %refs_4_.1), custom_call_target="tpu_custom_call" | custom-call | tf_op jit(solution)/shard_map/pallas_call | solution.py:190
  8.9 1.5 %collective-permute-start.7 = (f32[160,128]{1,0:T(8,128)}, f32[160,128]{1,0:T(8,128)S(1)}, u32[]{:S(2)}, u32[]{:S(2)}) collective-permute-start(f32[160,128]{1,0:T(8,128)} %shard_map.113.mine_ref), channel_id=1, source_target_pairs={{0,1},{1,0},{2,3},{3,2},{4,5},{5,4},{6,7},{7,6},{8,9},{9,8},{10,11... | collective-permute-start | bytes 245768 | tf_op jit(solution)/shard_map/ppermute | solution.py:44
  10.4 0.8 %collective-permute-start = (bf16[512,128]{1,0:T(8,128)(2,1)S(1)}, bf16[512,128]{1,0:T(8,128)(2,1)S(1)}, u32[]{:S(2)}, u32[]{:S(2)}) collective-permute-start(bf16[512,128]{1,0:T(8,128)(2,1)S(1)} %copy-done), channel_id=1, source_target_pairs={{0,2},{1,3},{2,0},{3,1},{4,6},{5,7},{6,4},{7,5},{8,10},{9,11},{10,... | collective-permute-start | bytes 393224 | tf_op jit(solution)/shard_map/ppermute | solution.py:40
  11.2 2.4 %collective-permute-done.7.theirs_ref = f32[160,128]{1,0:T(8,128)S(1)} collective-permute-done((f32[160,128]{1,0:T(8,128)}, f32[160,128]{1,0:T(8,128)S(1)}, u32[]{:S(2)}, u32[]{:S(2)}) %collective-permute-start.7) | collective-permute-done | bytes 81952 | tf_op jit(solution)/shard_map/ppermute | solution.py:44
  13.6 0.9 %copy-done.1 = f32[160,128]{1,0:T(8,128)S(1)} copy-done((f32[160,128]{1,0:T(8,128)S(1)}, f32[160,128]{1,0:T(8,128)}, u32[]{:S(2)}) %copy-start.1) | copy-done | bytes 81944
  14.6 1.3 %collective-permute-start.10 = (f32[160,128]{1,0:T(8,128)S(1)}, f32[160,128]{1,0:T(8,128)S(1)}, u32[]{:S(2)}, u32[]{:S(2)}) collective-permute-start(f32[160,128]{1,0:T(8,128)S(1)} %shard_map.114.refs_0_), channel_id=1, source_target_pairs={{0,6},{1,7},{2,4},{3,5},{4,2},{5,3},{6,0},{7,1},{8,14},{9,15},{10,... | collective-permute-start | bytes 245768 | tf_op jit(solution)/shard_map/ppermute | solution.py:40
  15.9 1.3 %collective-permute-start.3 = (bf16[512,128]{1,0:T(8,128)(2,1)S(1)}, bf16[512,128]{1,0:T(8,128)(2,1)S(1)}, u32[]{:S(2)}, u32[]{:S(2)}) collective-permute-start(bf16[512,128]{1,0:T(8,128)(2,1)S(1)} %copy-done), channel_id=1, source_target_pairs={{0,1},{1,0},{2,3},{3,2},{4,5},{5,4},{6,7},{7,6},{8,9},{9,8},{10,11... | collective-permute-start | bytes 393224 | tf_op jit(solution)/shard_map/ppermute | solution.py:44
  17.1 6.0 %collective-permute-done.1.refs_2_ = bf16[512,128]{1,0:T(8,128)(2,1)S(1)} collective-permute-done((bf16[512,128]{1,0:T(8,128)(2,1)S(1)}, bf16[512,128]{1,0:T(8,128)(2,1)S(1)}, u32[]{:S(2)}, u32[]{:S(2)}) %collective-permute-start.1) | collective-permute-done | bytes 131104 | tf_op jit(solution)/shard_map/ppermute | solution.py:40
  23.1 1.8 %collective-permute-start.6 = (bf16[512,128]{1,0:T(8,128)(2,1)S(1)}, bf16[512,128]{1,0:T(8,128)(2,1)S(1)}, u32[]{:S(2)}, u32[]{:S(2)}) collective-permute-start(bf16[512,128]{1,0:T(8,128)(2,1)S(1)} %collective-permute-done.2.refs_3_), channel_id=1, source_target_pairs={{0,1},{1,0},{2,3},{3,2},{4,5},{5,4},{6,7},{7,6},{8,9},{9,8},{10,11... | collective-permute-start | bytes 393224 | tf_op jit(solution)/shard_map/ppermute | solution.py:44
  25.2 0.6 %collective-permute-done.9.refs_2_ = f32[160,128]{1,0:T(8,128)S(1)} collective-permute-done((f32[160,128]{1,0:T(8,128)S(1)}, f32[160,128]{1,0:T(8,128)S(1)}, u32[]{:S(2)}, u32[]{:S(2)}) %collective-permute-start.9) | collective-permute-done | bytes 81952 | tf_op jit(solution)/shard_map/ppermute | solution.py:40
  25.8 1.5 %collective-permute-start.4 = (bf16[512,128]{1,0:T(8,128)(2,1)S(1)}, bf16[512,128]{1,0:T(8,128)(2,1)S(1)}, u32[]{:S(2)}, u32[]{:S(2)}) collective-permute-start(bf16[512,128]{1,0:T(8,128)(2,1)S(1)} %collective-permute-done.refs_1_), channel_id=1, source_target_pairs={{0,1},{1,0},{2,3},{3,2},{4,5},{5,4},{6,7},{7,6},{8,9},{9,8},{10,11... | collective-permute-start | bytes 393224 | tf_op jit(solution)/shard_map/ppermute | solution.py:44
  27.3 0.3 collective-permute-done.8.refs_1_
  27.7 1.6 %collective-permute-start.12 = (bf16[128,128]{1,0:T(8,128)(2,1)S(1)}, bf16[128,128]{1,0:T(8,128)(2,1)S(1)}, u32[]{:S(2)}, u32[]{:S(2)}) collective-permute-start(bf16[128,128]{1,0:T(8,128)(2,1)S(1)} %get-tuple-element.18.refs_8_), channel_id=1, source_target_pairs={{0,16},{8,24},{16,0},{24,8},{1,17},{9,25},{17,1},{25,9},{2,18},{10... | collective-permute-start | bytes 98312 | tf_op jit(solution)/shard_map/ppermute | solution.py:57
  29.3 2.0 %collective-permute-done.13.refs_11_ = bf16[128,128]{1,0:T(8,128)(2,1)S(1)} collective-permute-done((bf16[128,128]{1,0:T(8,128)(2,1)S(1)}, bf16[128,128]{1,0:T(8,128)(2,1)S(1)}, u32[]{:S(2)}, u32[]{:S(2)}) %collective-permute-start.13) | collective-permute-done | bytes 32800 | tf_op jit(solution)/shard_map/ppermute | solution.py:57
  31.5 0.2 collective-permute-done.12.refs_10_
  31.8 0.8 %collective-permute-done.11.refs_9_ = bf16[128,128]{1,0:T(8,128)(2,1)S(1)} collective-permute-done((bf16[128,128]{1,0:T(8,128)(2,1)S(1)}, bf16[128,128]{1,0:T(8,128)(2,1)S(1)}, u32[]{:S(2)}, u32[]{:S(2)}) %collective-permute-start.11) | collective-permute-done | bytes 32800 | tf_op jit(solution)/shard_map/ppermute | solution.py:57
  32.6 0.9 %shard_map.116 = (f32[128,128]{1,0:T(8,128)S(1)}, f32[128,128]{1,0:T(8,128)S(1)}, f32[128,128]{1,0:T(8,128)S(1)}, bf16[128,128]{1,0:T(8,128)(2,1)S(1)}, bf16[512,1024]{1,0:T(8,128)(2,1)S(1)}) custom-call(bf16[512,128]{1,0:T(8,128)(2,1)S(1)} %copy-done, bf16[512,128]{1,0:T(8,128)(2,1)S(1)} %collective-permute-done.refs_1_, ...), custom_call_target="tpu_custom_call" | custom-call | tf_op jit(solution)/shard_map/pallas_call | solution.py:190
  33.5 1.1 %collective-permute-start.16 = (bf16[128,128]{1,0:T(8,128)(2,1)S(1)}, bf16[128,128]{1,0:T(8,128)(2,1)S(1)}, u32[]{:S(2)}, u32[]{:S(2)}) collective-permute-start(bf16[128,128]{1,0:T(8,128)(2,1)S(1)} %get-tuple-element.25.refs_1_), channel_id=1, source_target_pairs={{0,24},{8,16},{16,8},{24,0},{1,25},{9,17},{17,9},{25,1},{2,26},{10... | collective-permute-start | bytes 98312 | tf_op jit(solution)/shard_map/ppermute | solution.py:57
  34.5 0.8 %collective-permute-start.15 = (bf16[128,128]{1,0:T(8,128)(2,1)S(1)}, bf16[128,128]{1,0:T(8,128)(2,1)S(1)}, u32[]{:S(2)}, u32[]{:S(2)}) collective-permute-start(bf16[128,128]{1,0:T(8,128)(2,1)S(1)} %get-tuple-element.25.refs_1_), channel_id=1, source_target_pairs={{0,16},{8,24},{16,0},{24,8},{1,17},{9,25},{17,1},{25,9},{2,18},{10... | collective-permute-start | bytes 98312 | tf_op jit(solution)/shard_map/ppermute | solution.py:57
  35.4 1.5 %collective-permute-done.16.refs_4_ = bf16[128,128]{1,0:T(8,128)(2,1)S(1)} collective-permute-done((bf16[128,128]{1,0:T(8,128)(2,1)S(1)}, bf16[128,128]{1,0:T(8,128)(2,1)S(1)}, u32[]{:S(2)}, u32[]{:S(2)}) %collective-permute-start.16) | collective-permute-done | bytes 32800 | tf_op jit(solution)/shard_map/ppermute | solution.py:57
  36.9 1.6 %collective-permute-done.15.refs_3_ = bf16[128,128]{1,0:T(8,128)(2,1)S(1)} collective-permute-done((bf16[128,128]{1,0:T(8,128)(2,1)S(1)}, bf16[128,128]{1,0:T(8,128)(2,1)S(1)}, u32[]{:S(2)}, u32[]{:S(2)}) %collective-permute-start.15) | collective-permute-done | bytes 32800 | tf_op jit(solution)/shard_map/ppermute | solution.py:57
  38.5 0.6 %shard_map.117 = (f32[128,128]{1,0:T(8,128)S(1)}, f32[128,128]{1,0:T(8,128)S(1)}, f32[128,128]{1,0:T(8,128)S(1)}, bf16[128,128]{1,0:T(8,128)(2,1)S(1)}) custom-call(bf16[512,1024]{1,0:T(8,128)(2,1)S(1)} %get-tuple-element.24.refs_0_, bf16[128,128]{1,0:T(8,128)(2,1)S(1)} %get-tuple-element.25.refs_1_, bf16[128,128]{1,0:T(8,128)(2,1)S(1)} %collective-permute-done.14.refs_2_, ...), custom_call_target="tpu_custom_call" | custom-call | tf_op jit(solution)/shard_map/pallas_call | solution.py:190
  39.2 0.9 %collective-permute-start.18 = (bf16[128,128]{1,0:T(8,128)(2,1)S(1)}, bf16[128,128]{1,0:T(8,128)(2,1)S(1)}, u32[]{:S(2)}, u32[]{:S(2)}) collective-permute-start(bf16[128,128]{1,0:T(8,128)(2,1)S(1)} %get-tuple-element.29.refs_1_), channel_id=1, source_target_pairs={{0,16},{8,24},{16,0},{24,8},{1,17},{9,25},{17,1},{25,9},{2,18},{10... | collective-permute-start | bytes 98312 | tf_op jit(solution)/shard_map/ppermute | solution.py:57
  40.1 1.0 %collective-permute-start.17 = (bf16[128,128]{1,0:T(8,128)(2,1)S(1)}, bf16[128,128]{1,0:T(8,128)(2,1)S(1)}, u32[]{:S(2)}, u32[]{:S(2)}) collective-permute-start(bf16[128,128]{1,0:T(8,128)(2,1)S(1)} %get-tuple-element.29.refs_1_), channel_id=1, source_target_pairs={{0,8},{8,0},{16,24},{24,16},{1,9},{9,1},{17,25},{25,17},{2,10},{10... | collective-permute-start | bytes 98312 | tf_op jit(solution)/shard_map/ppermute | solution.py:57
  41.0 1.5 %collective-permute-done.19.refs_4_ = bf16[128,128]{1,0:T(8,128)(2,1)S(1)} collective-permute-done((bf16[128,128]{1,0:T(8,128)(2,1)S(1)}, bf16[128,128]{1,0:T(8,128)(2,1)S(1)}, u32[]{:S(2)}, u32[]{:S(2)}) %collective-permute-start.19) | collective-permute-done | bytes 32800 | tf_op jit(solution)/shard_map/ppermute | solution.py:57
  42.5 0.9 %collective-permute-done.18.refs_3_ = bf16[128,128]{1,0:T(8,128)(2,1)S(1)} collective-permute-done((bf16[128,128]{1,0:T(8,128)(2,1)S(1)}, bf16[128,128]{1,0:T(8,128)(2,1)S(1)}, u32[]{:S(2)}, u32[]{:S(2)}) %collective-permute-start.18) | collective-permute-done | bytes 32800 | tf_op jit(solution)/shard_map/ppermute | solution.py:57
  43.4 0.4 shard_map.118.mine_ref
  43.8 1.8 %collective-permute-start.20 = (f32[96,128]{1,0:T(8,128)S(1)}, f32[96,128]{1,0:T(8,128)S(1)}, u32[]{:S(2)}, u32[]{:S(2)}) collective-permute-start(f32[96,128]{1,0:T(8,128)S(1)} %shard_map.118.mine_ref), channel_id=1, source_target_pairs={{0,1},{1,0},{2,3},{3,2},{4,5},{5,4},{6,7},{7,6},{8,9},{9,8},{10,11... | collective-permute-start | bytes 147464 | tf_op jit(solution)/shard_map/ppermute | solution.py:44
  45.6 2.3 %collective-permute-done.20.theirs_ref = f32[96,128]{1,0:T(8,128)S(1)} collective-permute-done((f32[96,128]{1,0:T(8,128)S(1)}, f32[96,128]{1,0:T(8,128)S(1)}, u32[]{:S(2)}, u32[]{:S(2)}) %collective-permute-start.20) | collective-permute-done | bytes 49184 | tf_op jit(solution)/shard_map/ppermute | solution.py:44
  47.9 0.7 %shard_map.119 = (f32[32,128]{1,0:T(8,128)}, f32[32,128]{1,0:T(8,128)}, f32[32,128]{1,0:T(8,128)}) custom-call(f32[96,128]{1,0:T(8,128)S(1)} %shard_map.118.mine_ref, f32[96,128]{1,0:T(8,128)S(1)} %collective-permute-done.20.theirs_ref), custom_call_target="tpu_custom_call" | custom-call | tf_op jit(solution)/shard_map/pallas_call | solution.py:190
  (22 shorter events, 0.8 us)
Async XLA Ops:
  2.5 8.0 %copy-start = (bf16[512,128]{1,0:T(8,128)(2,1)S(1)}, bf16[512,128]{1,0:T(8,128)(2,1)}, u32[]{:S(2)}) copy-start(bf16[512,128]{1,0:T(8,128)(2,1)} %shard_map.112.refs_0_) | copy-start | bytes 393220
  2.5 13.4 %collective-permute-start.2 = (bf16[512,128]{1,0:T(8,128)(2,1)}, bf16[512,128]{1,0:T(8,128)(2,1)S(1)}, u32[]{:S(2)}, u32[]{:S(2)}) collective-permute-start(bf16[512,128]{1,0:T(8,128)(2,1)} %shard_map.112.refs_0_), channel_id=1, source_target_pairs={{0,6},{1,7},{2,4},{3,5},{4,2},{5,3},{6,0},{7,1},{8,14},{9,15},{10,... | collective-permute-start | bytes 393224 | tf_op jit(solution)/shard_map/ppermute | solution.py:40
  8.9 4.7 %collective-permute-start.7 = (f32[160,128]{1,0:T(8,128)}, f32[160,128]{1,0:T(8,128)S(1)}, u32[]{:S(2)}, u32[]{:S(2)}) collective-permute-start(f32[160,128]{1,0:T(8,128)} %shard_map.113.mine_ref), channel_id=1, source_target_pairs={{0,1},{1,0},{2,3},{3,2},{4,5},{5,4},{6,7},{7,6},{8,9},{9,8},{10,11... | collective-permute-start | bytes 245768 | tf_op jit(solution)/shard_map/ppermute | solution.py:44
  10.4 12.7 %collective-permute-start.1 = (bf16[512,128]{1,0:T(8,128)(2,1)S(1)}, bf16[512,128]{1,0:T(8,128)(2,1)S(1)}, u32[]{:S(2)}, u32[]{:S(2)}) collective-permute-start(bf16[512,128]{1,0:T(8,128)(2,1)S(1)} %copy-done), channel_id=1, source_target_pairs={{0,4},{1,5},{2,6},{3,7},{4,0},{5,1},{6,2},{7,3},{8,12},{9,13},{10,... | collective-permute-start | bytes 393224 | tf_op jit(solution)/shard_map/ppermute | solution.py:40
  10.4 12.7 %collective-permute-start = (bf16[512,128]{1,0:T(8,128)(2,1)S(1)}, bf16[512,128]{1,0:T(8,128)(2,1)S(1)}, u32[]{:S(2)}, u32[]{:S(2)}) collective-permute-start(bf16[512,128]{1,0:T(8,128)(2,1)S(1)} %copy-done), channel_id=1, source_target_pairs={{0,2},{1,3},{2,0},{3,1},{4,6},{5,7},{6,4},{7,5},{8,10},{9,11},{10,... | collective-permute-start | bytes 393224 | tf_op jit(solution)/shard_map/ppermute | solution.py:40
  13.6 0.9 %copy-start.1 = (f32[160,128]{1,0:T(8,128)S(1)}, f32[160,128]{1,0:T(8,128)}, u32[]{:S(2)}) copy-start(f32[160,128]{1,0:T(8,128)} %shard_map.113.mine_ref) | copy-start | bytes 245764
  14.6 10.4 %collective-permute-start.10 = (f32[160,128]{1,0:T(8,128)S(1)}, f32[160,128]{1,0:T(8,128)S(1)}, u32[]{:S(2)}, u32[]{:S(2)}) collective-permute-start(f32[160,128]{1,0:T(8,128)S(1)} %shard_map.114.refs_0_), channel_id=1, source_target_pairs={{0,6},{1,7},{2,4},{3,5},{4,2},{5,3},{6,0},{7,1},{8,14},{9,15},{10,... | collective-permute-start | bytes 245768 | tf_op jit(solution)/shard_map/ppermute | solution.py:40
  15.9 10.0 %collective-permute-start.9 = (f32[160,128]{1,0:T(8,128)S(1)}, f32[160,128]{1,0:T(8,128)S(1)}, u32[]{:S(2)}, u32[]{:S(2)}) collective-permute-start(f32[160,128]{1,0:T(8,128)S(1)} %shard_map.114.refs_0_), channel_id=1, source_target_pairs={{0,4},{1,5},{2,6},{3,7},{4,0},{5,1},{6,2},{7,3},{8,12},{9,13},{10,... | collective-permute-start | bytes 245768 | tf_op jit(solution)/shard_map/ppermute | solution.py:40
  15.9 11.9 %collective-permute-start.3 = (bf16[512,128]{1,0:T(8,128)(2,1)S(1)}, bf16[512,128]{1,0:T(8,128)(2,1)S(1)}, u32[]{:S(2)}, u32[]{:S(2)}) collective-permute-start(bf16[512,128]{1,0:T(8,128)(2,1)S(1)} %copy-done), channel_id=1, source_target_pairs={{0,1},{1,0},{2,3},{3,2},{4,5},{5,4},{6,7},{7,6},{8,9},{9,8},{10,11... | collective-permute-start | bytes 393224 | tf_op jit(solution)/shard_map/ppermute | solution.py:44
  23.1 4.4 %collective-permute-start.8 = (f32[160,128]{1,0:T(8,128)S(1)}, f32[160,128]{1,0:T(8,128)S(1)}, u32[]{:S(2)}, u32[]{:S(2)}) collective-permute-start(f32[160,128]{1,0:T(8,128)S(1)} %shard_map.114.refs_0_), channel_id=1, source_target_pairs={{0,2},{1,3},{2,0},{3,1},{4,6},{5,7},{6,4},{7,5},{8,10},{9,11},{10,... | collective-permute-start | bytes 245768 | tf_op jit(solution)/shard_map/ppermute | solution.py:40
  23.1 9.4 %collective-permute-start.6 = (bf16[512,128]{1,0:T(8,128)(2,1)S(1)}, bf16[512,128]{1,0:T(8,128)(2,1)S(1)}, u32[]{:S(2)}, u32[]{:S(2)}) collective-permute-start(bf16[512,128]{1,0:T(8,128)(2,1)S(1)} %collective-permute-done.2.refs_3_), channel_id=1, source_target_pairs={{0,1},{1,0},{2,3},{3,2},{4,5},{5,4},{6,7},{7,6},{8,9},{9,8},{10,11... | collective-permute-start | bytes 393224 | tf_op jit(solution)/shard_map/ppermute | solution.py:44
  24.9 7.6 %collective-permute-start.5 = (bf16[512,128]{1,0:T(8,128)(2,1)S(1)}, bf16[512,128]{1,0:T(8,128)(2,1)S(1)}, u32[]{:S(2)}, u32[]{:S(2)}) collective-permute-start(bf16[512,128]{1,0:T(8,128)(2,1)S(1)} %collective-permute-done.1.refs_2_), channel_id=1, source_target_pairs={{0,1},{1,0},{2,3},{3,2},{4,5},{5,4},{6,7},{7,6},{8,9},{9,8},{10,11... | collective-permute-start | bytes 393224 | tf_op jit(solution)/shard_map/ppermute | solution.py:44
  25.8 6.7 %collective-permute-start.4 = (bf16[512,128]{1,0:T(8,128)(2,1)S(1)}, bf16[512,128]{1,0:T(8,128)(2,1)S(1)}, u32[]{:S(2)}, u32[]{:S(2)}) collective-permute-start(bf16[512,128]{1,0:T(8,128)(2,1)S(1)} %collective-permute-done.refs_1_), channel_id=1, source_target_pairs={{0,1},{1,0},{2,3},{3,2},{4,5},{5,4},{6,7},{7,6},{8,9},{9,8},{10,11... | collective-permute-start | bytes 393224 | tf_op jit(solution)/shard_map/ppermute | solution.py:44
  27.7 3.7 %collective-permute-start.13 = (bf16[128,128]{1,0:T(8,128)(2,1)S(1)}, bf16[128,128]{1,0:T(8,128)(2,1)S(1)}, u32[]{:S(2)}, u32[]{:S(2)}) collective-permute-start(bf16[128,128]{1,0:T(8,128)(2,1)S(1)} %get-tuple-element.18.refs_8_), channel_id=1, source_target_pairs={{0,24},{8,16},{16,8},{24,0},{1,25},{9,17},{17,9},{25,1},{2,26},{10... | collective-permute-start | bytes 98312 | tf_op jit(solution)/shard_map/ppermute | solution.py:57
  27.7 4.0 %collective-permute-start.12 = (bf16[128,128]{1,0:T(8,128)(2,1)S(1)}, bf16[128,128]{1,0:T(8,128)(2,1)S(1)}, u32[]{:S(2)}, u32[]{:S(2)}) collective-permute-start(bf16[128,128]{1,0:T(8,128)(2,1)S(1)} %get-tuple-element.18.refs_8_), channel_id=1, source_target_pairs={{0,16},{8,24},{16,0},{24,8},{1,17},{9,25},{17,1},{25,9},{2,18},{10... | collective-permute-start | bytes 98312 | tf_op jit(solution)/shard_map/ppermute | solution.py:57
  31.3 1.2 %collective-permute-start.11 = (bf16[128,128]{1,0:T(8,128)(2,1)S(1)}, bf16[128,128]{1,0:T(8,128)(2,1)S(1)}, u32[]{:S(2)}, u32[]{:S(2)}) collective-permute-start(bf16[128,128]{1,0:T(8,128)(2,1)S(1)} %get-tuple-element.18.refs_8_), channel_id=1, source_target_pairs={{0,8},{8,0},{16,24},{24,16},{1,9},{9,1},{17,25},{25,17},{2,10},{10... | collective-permute-start | bytes 98312 | tf_op jit(solution)/shard_map/ppermute | solution.py:57
  33.5 3.4 %collective-permute-start.16 = (bf16[128,128]{1,0:T(8,128)(2,1)S(1)}, bf16[128,128]{1,0:T(8,128)(2,1)S(1)}, u32[]{:S(2)}, u32[]{:S(2)}) collective-permute-start(bf16[128,128]{1,0:T(8,128)(2,1)S(1)} %get-tuple-element.25.refs_1_), channel_id=1, source_target_pairs={{0,24},{8,16},{16,8},{24,0},{1,25},{9,17},{17,9},{25,1},{2,26},{10... | collective-permute-start | bytes 98312 | tf_op jit(solution)/shard_map/ppermute | solution.py:57
  34.5 3.9 %collective-permute-start.15 = (bf16[128,128]{1,0:T(8,128)(2,1)S(1)}, bf16[128,128]{1,0:T(8,128)(2,1)S(1)}, u32[]{:S(2)}, u32[]{:S(2)}) collective-permute-start(bf16[128,128]{1,0:T(8,128)(2,1)S(1)} %get-tuple-element.25.refs_1_), channel_id=1, source_target_pairs={{0,16},{8,24},{16,0},{24,8},{1,17},{9,25},{17,1},{25,9},{2,18},{10... | collective-permute-start | bytes 98312 | tf_op jit(solution)/shard_map/ppermute | solution.py:57
  35.3 3.1 %collective-permute-start.14 = (bf16[128,128]{1,0:T(8,128)(2,1)S(1)}, bf16[128,128]{1,0:T(8,128)(2,1)S(1)}, u32[]{:S(2)}, u32[]{:S(2)}) collective-permute-start(bf16[128,128]{1,0:T(8,128)(2,1)S(1)} %get-tuple-element.25.refs_1_), channel_id=1, source_target_pairs={{0,8},{8,0},{16,24},{24,16},{1,9},{9,1},{17,25},{25,17},{2,10},{10... | collective-permute-start | bytes 98312 | tf_op jit(solution)/shard_map/ppermute | solution.py:57
  39.1 3.4 %collective-permute-start.19 = (bf16[128,128]{1,0:T(8,128)(2,1)S(1)}, bf16[128,128]{1,0:T(8,128)(2,1)S(1)}, u32[]{:S(2)}, u32[]{:S(2)}) collective-permute-start(bf16[128,128]{1,0:T(8,128)(2,1)S(1)} %get-tuple-element.29.refs_1_), channel_id=1, source_target_pairs={{0,24},{8,16},{16,8},{24,0},{1,25},{9,17},{17,9},{25,1},{2,26},{10... | collective-permute-start | bytes 98312 | tf_op jit(solution)/shard_map/ppermute | solution.py:57
  39.2 4.2 %collective-permute-start.18 = (bf16[128,128]{1,0:T(8,128)(2,1)S(1)}, bf16[128,128]{1,0:T(8,128)(2,1)S(1)}, u32[]{:S(2)}, u32[]{:S(2)}) collective-permute-start(bf16[128,128]{1,0:T(8,128)(2,1)S(1)} %get-tuple-element.29.refs_1_), channel_id=1, source_target_pairs={{0,16},{8,24},{16,0},{24,8},{1,17},{9,25},{17,1},{25,9},{2,18},{10... | collective-permute-start | bytes 98312 | tf_op jit(solution)/shard_map/ppermute | solution.py:57
  40.1 3.3 %collective-permute-start.17 = (bf16[128,128]{1,0:T(8,128)(2,1)S(1)}, bf16[128,128]{1,0:T(8,128)(2,1)S(1)}, u32[]{:S(2)}, u32[]{:S(2)}) collective-permute-start(bf16[128,128]{1,0:T(8,128)(2,1)S(1)} %get-tuple-element.29.refs_1_), channel_id=1, source_target_pairs={{0,8},{8,0},{16,24},{24,16},{1,9},{9,1},{17,25},{25,17},{2,10},{10... | collective-permute-start | bytes 98312 | tf_op jit(solution)/shard_map/ppermute | solution.py:57
  43.8 4.1 %collective-permute-start.20 = (f32[96,128]{1,0:T(8,128)S(1)}, f32[96,128]{1,0:T(8,128)S(1)}, u32[]{:S(2)}, u32[]{:S(2)}) collective-permute-start(f32[96,128]{1,0:T(8,128)S(1)} %shard_map.118.mine_ref), channel_id=1, source_target_pairs={{0,1},{1,0},{2,3},{3,2},{4,5},{5,4},{6,7},{7,6},{8,9},{9,8},{10,11... | collective-permute-start | bytes 147464 | tf_op jit(solution)/shard_map/ppermute | solution.py:44

commit v3 on v2

--- a/solution.py
+++ b/solution.py
@@ -8,7 +8,9 @@
 from jax.sharding import PartitionSpec as P
 
 time_step = 0.25
+PAIR = 2
 VMEM = pl.BlockSpec(memory_space=pltpu.VMEM)
+HBM = pl.BlockSpec(memory_space=pltpu.HBM)
 
 
 def partner(index, step, count):
@@ -19,24 +21,14 @@
     return index ^ step if count & (count - 1) == 0 else (index + count - step) % count
 
 
-def pair_of(sources):
-    return 2 if sources % 2 == 0 else 1
-
-
 def block_order(me, sources):
-    pair = pair_of(sources)
-    line = sources // pair
-    far, near = me // pair, me % pair
-    return [
-        origin(far, step, line) * pair + origin(near, side, pair) for side in range(pair) for step in range(line)
-    ]
+    line = sources // PAIR
+    return [origin(me // PAIR, step, line) * PAIR + (me % PAIR ^ side) for side in range(PAIR) for step in range(line)]
 
 
 def along_line(block, step):
     sources = lax.axis_size("src")
-    pair = pair_of(sources)
-    line = sources // pair
-    moves = [(i, partner(i // pair, step, line) * pair + i % pair) for i in range(sources)]
+    moves = [(i, partner(i // PAIR, step, sources // PAIR) * PAIR + i % PAIR) for i in range(sources)]
     return lax.ppermute(block, "src", moves)
 
 
@@ -44,11 +36,17 @@
     return lax.ppermute(block, "src", [(i, i ^ 1) for i in range(lax.axis_size("src"))])
 
 
-def gather_source(block):
-    sources = lax.axis_size("src")
-    pair = pair_of(sources)
-    blocks = [block] + [along_line(block, step) for step in range(1, sources // pair)]
-    return blocks + ([across_pair(held) for held in blocks] if pair == 2 else [])
+def gather_line(block, ready=()):
+    line = lax.axis_size("src") // PAIR
+    blocks = [block]
+    for step in range(1, line):
+        low = step & -step
+        if line & (line - 1) or step == low:
+            blocks.append(along_line(block, step))
+        else:
+            held, *_ = lax.optimization_barrier((blocks[step ^ low], *ready))
+            blocks.append(along_line(held, low))
+    return blocks
 
 
 def gather_target(block):
@@ -73,14 +71,19 @@
     return lax.broadcasted_iota(jnp.int32, shape, len(shape) - 1) // half
 
 
-def pack_kernel(*refs):
-    packed_ref = refs[-1]
-    own = refs[0].shape[0]
-    for i, ref in enumerate(refs[:-1]):
-        packed_ref[i * own : (i + 1) * own] = ref[...]
-
-
-def dense_kernel(near_ref, rank_ref, shear_ref, normal_ref, dense_ref):
+def prepare_kernel(*refs):
+    given, (packed_ref, dense_ref), held, sems = refs[:9], refs[9:11], refs[11:15], refs[15]
+    own = given[4].shape[0]
+    copies = [pltpu.make_async_copy(ref, place, sems.at[i]) for i, (ref, place) in enumerate(zip(given, held))]
+    copies += [
+        pltpu.make_async_copy(ref, packed_ref.at[pl.ds(i * own, own)], sems.at[4 + i])
+        for i, ref in enumerate(given[4:])
+    ]
+    for copy in copies:
+        copy.start()
+    for copy in copies:
+        copy.wait()
+    near_ref, rank_ref, shear_ref, normal_ref = held
     leaf_rows, leaf_cols, block, _ = shear_ref.shape
     half = block // 2
     rank_ids = lax.broadcasted_iota(jnp.int32, (block, half), 1)
@@ -186,14 +189,14 @@
     outs[3][...] = deviation_of(friction(*moved, friction_a))
 
 
-def call(kernel, outs, given, scratch=(), limit=48 << 20):
+def call(kernel, outs, given, scratch=(), space=VMEM):
     return pl.pallas_call(
         kernel,
         out_shape=tuple(outs),
-        in_specs=[VMEM] * len(given),
+        in_specs=[space] * len(given),
         out_specs=(VMEM,) * len(outs),
         scratch_shapes=list(scratch),
-        compiler_params=pltpu.CompilerParams(vmem_limit_bytes=limit),
+        compiler_params=pltpu.CompilerParams(vmem_limit_bytes=32 << 20),
     )(*given)
 
 
@@ -212,16 +215,20 @@
     wide = floats(rows // 2)
     dev_type = jax.ShapeDtypeStruct((rows // 2, members), jnp.bfloat16)
 
-    (packed,) = call(pack_kernel, (floats(len(arrays) * own),), arrays, limit=60 << 20)
-    (dense,) = call(
-        dense_kernel,
-        (jax.ShapeDtypeStruct((2 * rows, leaf_cols * block), jnp.bfloat16),),
-        (near_flags.T, ranks.T, shear_leaves, normal_leaves),
-        limit=60 << 20,
+    given = (near_flags.T, ranks.T, shear_leaves, normal_leaves, *arrays)
+    given = tuple(pltpu.with_memory_space_constraint(value, pltpu.HBM) for value in given)
+    packed, dense = call(
+        prepare_kernel,
+        (floats(len(arrays) * own), jax.ShapeDtypeStruct((2 * rows, leaf_cols * block), jnp.bfloat16)),
+        given,
+        [pltpu.VMEM(value.shape, value.dtype) for value in given[:4]] + [pltpu.SemaphoreType.DMA((len(given),))],
+        HBM,
     )
     (joined,) = call(join_kernel, (floats(len(arrays) * own),), (packed, across_pair(packed)))
-    joined_blocks = [joined] + [along_line(joined, step) for step in range(1, sources // 2)]
-    dense_blocks = gather_source(dense)
+    joined_blocks = gather_line(joined)
+    other = across_pair(dense)
+    held = gather_line(dense, (other,))
+    dense_blocks = held + [other] + [across_pair(value) for value in held[1:]]
     *begin, all_a, all_h, dev = call(
         functools.partial(unpack_kernel, len(arrays)), (wide,) * len(arrays) + (dev_type,), joined_blocks
     )

time: 48.9 us -> 46.7 us (0.955)
  starting transfers between devices: 21 us -> 24.1 us
  waiting for transfers between devices: 20 us -> 17.7 us
  Pallas kernels: 6.02 us -> 4.04 us
  local copies, waits for them, and re-layouts: 0.89 us -> 0 us
    ppermute x6, starting transfers between devices: 7.14 us -> 10.8 us  [along_line(): return lax.ppermute(block, 'src', moves)]
    ppermute x6, waiting for transfers between devices: 4.67 us -> 2.48 us  [across_pair(): lax.ppermute(block, 'src', [(i, i ^ 1) for i in range(lax.axis_size('src'...]
    pallas_call x8 -> x7, Pallas kernels: 6.02 us -> 4.04 us  [call(): pl.pallas_call(kernel, out_shape=tuple(outs), in_specs=[space] * len(give...]
    unnamed x4 -> x0, local copies, waits for them, and re-layouts: 0.89 us -> none
    ppermute x9, waiting for transfers between devices: 8.45 us -> 7.6 us  [gather_target(): lax.ppermute(block, 'tgt', [(i, partner(i, step, targets)) for i in range...]
    ppermute x6, starting transfers between devices: 8.12 us -> 7.3 us  [across_pair(): lax.ppermute(block, 'src', [(i, i ^ 1) for i in range(lax.axis_size('src'...]
    ppermute x6, waiting for transfers between devices: 6.92 us -> 7.64 us  [along_line(): return lax.ppermute(block, 'src', moves)]
  transfers between devices with their start and end apart: 21 -> 21, of which waited for: 12 -> 11; matrix products, arithmetic and copies ran while one was open for 0% -> 0% of each run, Pallas kernels for 3% -> 0%
where the time goes in v3:
time: 46.7 us; the launch traced here: 46.5 us
  starting transfers between devices  24.1 us (52%)
  waiting for transfers between devices  17.7 us (38%)
  Pallas kernels  4.04 us (9%)
  between operations  0.69 us (1%)
    ppermute x6, starting transfers between devices, along_line(): return lax.ppermute(block, 'src', moves)  10.8 us
    ppermute x6, waiting for transfers between devices, along_line(): return lax.ppermute(block, 'src', moves)  7.64 us
    ppermute x9, waiting for transfers between devices, gather_target(): lax.ppermute(block, 'tgt', [(i, partner(i, step, targets)) for i in range...  7.6 us
    ppermute x6, starting transfers between devices, across_pair(): lax.ppermute(block, 'src', [(i, i ^ 1) for i in range(lax.axis_size('src'...  7.3 us
    ppermute x9, starting transfers between devices, gather_target(): lax.ppermute(block, 'tgt', [(i, partner(i, step, targets)) for i in range...  5.99 us
    pallas_call x7, Pallas kernels, call(): pl.pallas_call(kernel, out_shape=tuple(outs), in_specs=[space] * len(give...  4.04 us
    ppermute x6, waiting for transfers between devices, across_pair(): lax.ppermute(block, 'src', [(i, i ^ 1) for i in range(lax.axis_size('src'...  2.48 us
  transfers between devices with their start and end apart: 21, of which 11 were waited for; matrix products, arithmetic and copies ran while one was open for 0% of the time, Pallas kernels for 0%

profile of v3, /device:TPU:0, one launch (start us, length us, event | category | flops | bytes accessed | tf_op | source)
XLA Modules:
  0.0 46.5 jit_solution(1023829675676268683)
XLA Ops:
  0.6 1.3 %shard_map.112 = (f32[160,128]{1,0:T(8,128)S(1)}, bf16[512,128]{1,0:T(8,128)(2,1)S(1)}) custom-call(s32[1,2]{1,0:T(1,128)} %bitcast.2, s32[1,2]{1,0:T(1,128)} %bitcast.3, bf16[2,1,128,128]{3,2,1,0:T(8,128)(2,1)} %refs_2_.1, bf16[2,1,128,128]{3,2,1,0:T(8,128)(2,1)} %refs_3_.1, f32[32,128]{1,0:T(8,128)} %refs_4_.1, f32[32,128]{1,0:T(8,128)} %refs_5_.1, ...), custom_call_target="tpu_custom_call" | custom-call | tf_op jit(solution)/shard_map/pallas_call | solution.py:193
  1.9 3.0 %collective-permute-start.2 = (bf16[512,128]{1,0:T(8,128)(2,1)S(1)}, bf16[512,128]{1,0:T(8,128)(2,1)S(1)}, u32[]{:S(2)}, u32[]{:S(2)}) collective-permute-start(bf16[512,128]{1,0:T(8,128)(2,1)S(1)} %get-tuple-element.21.refs_0_), channel_id=1, source_target_pairs={{0,1},{1,0},{2,3},{3,2},{4,5},{5,4},{6,7},{7,6},{8,9},{9,8},{10,11... | collective-permute-start | bytes 393224 | tf_op jit(solution)/shard_map/ppermute | solution.py:36
  4.9 2.6 %collective-permute-start.1 = (bf16[512,128]{1,0:T(8,128)(2,1)S(1)}, bf16[512,128]{1,0:T(8,128)(2,1)S(1)}, u32[]{:S(2)}, u32[]{:S(2)}) collective-permute-start(bf16[512,128]{1,0:T(8,128)(2,1)S(1)} %get-tuple-element.21.refs_0_), channel_id=1, source_target_pairs={{0,4},{1,5},{2,6},{3,7},{4,0},{5,1},{6,2},{7,3},{8,12},{9,13},{10,... | collective-permute-start | bytes 393224 | tf_op jit(solution)/shard_map/ppermute | solution.py:32
  7.5 0.5 %collective-permute-start.7 = (f32[160,128]{1,0:T(8,128)S(1)}, f32[160,128]{1,0:T(8,128)S(1)}, u32[]{:S(2)}, u32[]{:S(2)}) collective-permute-start(f32[160,128]{1,0:T(8,128)S(1)} %get-tuple-element.23.mine_ref), channel_id=1, source_target_pairs={{0,1},{1,0},{2,3},{3,2},{4,5},{5,4},{6,7},{7,6},{8,9},{9,8},{10,11... | collective-permute-start | bytes 245768 | tf_op jit(solution)/shard_map/ppermute | solution.py:36
  8.0 1.6 %collective-permute-start = (bf16[512,128]{1,0:T(8,128)(2,1)S(1)}, bf16[512,128]{1,0:T(8,128)(2,1)S(1)}, u32[]{:S(2)}, u32[]{:S(2)}) collective-permute-start(bf16[512,128]{1,0:T(8,128)(2,1)S(1)} %get-tuple-element.21.refs_0_), channel_id=1, source_target_pairs={{0,2},{1,3},{2,0},{3,1},{4,6},{5,7},{6,4},{7,5},{8,10},{9,11},{10,... | collective-permute-start | bytes 393224 | tf_op jit(solution)/shard_map/ppermute | solution.py:32
  9.6 4.1 %collective-permute-done.1.refs_2_ = bf16[512,128]{1,0:T(8,128)(2,1)S(1)} collective-permute-done((bf16[512,128]{1,0:T(8,128)(2,1)S(1)}, bf16[512,128]{1,0:T(8,128)(2,1)S(1)}, u32[]{:S(2)}, u32[]{:S(2)}) %collective-permute-start.1) | collective-permute-done | bytes 131104 | tf_op jit(solution)/shard_map/ppermute | solution.py:32
  13.7 0.6 %collective-permute-start.3 = (bf16[512,128]{1,0:T(8,128)(2,1)S(1)}, bf16[512,128]{1,0:T(8,128)(2,1)S(1)}, u32[]{:S(2)}, u32[]{:S(2)}) collective-permute-start(bf16[512,128]{1,0:T(8,128)(2,1)S(1)} %collective-permute-done.1.refs_2_), channel_id=1, source_target_pairs={{0,2},{1,3},{2,0},{3,1},{4,6},{5,7},{6,4},{7,5},{8,10},{9,11},{10,... | collective-permute-start | bytes 393224 | tf_op jit(solution)/shard_map/ppermute | solution.py:32
  14.3 3.4 %collective-permute-start.9 = (f32[160,128]{1,0:T(8,128)S(1)}, f32[160,128]{1,0:T(8,128)S(1)}, u32[]{:S(2)}, u32[]{:S(2)}) collective-permute-start(f32[160,128]{1,0:T(8,128)S(1)} %shard_map.113.refs_0_), channel_id=1, source_target_pairs={{0,4},{1,5},{2,6},{3,7},{4,0},{5,1},{6,2},{7,3},{8,12},{9,13},{10,... | collective-permute-start | bytes 245768 | tf_op jit(solution)/shard_map/ppermute | solution.py:32
  17.8 0.6 %collective-permute-start.5 = (bf16[512,128]{1,0:T(8,128)(2,1)S(1)}, bf16[512,128]{1,0:T(8,128)(2,1)S(1)}, u32[]{:S(2)}, u32[]{:S(2)}) collective-permute-start(bf16[512,128]{1,0:T(8,128)(2,1)S(1)} %collective-permute-done.1.refs_2_), channel_id=1, source_target_pairs={{0,1},{1,0},{2,3},{3,2},{4,5},{5,4},{6,7},{7,6},{8,9},{9,8},{10,11... | collective-permute-start | bytes 393224 | tf_op jit(solution)/shard_map/ppermute | solution.py:36
  18.4 1.4 %collective-permute-start.4 = (bf16[512,128]{1,0:T(8,128)(2,1)S(1)}, bf16[512,128]{1,0:T(8,128)(2,1)S(1)}, u32[]{:S(2)}, u32[]{:S(2)}) collective-permute-start(bf16[512,128]{1,0:T(8,128)(2,1)S(1)} %collective-permute-done.refs_1_), channel_id=1, source_target_pairs={{0,1},{1,0},{2,3},{3,2},{4,5},{5,4},{6,7},{7,6},{8,9},{9,8},{10,11... | collective-permute-start | bytes 393224 | tf_op jit(solution)/shard_map/ppermute | solution.py:36
  19.8 0.6 %collective-permute-done.3.refs_3_ = bf16[512,128]{1,0:T(8,128)(2,1)S(1)} collective-permute-done((bf16[512,128]{1,0:T(8,128)(2,1)S(1)}, bf16[512,128]{1,0:T(8,128)(2,1)S(1)}, u32[]{:S(2)}, u32[]{:S(2)}) %collective-permute-start.3) | collective-permute-done | bytes 131104 | tf_op jit(solution)/shard_map/ppermute | solution.py:32
  20.5 2.6 %collective-permute-start.10 = (f32[160,128]{1,0:T(8,128)S(1)}, f32[160,128]{1,0:T(8,128)S(1)}, u32[]{:S(2)}, u32[]{:S(2)}) collective-permute-start(f32[160,128]{1,0:T(8,128)S(1)} %collective-permute-done.9.refs_2_), channel_id=1, source_target_pairs={{0,2},{1,3},{2,0},{3,1},{4,6},{5,7},{6,4},{7,5},{8,10},{9,11},{10,... | collective-permute-start | bytes 245768 | tf_op jit(solution)/shard_map/ppermute | solution.py:32
  23.1 2.1 %collective-permute-done.8.refs_1_ = f32[160,128]{1,0:T(8,128)S(1)} collective-permute-done((f32[160,128]{1,0:T(8,128)S(1)}, f32[160,128]{1,0:T(8,128)S(1)}, u32[]{:S(2)}, u32[]{:S(2)}) %collective-permute-start.8) | collective-permute-done | bytes 81952 | tf_op jit(solution)/shard_map/ppermute | solution.py:32
  25.2 0.9 %collective-permute-done.10.refs_3_ = f32[160,128]{1,0:T(8,128)S(1)} collective-permute-done((f32[160,128]{1,0:T(8,128)S(1)}, f32[160,128]{1,0:T(8,128)S(1)}, u32[]{:S(2)}, u32[]{:S(2)}) %collective-permute-start.10) | collective-permute-done | bytes 81952 | tf_op jit(solution)/shard_map/ppermute | solution.py:32
  26.2 1.7 %collective-permute-start.12 = (bf16[128,128]{1,0:T(8,128)(2,1)S(1)}, bf16[128,128]{1,0:T(8,128)(2,1)S(1)}, u32[]{:S(2)}, u32[]{:S(2)}) collective-permute-start(bf16[128,128]{1,0:T(8,128)(2,1)S(1)} %get-tuple-element.24.refs_8_), channel_id=1, source_target_pairs={{0,16},{8,24},{16,0},{24,8},{1,17},{9,25},{17,1},{25,9},{2,18},{10... | collective-permute-start | bytes 98312 | tf_op jit(solution)/shard_map/ppermute | solution.py:55
  27.9 0.2 collective-permute-start.11
  28.1 1.7 %collective-permute-done.13.refs_11_ = bf16[128,128]{1,0:T(8,128)(2,1)S(1)} collective-permute-done((bf16[128,128]{1,0:T(8,128)(2,1)S(1)}, bf16[128,128]{1,0:T(8,128)(2,1)S(1)}, u32[]{:S(2)}, u32[]{:S(2)}) %collective-permute-start.13) | collective-permute-done | bytes 32800 | tf_op jit(solution)/shard_map/ppermute | solution.py:55
  29.7 0.5 %collective-permute-done.12.refs_10_ = bf16[128,128]{1,0:T(8,128)(2,1)S(1)} collective-permute-done((bf16[128,128]{1,0:T(8,128)(2,1)S(1)}, bf16[128,128]{1,0:T(8,128)(2,1)S(1)}, u32[]{:S(2)}, u32[]{:S(2)}) %collective-permute-start.12) | collective-permute-done | bytes 32800 | tf_op jit(solution)/shard_map/ppermute | solution.py:55
  30.2 0.9 %shard_map.115 = (f32[128,128]{1,0:T(8,128)S(1)}, f32[128,128]{1,0:T(8,128)S(1)}, f32[128,128]{1,0:T(8,128)S(1)}, bf16[128,128]{1,0:T(8,128)(2,1)S(1)}, bf16[512,1024]{1,0:T(8,128)(2,1)S(1)}) custom-call(bf16[512,128]{1,0:T(8,128)(2,1)S(1)} %get-tuple-element.21.refs_0_, bf16[512,128]{1,0:T(8,128)(2,1)S(1)} %collective-permute-done.refs_1_, ...), custom_call_target="tpu_custom_call" | custom-call | tf_op jit(solution)/shard_map/pallas_call | solution.py:193
  31.1 1.1 %collective-permute-start.16 = (bf16[128,128]{1,0:T(8,128)(2,1)S(1)}, bf16[128,128]{1,0:T(8,128)(2,1)S(1)}, u32[]{:S(2)}, u32[]{:S(2)}) collective-permute-start(bf16[128,128]{1,0:T(8,128)(2,1)S(1)} %get-tuple-element.31.refs_1_), channel_id=1, source_target_pairs={{0,24},{8,16},{16,8},{24,0},{1,25},{9,17},{17,9},{25,1},{2,26},{10... | collective-permute-start | bytes 98312 | tf_op jit(solution)/shard_map/ppermute | solution.py:55
  32.3 1.0 %collective-permute-start.15 = (bf16[128,128]{1,0:T(8,128)(2,1)S(1)}, bf16[128,128]{1,0:T(8,128)(2,1)S(1)}, u32[]{:S(2)}, u32[]{:S(2)}) collective-permute-start(bf16[128,128]{1,0:T(8,128)(2,1)S(1)} %get-tuple-element.31.refs_1_), channel_id=1, source_target_pairs={{0,16},{8,24},{16,0},{24,8},{1,17},{9,25},{17,1},{25,9},{2,18},{10... | collective-permute-start | bytes 98312 | tf_op jit(solution)/shard_map/ppermute | solution.py:55
  33.3 1.3 %collective-permute-done.16.refs_4_ = bf16[128,128]{1,0:T(8,128)(2,1)S(1)} collective-permute-done((bf16[128,128]{1,0:T(8,128)(2,1)S(1)}, bf16[128,128]{1,0:T(8,128)(2,1)S(1)}, u32[]{:S(2)}, u32[]{:S(2)}) %collective-permute-start.16) | collective-permute-done | bytes 32800 | tf_op jit(solution)/shard_map/ppermute | solution.py:55
  34.5 1.7 %collective-permute-done.15.refs_3_ = bf16[128,128]{1,0:T(8,128)(2,1)S(1)} collective-permute-done((bf16[128,128]{1,0:T(8,128)(2,1)S(1)}, bf16[128,128]{1,0:T(8,128)(2,1)S(1)}, u32[]{:S(2)}, u32[]{:S(2)}) %collective-permute-start.15) | collective-permute-done | bytes 32800 | tf_op jit(solution)/shard_map/ppermute | solution.py:55
  36.2 0.6 %shard_map.116 = (f32[128,128]{1,0:T(8,128)S(1)}, f32[128,128]{1,0:T(8,128)S(1)}, f32[128,128]{1,0:T(8,128)S(1)}, bf16[128,128]{1,0:T(8,128)(2,1)S(1)}) custom-call(bf16[512,1024]{1,0:T(8,128)(2,1)S(1)} %get-tuple-element.30.refs_0_, bf16[128,128]{1,0:T(8,128)(2,1)S(1)} %get-tuple-element.31.refs_1_, bf16[128,128]{1,0:T(8,128)(2,1)S(1)} %collective-permute-done.14.refs_2_, ...), custom_call_target="tpu_custom_call" | custom-call | tf_op jit(solution)/shard_map/pallas_call | solution.py:193
  37.0 1.4 %collective-permute-start.18 = (bf16[128,128]{1,0:T(8,128)(2,1)S(1)}, bf16[128,128]{1,0:T(8,128)(2,1)S(1)}, u32[]{:S(2)}, u32[]{:S(2)}) collective-permute-start(bf16[128,128]{1,0:T(8,128)(2,1)S(1)} %get-tuple-element.35.refs_1_), channel_id=1, source_target_pairs={{0,16},{8,24},{16,0},{24,8},{1,17},{9,25},{17,1},{25,9},{2,18},{10... | collective-permute-start | bytes 98312 | tf_op jit(solution)/shard_map/ppermute | solution.py:55
  38.4 0.4 collective-permute-start.17
  38.8 1.8 %collective-permute-done.19.refs_4_ = bf16[128,128]{1,0:T(8,128)(2,1)S(1)} collective-permute-done((bf16[128,128]{1,0:T(8,128)(2,1)S(1)}, bf16[128,128]{1,0:T(8,128)(2,1)S(1)}, u32[]{:S(2)}, u32[]{:S(2)}) %collective-permute-start.19) | collective-permute-done | bytes 32800 | tf_op jit(solution)/shard_map/ppermute | solution.py:55
  40.6 0.7 %collective-permute-done.18.refs_3_ = bf16[128,128]{1,0:T(8,128)(2,1)S(1)} collective-permute-done((bf16[128,128]{1,0:T(8,128)(2,1)S(1)}, bf16[128,128]{1,0:T(8,128)(2,1)S(1)}, u32[]{:S(2)}, u32[]{:S(2)}) %collective-permute-start.18) | collective-permute-done | bytes 32800 | tf_op jit(solution)/shard_map/ppermute | solution.py:55
  41.3 0.4 shard_map.117.mine_ref
  41.7 1.7 %collective-permute-start.20 = (f32[96,128]{1,0:T(8,128)S(1)}, f32[96,128]{1,0:T(8,128)S(1)}, u32[]{:S(2)}, u32[]{:S(2)}) collective-permute-start(f32[96,128]{1,0:T(8,128)S(1)} %shard_map.117.mine_ref), channel_id=1, source_target_pairs={{0,1},{1,0},{2,3},{3,2},{4,5},{5,4},{6,7},{7,6},{8,9},{9,8},{10,11... | collective-permute-start | bytes 147464 | tf_op jit(solution)/shard_map/ppermute | solution.py:36
  43.3 2.5 %collective-permute-done.20.theirs_ref = f32[96,128]{1,0:T(8,128)S(1)} collective-permute-done((f32[96,128]{1,0:T(8,128)S(1)}, f32[96,128]{1,0:T(8,128)S(1)}, u32[]{:S(2)}, u32[]{:S(2)}) %collective-permute-start.20) | collective-permute-done | bytes 49184 | tf_op jit(solution)/shard_map/ppermute | solution.py:36
  45.8 0.7 %shard_map.118 = (f32[32,128]{1,0:T(8,128)}, f32[32,128]{1,0:T(8,128)}, f32[32,128]{1,0:T(8,128)}) custom-call(f32[96,128]{1,0:T(8,128)S(1)} %shard_map.117.mine_ref, f32[96,128]{1,0:T(8,128)S(1)} %collective-permute-done.20.theirs_ref), custom_call_target="tpu_custom_call" | custom-call | tf_op jit(solution)/shard_map/pallas_call | solution.py:193
  (17 shorter events, 0.4 us)
Async XLA Ops:
  1.9 7.7 %collective-permute-start.2 = (bf16[512,128]{1,0:T(8,128)(2,1)S(1)}, bf16[512,128]{1,0:T(8,128)(2,1)S(1)}, u32[]{:S(2)}, u32[]{:S(2)}) collective-permute-start(bf16[512,128]{1,0:T(8,128)(2,1)S(1)} %get-tuple-element.21.refs_0_), channel_id=1, source_target_pairs={{0,1},{1,0},{2,3},{3,2},{4,5},{5,4},{6,7},{7,6},{8,9},{9,8},{10,11... | collective-permute-start | bytes 393224 | tf_op jit(solution)/shard_map/ppermute | solution.py:36
  4.9 8.8 %collective-permute-start.1 = (bf16[512,128]{1,0:T(8,128)(2,1)S(1)}, bf16[512,128]{1,0:T(8,128)(2,1)S(1)}, u32[]{:S(2)}, u32[]{:S(2)}) collective-permute-start(bf16[512,128]{1,0:T(8,128)(2,1)S(1)} %get-tuple-element.21.refs_0_), channel_id=1, source_target_pairs={{0,4},{1,5},{2,6},{3,7},{4,0},{5,1},{6,2},{7,3},{8,12},{9,13},{10,... | collective-permute-start | bytes 393224 | tf_op jit(solution)/shard_map/ppermute | solution.py:32
  7.5 6.8 %collective-permute-start.7 = (f32[160,128]{1,0:T(8,128)S(1)}, f32[160,128]{1,0:T(8,128)S(1)}, u32[]{:S(2)}, u32[]{:S(2)}) collective-permute-start(f32[160,128]{1,0:T(8,128)S(1)} %get-tuple-element.23.mine_ref), channel_id=1, source_target_pairs={{0,1},{1,0},{2,3},{3,2},{4,5},{5,4},{6,7},{7,6},{8,9},{9,8},{10,11... | collective-permute-start | bytes 245768 | tf_op jit(solution)/shard_map/ppermute | solution.py:36
  8.0 10.4 %collective-permute-start = (bf16[512,128]{1,0:T(8,128)(2,1)S(1)}, bf16[512,128]{1,0:T(8,128)(2,1)S(1)}, u32[]{:S(2)}, u32[]{:S(2)}) collective-permute-start(bf16[512,128]{1,0:T(8,128)(2,1)S(1)} %get-tuple-element.21.refs_0_), channel_id=1, source_target_pairs={{0,2},{1,3},{2,0},{3,1},{4,6},{5,7},{6,4},{7,5},{8,10},{9,11},{10,... | collective-permute-start | bytes 393224 | tf_op jit(solution)/shard_map/ppermute | solution.py:32
  13.7 6.7 %collective-permute-start.3 = (bf16[512,128]{1,0:T(8,128)(2,1)S(1)}, bf16[512,128]{1,0:T(8,128)(2,1)S(1)}, u32[]{:S(2)}, u32[]{:S(2)}) collective-permute-start(bf16[512,128]{1,0:T(8,128)(2,1)S(1)} %collective-permute-done.1.refs_2_), channel_id=1, source_target_pairs={{0,2},{1,3},{2,0},{3,1},{4,6},{5,7},{6,4},{7,5},{8,10},{9,11},{10,... | collective-permute-start | bytes 393224 | tf_op jit(solution)/shard_map/ppermute | solution.py:32
  14.3 6.1 %collective-permute-start.9 = (f32[160,128]{1,0:T(8,128)S(1)}, f32[160,128]{1,0:T(8,128)S(1)}, u32[]{:S(2)}, u32[]{:S(2)}) collective-permute-start(f32[160,128]{1,0:T(8,128)S(1)} %shard_map.113.refs_0_), channel_id=1, source_target_pairs={{0,4},{1,5},{2,6},{3,7},{4,0},{5,1},{6,2},{7,3},{8,12},{9,13},{10,... | collective-permute-start | bytes 245768 | tf_op jit(solution)/shard_map/ppermute | solution.py:32
  17.8 10.1 %collective-permute-start.5 = (bf16[512,128]{1,0:T(8,128)(2,1)S(1)}, bf16[512,128]{1,0:T(8,128)(2,1)S(1)}, u32[]{:S(2)}, u32[]{:S(2)}) collective-permute-start(bf16[512,128]{1,0:T(8,128)(2,1)S(1)} %collective-permute-done.1.refs_2_), channel_id=1, source_target_pairs={{0,1},{1,0},{2,3},{3,2},{4,5},{5,4},{6,7},{7,6},{8,9},{9,8},{10,11... | collective-permute-start | bytes 393224 | tf_op jit(solution)/shard_map/ppermute | solution.py:36
  18.4 9.6 %collective-permute-start.4 = (bf16[512,128]{1,0:T(8,128)(2,1)S(1)}, bf16[512,128]{1,0:T(8,128)(2,1)S(1)}, u32[]{:S(2)}, u32[]{:S(2)}) collective-permute-start(bf16[512,128]{1,0:T(8,128)(2,1)S(1)} %collective-permute-done.refs_1_), channel_id=1, source_target_pairs={{0,1},{1,0},{2,3},{3,2},{4,5},{5,4},{6,7},{7,6},{8,9},{9,8},{10,11... | collective-permute-start | bytes 393224 | tf_op jit(solution)/shard_map/ppermute | solution.py:36
  20.4 9.8 %collective-permute-start.6 = (bf16[512,128]{1,0:T(8,128)(2,1)S(1)}, bf16[512,128]{1,0:T(8,128)(2,1)S(1)}, u32[]{:S(2)}, u32[]{:S(2)}) collective-permute-start(bf16[512,128]{1,0:T(8,128)(2,1)S(1)} %collective-permute-done.3.refs_3_), channel_id=1, source_target_pairs={{0,1},{1,0},{2,3},{3,2},{4,5},{5,4},{6,7},{7,6},{8,9},{9,8},{10,11... | collective-permute-start | bytes 393224 | tf_op jit(solution)/shard_map/ppermute | solution.py:36
  20.5 4.7 %collective-permute-start.8 = (f32[160,128]{1,0:T(8,128)S(1)}, f32[160,128]{1,0:T(8,128)S(1)}, u32[]{:S(2)}, u32[]{:S(2)}) collective-permute-start(f32[160,128]{1,0:T(8,128)S(1)} %shard_map.113.refs_0_), channel_id=1, source_target_pairs={{0,2},{1,3},{2,0},{3,1},{4,6},{5,7},{6,4},{7,5},{8,10},{9,11},{10,... | collective-permute-start | bytes 245768 | tf_op jit(solution)/shard_map/ppermute | solution.py:32
  20.5 5.6 %collective-permute-start.10 = (f32[160,128]{1,0:T(8,128)S(1)}, f32[160,128]{1,0:T(8,128)S(1)}, u32[]{:S(2)}, u32[]{:S(2)}) collective-permute-start(f32[160,128]{1,0:T(8,128)S(1)} %collective-permute-done.9.refs_2_), channel_id=1, source_target_pairs={{0,2},{1,3},{2,0},{3,1},{4,6},{5,7},{6,4},{7,5},{8,10},{9,11},{10,... | collective-permute-start | bytes 245768 | tf_op jit(solution)/shard_map/ppermute | solution.py:32
  26.1 3.6 %collective-permute-start.13 = (bf16[128,128]{1,0:T(8,128)(2,1)S(1)}, bf16[128,128]{1,0:T(8,128)(2,1)S(1)}, u32[]{:S(2)}, u32[]{:S(2)}) collective-permute-start(bf16[128,128]{1,0:T(8,128)(2,1)S(1)} %get-tuple-element.24.refs_8_), channel_id=1, source_target_pairs={{0,24},{8,16},{16,8},{24,0},{1,25},{9,17},{17,9},{25,1},{2,26},{10... | collective-permute-start | bytes 98312 | tf_op jit(solution)/shard_map/ppermute | solution.py:55
  26.2 4.0 %collective-permute-start.12 = (bf16[128,128]{1,0:T(8,128)(2,1)S(1)}, bf16[128,128]{1,0:T(8,128)(2,1)S(1)}, u32[]{:S(2)}, u32[]{:S(2)}) collective-permute-start(bf16[128,128]{1,0:T(8,128)(2,1)S(1)} %get-tuple-element.24.refs_8_), channel_id=1, source_target_pairs={{0,16},{8,24},{16,0},{24,8},{1,17},{9,25},{17,1},{25,9},{2,18},{10... | collective-permute-start | bytes 98312 | tf_op jit(solution)/shard_map/ppermute | solution.py:55
  27.9 2.4 %collective-permute-start.11 = (bf16[128,128]{1,0:T(8,128)(2,1)S(1)}, bf16[128,128]{1,0:T(8,128)(2,1)S(1)}, u32[]{:S(2)}, u32[]{:S(2)}) collective-permute-start(bf16[128,128]{1,0:T(8,128)(2,1)S(1)} %get-tuple-element.24.refs_8_), channel_id=1, source_target_pairs={{0,8},{8,0},{16,24},{24,16},{1,9},{9,1},{17,25},{25,17},{2,10},{10... | collective-permute-start | bytes 98312 | tf_op jit(solution)/shard_map/ppermute | solution.py:55
  31.1 3.4 %collective-permute-start.16 = (bf16[128,128]{1,0:T(8,128)(2,1)S(1)}, bf16[128,128]{1,0:T(8,128)(2,1)S(1)}, u32[]{:S(2)}, u32[]{:S(2)}) collective-permute-start(bf16[128,128]{1,0:T(8,128)(2,1)S(1)} %get-tuple-element.31.refs_1_), channel_id=1, source_target_pairs={{0,24},{8,16},{16,8},{24,0},{1,25},{9,17},{17,9},{25,1},{2,26},{10... | collective-permute-start | bytes 98312 | tf_op jit(solution)/shard_map/ppermute | solution.py:55
  32.3 3.9 %collective-permute-start.15 = (bf16[128,128]{1,0:T(8,128)(2,1)S(1)}, bf16[128,128]{1,0:T(8,128)(2,1)S(1)}, u32[]{:S(2)}, u32[]{:S(2)}) collective-permute-start(bf16[128,128]{1,0:T(8,128)(2,1)S(1)} %get-tuple-element.31.refs_1_), channel_id=1, source_target_pairs={{0,16},{8,24},{16,0},{24,8},{1,17},{9,25},{17,1},{25,9},{2,18},{10... | collective-permute-start | bytes 98312 | tf_op jit(solution)/shard_map/ppermute | solution.py:55
  33.3 2.9 %collective-permute-start.14 = (bf16[128,128]{1,0:T(8,128)(2,1)S(1)}, bf16[128,128]{1,0:T(8,128)(2,1)S(1)}, u32[]{:S(2)}, u32[]{:S(2)}) collective-permute-start(bf16[128,128]{1,0:T(8,128)(2,1)S(1)} %get-tuple-element.31.refs_1_), channel_id=1, source_target_pairs={{0,8},{8,0},{16,24},{24,16},{1,9},{9,1},{17,25},{25,17},{2,10},{10... | collective-permute-start | bytes 98312 | tf_op jit(solution)/shard_map/ppermute | solution.py:55
  36.9 3.8 %collective-permute-start.19 = (bf16[128,128]{1,0:T(8,128)(2,1)S(1)}, bf16[128,128]{1,0:T(8,128)(2,1)S(1)}, u32[]{:S(2)}, u32[]{:S(2)}) collective-permute-start(bf16[128,128]{1,0:T(8,128)(2,1)S(1)} %get-tuple-element.35.refs_1_), channel_id=1, source_target_pairs={{0,24},{8,16},{16,8},{24,0},{1,25},{9,17},{17,9},{25,1},{2,26},{10... | collective-permute-start | bytes 98312 | tf_op jit(solution)/shard_map/ppermute | solution.py:55
  37.0 4.3 %collective-permute-start.18 = (bf16[128,128]{1,0:T(8,128)(2,1)S(1)}, bf16[128,128]{1,0:T(8,128)(2,1)S(1)}, u32[]{:S(2)}, u32[]{:S(2)}) collective-permute-start(bf16[128,128]{1,0:T(8,128)(2,1)S(1)} %get-tuple-element.35.refs_1_), channel_id=1, source_target_pairs={{0,16},{8,24},{16,0},{24,8},{1,17},{9,25},{17,1},{25,9},{2,18},{10... | collective-permute-start | bytes 98312 | tf_op jit(solution)/shard_map/ppermute | solution.py:55
  38.4 2.9 %collective-permute-start.17 = (bf16[128,128]{1,0:T(8,128)(2,1)S(1)}, bf16[128,128]{1,0:T(8,128)(2,1)S(1)}, u32[]{:S(2)}, u32[]{:S(2)}) collective-permute-start(bf16[128,128]{1,0:T(8,128)(2,1)S(1)} %get-tuple-element.35.refs_1_), channel_id=1, source_target_pairs={{0,8},{8,0},{16,24},{24,16},{1,9},{9,1},{17,25},{25,17},{2,10},{10... | collective-permute-start | bytes 98312 | tf_op jit(solution)/shard_map/ppermute | solution.py:55
  41.7 4.1 %collective-permute-start.20 = (f32[96,128]{1,0:T(8,128)S(1)}, f32[96,128]{1,0:T(8,128)S(1)}, u32[]{:S(2)}, u32[]{:S(2)}) collective-permute-start(f32[96,128]{1,0:T(8,128)S(1)} %shard_map.117.mine_ref), channel_id=1, source_target_pairs={{0,1},{1,0},{2,3},{3,2},{4,5},{5,4},{6,7},{7,6},{8,9},{9,8},{10,11... | collective-permute-start | bytes 147464 | tf_op jit(solution)/shard_map/ppermute | solution.py:36

commit v4 on v3

--- a/solution.py
+++ b/solution.py
@@ -113,14 +113,16 @@
 
 
 def unpack_kernel(count, *refs):
-    blocks, outs, dev_ref = refs[: -count - 1], refs[-count - 1 : -1], refs[-1]
+    blocks, outs, (dev_ref, slips) = refs[: -count - 2], refs[-count - 2 : -2], refs[-2:]
+    blocks, slips_in = blocks[: len(blocks) // 2], blocks[len(blocks) // 2 :]
     own = blocks[0].shape[0] // count
     far = lax.axis_index("src") // 2
-    for step, block in enumerate(blocks):
+    for step, (block, slip_in) in enumerate(zip(blocks, slips_in)):
         start = pl.multiple_of(origin(far, step, len(blocks)) * own, own)
+        slips[pl.ds(start, own)] = slip_in[...]
         for i, out in enumerate(outs):
             out[pl.ds(start, own)] = block[i * own : (i + 1) * own]
-    dev_ref[...] = deviation_of(friction(*(out[...] for out in outs[:4])))
+    dev_ref[...] = deviation_of(slips[...])
 
 
 def stage_kernel(stage, own, dense_count, targets, *refs):
@@ -226,11 +228,15 @@
     )
     (joined,) = call(join_kernel, (floats(len(arrays) * own),), (packed, across_pair(packed)))
     joined_blocks = gather_line(joined)
+    first_slips = [friction(*jnp.split(value, len(arrays))[:4]) for value in joined_blocks]
     other = across_pair(dense)
     held = gather_line(dense, (other,))
     dense_blocks = held + [other] + [across_pair(value) for value in held[1:]]
     *begin, all_a, all_h, dev = call(
-        functools.partial(unpack_kernel, len(arrays)), (wide,) * len(arrays) + (dev_type,), joined_blocks
+        functools.partial(unpack_kernel, len(arrays)),
+        (wide,) * len(arrays) + (dev_type,),
+        joined_blocks + first_slips,
+        [pltpu.VMEM(wide.shape, wide.dtype)],
     )
     now = ()
     matrix_type = jax.ShapeDtypeStruct((2 * rows, sources * leaf_cols * block), jnp.bfloat16)

time: 46.7 us -> 43.4 us (0.929)
  waiting for transfers between devices: 17.7 us -> 14.8 us
  starting transfers between devices: 24.1 us -> 23.6 us
    ppermute x6, waiting for transfers between devices: 7.64 us -> 4.11 us  [along_line(): return lax.ppermute(block, 'src', moves)]
    ppermute x6, starting transfers between devices: 10.8 us -> 9.48 us  [along_line(): return lax.ppermute(block, 'src', moves)]
    ppermute x6, starting transfers between devices: 7.3 us -> 8.19 us  [across_pair(): lax.ppermute(block, 'src', [(i, i ^ 1) for i in range(lax.axis_size('src'...]
    ppermute x6, waiting for transfers between devices: 2.48 us -> 3.11 us  [across_pair(): lax.ppermute(block, 'src', [(i, i ^ 1) for i in range(lax.axis_size('src'...]
  transfers between devices with their start and end apart: 21 -> 21, of which waited for: 11 -> 9; matrix products, arithmetic and copies ran while one was open for 0% -> 0% of each run, Pallas kernels for 0% -> 0%
where the time goes in v4:
time: 43.4 us; the launch traced here: 43.2 us
  starting transfers between devices  23.6 us (54%)
  waiting for transfers between devices  14.8 us (34%)
  Pallas kernels  4.01 us (9%)
  between operations  0.72 us (2%)
    ppermute x6, starting transfers between devices, along_line(): return lax.ppermute(block, 'src', moves)  9.48 us
    ppermute x6, starting transfers between devices, across_pair(): lax.ppermute(block, 'src', [(i, i ^ 1) for i in range(lax.axis_size('src'...  8.19 us
    ppermute x9, waiting for transfers between devices, gather_target(): lax.ppermute(block, 'tgt', [(i, partner(i, step, targets)) for i in range...  7.6 us
    ppermute x9, starting transfers between devices, gather_target(): lax.ppermute(block, 'tgt', [(i, partner(i, step, targets)) for i in range...  5.9 us
    ppermute x6, waiting for transfers between devices, along_line(): return lax.ppermute(block, 'src', moves)  4.11 us
    pallas_call x7, Pallas kernels, call(): pl.pallas_call(kernel, out_shape=tuple(outs), in_specs=[space] * len(give...  4.01 us
    ppermute x6, waiting for transfers between devices, across_pair(): lax.ppermute(block, 'src', [(i, i ^ 1) for i in range(lax.axis_size('src'...  3.11 us
  transfers between devices with their start and end apart: 21, of which 9 were waited for; matrix products, arithmetic and copies ran while one was open for 0% of the time, Pallas kernels for 0%

profile of v4, /device:TPU:0, one launch (start us, length us, event | category | flops | bytes accessed | tf_op | source)
XLA Modules:
  0.0 43.2 jit_solution(6513393885587627273)
XLA Ops:
  0.6 1.3 %shard_map.112 = (f32[160,128]{1,0:T(8,128)S(1)}, bf16[512,128]{1,0:T(8,128)(2,1)S(1)}) custom-call(s32[1,2]{1,0:T(1,128)} %bitcast.2, s32[1,2]{1,0:T(1,128)} %bitcast.3, bf16[2,1,128,128]{3,2,1,0:T(8,128)(2,1)} %refs_2_.1, bf16[2,1,128,128]{3,2,1,0:T(8,128)(2,1)} %refs_3_.1, f32[32,128]{1,0:T(8,128)} %refs_4_.1, f32[32,128]{1,0:T(8,128)} %refs_5_.1, ...), custom_call_target="tpu_custom_call" | custom-call | tf_op jit(solution)/shard_map/pallas_call | solution.py:195
  1.9 3.0 %collective-permute-start.7 = (f32[160,128]{1,0:T(8,128)S(1)}, f32[160,128]{1,0:T(8,128)S(1)}, u32[]{:S(2)}, u32[]{:S(2)}) collective-permute-start(f32[160,128]{1,0:T(8,128)S(1)} %get-tuple-element.23.mine_ref), channel_id=1, source_target_pairs={{0,1},{1,0},{2,3},{3,2},{4,5},{5,4},{6,7},{7,6},{8,9},{9,8},{10,11... | collective-permute-start | bytes 245768 | tf_op jit(solution)/shard_map/ppermute | solution.py:36
  5.0 3.0 %collective-permute-start.1 = (bf16[512,128]{1,0:T(8,128)(2,1)S(1)}, bf16[512,128]{1,0:T(8,128)(2,1)S(1)}, u32[]{:S(2)}, u32[]{:S(2)}) collective-permute-start(bf16[512,128]{1,0:T(8,128)(2,1)S(1)} %get-tuple-element.21.refs_0_), channel_id=1, source_target_pairs={{0,4},{1,5},{2,6},{3,7},{4,0},{5,1},{6,2},{7,3},{8,12},{9,13},{10,... | collective-permute-start | bytes 393224 | tf_op jit(solution)/shard_map/ppermute | solution.py:32
  8.0 1.6 %collective-permute-start = (bf16[512,128]{1,0:T(8,128)(2,1)S(1)}, bf16[512,128]{1,0:T(8,128)(2,1)S(1)}, u32[]{:S(2)}, u32[]{:S(2)}) collective-permute-start(bf16[512,128]{1,0:T(8,128)(2,1)S(1)} %get-tuple-element.21.refs_0_), channel_id=1, source_target_pairs={{0,2},{1,3},{2,0},{3,1},{4,6},{5,7},{6,4},{7,5},{8,10},{9,11},{10,... | collective-permute-start | bytes 393224 | tf_op jit(solution)/shard_map/ppermute | solution.py:32
  9.7 1.7 %collective-permute-start.9 = (f32[160,128]{1,0:T(8,128)S(1)}, f32[160,128]{1,0:T(8,128)S(1)}, u32[]{:S(2)}, u32[]{:S(2)}) collective-permute-start(f32[160,128]{1,0:T(8,128)S(1)} %shard_map.113.refs_0_), channel_id=1, source_target_pairs={{0,4},{1,5},{2,6},{3,7},{4,0},{5,1},{6,2},{7,3},{8,12},{9,13},{10,... | collective-permute-start | bytes 245768 | tf_op jit(solution)/shard_map/ppermute | solution.py:32
  11.4 1.6 %collective-permute-start.8 = (f32[160,128]{1,0:T(8,128)S(1)}, f32[160,128]{1,0:T(8,128)S(1)}, u32[]{:S(2)}, u32[]{:S(2)}) collective-permute-start(f32[160,128]{1,0:T(8,128)S(1)} %shard_map.113.refs_0_), channel_id=1, source_target_pairs={{0,2},{1,3},{2,0},{3,1},{4,6},{5,7},{6,4},{7,5},{8,10},{9,11},{10,... | collective-permute-start | bytes 245768 | tf_op jit(solution)/shard_map/ppermute | solution.py:32
  13.1 2.5 %collective-permute-done.1.refs_2_ = bf16[512,128]{1,0:T(8,128)(2,1)S(1)} collective-permute-done((bf16[512,128]{1,0:T(8,128)(2,1)S(1)}, bf16[512,128]{1,0:T(8,128)(2,1)S(1)}, u32[]{:S(2)}, u32[]{:S(2)}) %collective-permute-start.1) | collective-permute-done | bytes 131104 | tf_op jit(solution)/shard_map/ppermute | solution.py:32
  15.6 0.3 collective-permute-start.3
  15.9 1.5 %collective-permute-start.5 = (bf16[512,128]{1,0:T(8,128)(2,1)S(1)}, bf16[512,128]{1,0:T(8,128)(2,1)S(1)}, u32[]{:S(2)}, u32[]{:S(2)}) collective-permute-start(bf16[512,128]{1,0:T(8,128)(2,1)S(1)} %collective-permute-done.1.refs_2_), channel_id=1, source_target_pairs={{0,1},{1,0},{2,3},{3,2},{4,5},{5,4},{6,7},{7,6},{8,9},{9,8},{10,11... | collective-permute-start | bytes 393224 | tf_op jit(solution)/shard_map/ppermute | solution.py:36
  17.4 1.0 %collective-permute-start.4 = (bf16[512,128]{1,0:T(8,128)(2,1)S(1)}, bf16[512,128]{1,0:T(8,128)(2,1)S(1)}, u32[]{:S(2)}, u32[]{:S(2)}) collective-permute-start(bf16[512,128]{1,0:T(8,128)(2,1)S(1)} %collective-permute-done.refs_1_), channel_id=1, source_target_pairs={{0,1},{1,0},{2,3},{3,2},{4,5},{5,4},{6,7},{7,6},{8,9},{9,8},{10,11... | collective-permute-start | bytes 393224 | tf_op jit(solution)/shard_map/ppermute | solution.py:36
  18.4 1.2 %collective-permute-start.10 = (f32[160,128]{1,0:T(8,128)S(1)}, f32[160,128]{1,0:T(8,128)S(1)}, u32[]{:S(2)}, u32[]{:S(2)}) collective-permute-start(f32[160,128]{1,0:T(8,128)S(1)} %collective-permute-done.9.refs_2_), channel_id=1, source_target_pairs={{0,2},{1,3},{2,0},{3,1},{4,6},{5,7},{6,4},{7,5},{8,10},{9,11},{10,... | collective-permute-start | bytes 245768 | tf_op jit(solution)/shard_map/ppermute | solution.py:32
  19.7 1.6 %collective-permute-done.3.refs_3_ = bf16[512,128]{1,0:T(8,128)(2,1)S(1)} collective-permute-done((bf16[512,128]{1,0:T(8,128)(2,1)S(1)}, bf16[512,128]{1,0:T(8,128)(2,1)S(1)}, u32[]{:S(2)}, u32[]{:S(2)}) %collective-permute-start.3) | collective-permute-done | bytes 131104 | tf_op jit(solution)/shard_map/ppermute | solution.py:32
  21.3 1.5 %collective-permute-start.6 = (bf16[512,128]{1,0:T(8,128)(2,1)S(1)}, bf16[512,128]{1,0:T(8,128)(2,1)S(1)}, u32[]{:S(2)}, u32[]{:S(2)}) collective-permute-start(bf16[512,128]{1,0:T(8,128)(2,1)S(1)} %collective-permute-done.3.refs_3_), channel_id=1, source_target_pairs={{0,1},{1,0},{2,3},{3,2},{4,5},{5,4},{6,7},{7,6},{8,9},{9,8},{10,11... | collective-permute-start | bytes 393224 | tf_op jit(solution)/shard_map/ppermute | solution.py:36
  23.0 1.6 %collective-permute-start.12 = (bf16[128,128]{1,0:T(8,128)(2,1)S(1)}, bf16[128,128]{1,0:T(8,128)(2,1)S(1)}, u32[]{:S(2)}, u32[]{:S(2)}) collective-permute-start(bf16[128,128]{1,0:T(8,128)(2,1)S(1)} %get-tuple-element.24.refs_8_), channel_id=1, source_target_pairs={{0,16},{8,24},{16,0},{24,8},{1,17},{9,25},{17,1},{25,9},{2,18},{10... | collective-permute-start | bytes 98312 | tf_op jit(solution)/shard_map/ppermute | solution.py:55
  24.6 0.3 collective-permute-start.11
  24.9 1.7 %collective-permute-done.13.refs_11_ = bf16[128,128]{1,0:T(8,128)(2,1)S(1)} collective-permute-done((bf16[128,128]{1,0:T(8,128)(2,1)S(1)}, bf16[128,128]{1,0:T(8,128)(2,1)S(1)}, u32[]{:S(2)}, u32[]{:S(2)}) %collective-permute-start.13) | collective-permute-done | bytes 32800 | tf_op jit(solution)/shard_map/ppermute | solution.py:55
  26.6 0.4 collective-permute-done.12.refs_10_
  27.1 0.9 %shard_map.115 = (f32[128,128]{1,0:T(8,128)S(1)}, f32[128,128]{1,0:T(8,128)S(1)}, f32[128,128]{1,0:T(8,128)S(1)}, bf16[128,128]{1,0:T(8,128)(2,1)S(1)}, bf16[512,1024]{1,0:T(8,128)(2,1)S(1)}) custom-call(bf16[512,128]{1,0:T(8,128)(2,1)S(1)} %get-tuple-element.21.refs_0_, bf16[512,128]{1,0:T(8,128)(2,1)S(1)} %collective-permute-done.refs_1_, ...), custom_call_target="tpu_custom_call" | custom-call | tf_op jit(solution)/shard_map/pallas_call | solution.py:195
  27.9 1.0 %collective-permute-start.16 = (bf16[128,128]{1,0:T(8,128)(2,1)S(1)}, bf16[128,128]{1,0:T(8,128)(2,1)S(1)}, u32[]{:S(2)}, u32[]{:S(2)}) collective-permute-start(bf16[128,128]{1,0:T(8,128)(2,1)S(1)} %get-tuple-element.31.refs_1_), channel_id=1, source_target_pairs={{0,24},{8,16},{16,8},{24,0},{1,25},{9,17},{17,9},{25,1},{2,26},{10... | collective-permute-start | bytes 98312 | tf_op jit(solution)/shard_map/ppermute | solution.py:55
  29.0 1.0 %collective-permute-start.15 = (bf16[128,128]{1,0:T(8,128)(2,1)S(1)}, bf16[128,128]{1,0:T(8,128)(2,1)S(1)}, u32[]{:S(2)}, u32[]{:S(2)}) collective-permute-start(bf16[128,128]{1,0:T(8,128)(2,1)S(1)} %get-tuple-element.31.refs_1_), channel_id=1, source_target_pairs={{0,16},{8,24},{16,0},{24,8},{1,17},{9,25},{17,1},{25,9},{2,18},{10... | collective-permute-start | bytes 98312 | tf_op jit(solution)/shard_map/ppermute | solution.py:55
  30.0 1.4 %collective-permute-done.16.refs_4_ = bf16[128,128]{1,0:T(8,128)(2,1)S(1)} collective-permute-done((bf16[128,128]{1,0:T(8,128)(2,1)S(1)}, bf16[128,128]{1,0:T(8,128)(2,1)S(1)}, u32[]{:S(2)}, u32[]{:S(2)}) %collective-permute-start.16) | collective-permute-done | bytes 32800 | tf_op jit(solution)/shard_map/ppermute | solution.py:55
  31.4 1.6 %collective-permute-done.15.refs_3_ = bf16[128,128]{1,0:T(8,128)(2,1)S(1)} collective-permute-done((bf16[128,128]{1,0:T(8,128)(2,1)S(1)}, bf16[128,128]{1,0:T(8,128)(2,1)S(1)}, u32[]{:S(2)}, u32[]{:S(2)}) %collective-permute-start.15) | collective-permute-done | bytes 32800 | tf_op jit(solution)/shard_map/ppermute | solution.py:55
  32.9 0.6 %shard_map.116 = (f32[128,128]{1,0:T(8,128)S(1)}, f32[128,128]{1,0:T(8,128)S(1)}, f32[128,128]{1,0:T(8,128)S(1)}, bf16[128,128]{1,0:T(8,128)(2,1)S(1)}) custom-call(bf16[512,1024]{1,0:T(8,128)(2,1)S(1)} %get-tuple-element.30.refs_0_, bf16[128,128]{1,0:T(8,128)(2,1)S(1)} %get-tuple-element.31.refs_1_, bf16[128,128]{1,0:T(8,128)(2,1)S(1)} %collective-permute-done.14.refs_2_, ...), custom_call_target="tpu_custom_call" | custom-call | tf_op jit(solution)/shard_map/pallas_call | solution.py:195
  33.6 0.1 collective-permute-start.19
  33.7 1.4 %collective-permute-start.18 = (bf16[128,128]{1,0:T(8,128)(2,1)S(1)}, bf16[128,128]{1,0:T(8,128)(2,1)S(1)}, u32[]{:S(2)}, u32[]{:S(2)}) collective-permute-start(bf16[128,128]{1,0:T(8,128)(2,1)S(1)} %get-tuple-element.35.refs_1_), channel_id=1, source_target_pairs={{0,16},{8,24},{16,0},{24,8},{1,17},{9,25},{17,1},{25,9},{2,18},{10... | collective-permute-start | bytes 98312 | tf_op jit(solution)/shard_map/ppermute | solution.py:55
  35.1 0.4 %collective-permute-start.17 = (bf16[128,128]{1,0:T(8,128)(2,1)S(1)}, bf16[128,128]{1,0:T(8,128)(2,1)S(1)}, u32[]{:S(2)}, u32[]{:S(2)}) collective-permute-start(bf16[128,128]{1,0:T(8,128)(2,1)S(1)} %get-tuple-element.35.refs_1_), channel_id=1, source_target_pairs={{0,8},{8,0},{16,24},{24,16},{1,9},{9,1},{17,25},{25,17},{2,10},{10... | collective-permute-start | bytes 98312 | tf_op jit(solution)/shard_map/ppermute | solution.py:55
  35.5 1.8 %collective-permute-done.19.refs_4_ = bf16[128,128]{1,0:T(8,128)(2,1)S(1)} collective-permute-done((bf16[128,128]{1,0:T(8,128)(2,1)S(1)}, bf16[128,128]{1,0:T(8,128)(2,1)S(1)}, u32[]{:S(2)}, u32[]{:S(2)}) %collective-permute-start.19) | collective-permute-done | bytes 32800 | tf_op jit(solution)/shard_map/ppermute | solution.py:55
  37.3 0.7 %collective-permute-done.18.refs_3_ = bf16[128,128]{1,0:T(8,128)(2,1)S(1)} collective-permute-done((bf16[128,128]{1,0:T(8,128)(2,1)S(1)}, bf16[128,128]{1,0:T(8,128)(2,1)S(1)}, u32[]{:S(2)}, u32[]{:S(2)}) %collective-permute-start.18) | collective-permute-done | bytes 32800 | tf_op jit(solution)/shard_map/ppermute | solution.py:55
  38.0 0.4 shard_map.117.mine_ref
  38.4 1.0 %collective-permute-start.20 = (f32[96,128]{1,0:T(8,128)S(1)}, f32[96,128]{1,0:T(8,128)S(1)}, u32[]{:S(2)}, u32[]{:S(2)}) collective-permute-start(f32[96,128]{1,0:T(8,128)S(1)} %shard_map.117.mine_ref), channel_id=1, source_target_pairs={{0,1},{1,0},{2,3},{3,2},{4,5},{5,4},{6,7},{7,6},{8,9},{9,8},{10,11... | collective-permute-start | bytes 147464 | tf_op jit(solution)/shard_map/ppermute | solution.py:36
  39.4 3.1 %collective-permute-done.20.theirs_ref = f32[96,128]{1,0:T(8,128)S(1)} collective-permute-done((f32[96,128]{1,0:T(8,128)S(1)}, f32[96,128]{1,0:T(8,128)S(1)}, u32[]{:S(2)}, u32[]{:S(2)}) %collective-permute-start.20) | collective-permute-done | bytes 49184 | tf_op jit(solution)/shard_map/ppermute | solution.py:36
  42.5 0.7 %shard_map.118 = (f32[32,128]{1,0:T(8,128)}, f32[32,128]{1,0:T(8,128)}, f32[32,128]{1,0:T(8,128)}) custom-call(f32[96,128]{1,0:T(8,128)S(1)} %shard_map.117.mine_ref, f32[96,128]{1,0:T(8,128)S(1)} %collective-permute-done.20.theirs_ref), custom_call_target="tpu_custom_call" | custom-call | tf_op jit(solution)/shard_map/pallas_call | solution.py:195
  (21 shorter events, 0.4 us)
Async XLA Ops:
  1.9 7.7 %collective-permute-start.7 = (f32[160,128]{1,0:T(8,128)S(1)}, f32[160,128]{1,0:T(8,128)S(1)}, u32[]{:S(2)}, u32[]{:S(2)}) collective-permute-start(f32[160,128]{1,0:T(8,128)S(1)} %get-tuple-element.23.mine_ref), channel_id=1, source_target_pairs={{0,1},{1,0},{2,3},{3,2},{4,5},{5,4},{6,7},{7,6},{8,9},{9,8},{10,11... | collective-permute-start | bytes 245768 | tf_op jit(solution)/shard_map/ppermute | solution.py:36
  4.9 8.2 %collective-permute-start.2 = (bf16[512,128]{1,0:T(8,128)(2,1)S(1)}, bf16[512,128]{1,0:T(8,128)(2,1)S(1)}, u32[]{:S(2)}, u32[]{:S(2)}) collective-permute-start(bf16[512,128]{1,0:T(8,128)(2,1)S(1)} %get-tuple-element.21.refs_0_), channel_id=1, source_target_pairs={{0,1},{1,0},{2,3},{3,2},{4,5},{5,4},{6,7},{7,6},{8,9},{9,8},{10,11... | collective-permute-start | bytes 393224 | tf_op jit(solution)/shard_map/ppermute | solution.py:36
  5.0 10.6 %collective-permute-start.1 = (bf16[512,128]{1,0:T(8,128)(2,1)S(1)}, bf16[512,128]{1,0:T(8,128)(2,1)S(1)}, u32[]{:S(2)}, u32[]{:S(2)}) collective-permute-start(bf16[512,128]{1,0:T(8,128)(2,1)S(1)} %get-tuple-element.21.refs_0_), channel_id=1, source_target_pairs={{0,4},{1,5},{2,6},{3,7},{4,0},{5,1},{6,2},{7,3},{8,12},{9,13},{10,... | collective-permute-start | bytes 393224 | tf_op jit(solution)/shard_map/ppermute | solution.py:32
  8.0 9.3 %collective-permute-start = (bf16[512,128]{1,0:T(8,128)(2,1)S(1)}, bf16[512,128]{1,0:T(8,128)(2,1)S(1)}, u32[]{:S(2)}, u32[]{:S(2)}) collective-permute-start(bf16[512,128]{1,0:T(8,128)(2,1)S(1)} %get-tuple-element.21.refs_0_), channel_id=1, source_target_pairs={{0,2},{1,3},{2,0},{3,1},{4,6},{5,7},{6,4},{7,5},{8,10},{9,11},{10,... | collective-permute-start | bytes 393224 | tf_op jit(solution)/shard_map/ppermute | solution.py:32
  9.7 8.7 %collective-permute-start.9 = (f32[160,128]{1,0:T(8,128)S(1)}, f32[160,128]{1,0:T(8,128)S(1)}, u32[]{:S(2)}, u32[]{:S(2)}) collective-permute-start(f32[160,128]{1,0:T(8,128)S(1)} %shard_map.113.refs_0_), channel_id=1, source_target_pairs={{0,4},{1,5},{2,6},{3,7},{4,0},{5,1},{6,2},{7,3},{8,12},{9,13},{10,... | collective-permute-start | bytes 245768 | tf_op jit(solution)/shard_map/ppermute | solution.py:32
  11.4 8.2 %collective-permute-start.8 = (f32[160,128]{1,0:T(8,128)S(1)}, f32[160,128]{1,0:T(8,128)S(1)}, u32[]{:S(2)}, u32[]{:S(2)}) collective-permute-start(f32[160,128]{1,0:T(8,128)S(1)} %shard_map.113.refs_0_), channel_id=1, source_target_pairs={{0,2},{1,3},{2,0},{3,1},{4,6},{5,7},{6,4},{7,5},{8,10},{9,11},{10,... | collective-permute-start | bytes 245768 | tf_op jit(solution)/shard_map/ppermute | solution.py:32
  15.6 5.7 %collective-permute-start.3 = (bf16[512,128]{1,0:T(8,128)(2,1)S(1)}, bf16[512,128]{1,0:T(8,128)(2,1)S(1)}, u32[]{:S(2)}, u32[]{:S(2)}) collective-permute-start(bf16[512,128]{1,0:T(8,128)(2,1)S(1)} %collective-permute-done.1.refs_2_), channel_id=1, source_target_pairs={{0,2},{1,3},{2,0},{3,1},{4,6},{5,7},{6,4},{7,5},{8,10},{9,11},{10,... | collective-permute-start | bytes 393224 | tf_op jit(solution)/shard_map/ppermute | solution.py:32
  15.9 8.7 %collective-permute-start.5 = (bf16[512,128]{1,0:T(8,128)(2,1)S(1)}, bf16[512,128]{1,0:T(8,128)(2,1)S(1)}, u32[]{:S(2)}, u32[]{:S(2)}) collective-permute-start(bf16[512,128]{1,0:T(8,128)(2,1)S(1)} %collective-permute-done.1.refs_2_), channel_id=1, source_target_pairs={{0,1},{1,0},{2,3},{3,2},{4,5},{5,4},{6,7},{7,6},{8,9},{9,8},{10,11... | collective-permute-start | bytes 393224 | tf_op jit(solution)/shard_map/ppermute | solution.py:36
  17.4 7.5 %collective-permute-start.4 = (bf16[512,128]{1,0:T(8,128)(2,1)S(1)}, bf16[512,128]{1,0:T(8,128)(2,1)S(1)}, u32[]{:S(2)}, u32[]{:S(2)}) collective-permute-start(bf16[512,128]{1,0:T(8,128)(2,1)S(1)} %collective-permute-done.refs_1_), channel_id=1, source_target_pairs={{0,1},{1,0},{2,3},{3,2},{4,5},{5,4},{6,7},{7,6},{8,9},{9,8},{10,11... | collective-permute-start | bytes 393224 | tf_op jit(solution)/shard_map/ppermute | solution.py:36
  18.4 4.4 %collective-permute-start.10 = (f32[160,128]{1,0:T(8,128)S(1)}, f32[160,128]{1,0:T(8,128)S(1)}, u32[]{:S(2)}, u32[]{:S(2)}) collective-permute-start(f32[160,128]{1,0:T(8,128)S(1)} %collective-permute-done.9.refs_2_), channel_id=1, source_target_pairs={{0,2},{1,3},{2,0},{3,1},{4,6},{5,7},{6,4},{7,5},{8,10},{9,11},{10,... | collective-permute-start | bytes 245768 | tf_op jit(solution)/shard_map/ppermute | solution.py:32
  21.3 5.8 %collective-permute-start.6 = (bf16[512,128]{1,0:T(8,128)(2,1)S(1)}, bf16[512,128]{1,0:T(8,128)(2,1)S(1)}, u32[]{:S(2)}, u32[]{:S(2)}) collective-permute-start(bf16[512,128]{1,0:T(8,128)(2,1)S(1)} %collective-permute-done.3.refs_3_), channel_id=1, source_target_pairs={{0,1},{1,0},{2,3},{3,2},{4,5},{5,4},{6,7},{7,6},{8,9},{9,8},{10,11... | collective-permute-start | bytes 393224 | tf_op jit(solution)/shard_map/ppermute | solution.py:36
  22.9 3.7 %collective-permute-start.13 = (bf16[128,128]{1,0:T(8,128)(2,1)S(1)}, bf16[128,128]{1,0:T(8,128)(2,1)S(1)}, u32[]{:S(2)}, u32[]{:S(2)}) collective-permute-start(bf16[128,128]{1,0:T(8,128)(2,1)S(1)} %get-tuple-element.24.refs_8_), channel_id=1, source_target_pairs={{0,24},{8,16},{16,8},{24,0},{1,25},{9,17},{17,9},{25,1},{2,26},{10... | collective-permute-start | bytes 98312 | tf_op jit(solution)/shard_map/ppermute | solution.py:55
  23.0 4.0 %collective-permute-start.12 = (bf16[128,128]{1,0:T(8,128)(2,1)S(1)}, bf16[128,128]{1,0:T(8,128)(2,1)S(1)}, u32[]{:S(2)}, u32[]{:S(2)}) collective-permute-start(bf16[128,128]{1,0:T(8,128)(2,1)S(1)} %get-tuple-element.24.refs_8_), channel_id=1, source_target_pairs={{0,16},{8,24},{16,0},{24,8},{1,17},{9,25},{17,1},{25,9},{2,18},{10... | collective-permute-start | bytes 98312 | tf_op jit(solution)/shard_map/ppermute | solution.py:55
  24.6 2.4 %collective-permute-start.11 = (bf16[128,128]{1,0:T(8,128)(2,1)S(1)}, bf16[128,128]{1,0:T(8,128)(2,1)S(1)}, u32[]{:S(2)}, u32[]{:S(2)}) collective-permute-start(bf16[128,128]{1,0:T(8,128)(2,1)S(1)} %get-tuple-element.24.refs_8_), channel_id=1, source_target_pairs={{0,8},{8,0},{16,24},{24,16},{1,9},{9,1},{17,25},{25,17},{2,10},{10... | collective-permute-start | bytes 98312 | tf_op jit(solution)/shard_map/ppermute | solution.py:55
  27.9 3.4 %collective-permute-start.16 = (bf16[128,128]{1,0:T(8,128)(2,1)S(1)}, bf16[128,128]{1,0:T(8,128)(2,1)S(1)}, u32[]{:S(2)}, u32[]{:S(2)}) collective-permute-start(bf16[128,128]{1,0:T(8,128)(2,1)S(1)} %get-tuple-element.31.refs_1_), channel_id=1, source_target_pairs={{0,24},{8,16},{16,8},{24,0},{1,25},{9,17},{17,9},{25,1},{2,26},{10... | collective-permute-start | bytes 98312 | tf_op jit(solution)/shard_map/ppermute | solution.py:55
  29.0 3.9 %collective-permute-start.15 = (bf16[128,128]{1,0:T(8,128)(2,1)S(1)}, bf16[128,128]{1,0:T(8,128)(2,1)S(1)}, u32[]{:S(2)}, u32[]{:S(2)}) collective-permute-start(bf16[128,128]{1,0:T(8,128)(2,1)S(1)} %get-tuple-element.31.refs_1_), channel_id=1, source_target_pairs={{0,16},{8,24},{16,0},{24,8},{1,17},{9,25},{17,1},{25,9},{2,18},{10... | collective-permute-start | bytes 98312 | tf_op jit(solution)/shard_map/ppermute | solution.py:55
  30.0 2.9 %collective-permute-start.14 = (bf16[128,128]{1,0:T(8,128)(2,1)S(1)}, bf16[128,128]{1,0:T(8,128)(2,1)S(1)}, u32[]{:S(2)}, u32[]{:S(2)}) collective-permute-start(bf16[128,128]{1,0:T(8,128)(2,1)S(1)} %get-tuple-element.31.refs_1_), channel_id=1, source_target_pairs={{0,8},{8,0},{16,24},{24,16},{1,9},{9,1},{17,25},{25,17},{2,10},{10... | collective-permute-start | bytes 98312 | tf_op jit(solution)/shard_map/ppermute | solution.py:55
  33.6 3.8 %collective-permute-start.19 = (bf16[128,128]{1,0:T(8,128)(2,1)S(1)}, bf16[128,128]{1,0:T(8,128)(2,1)S(1)}, u32[]{:S(2)}, u32[]{:S(2)}) collective-permute-start(bf16[128,128]{1,0:T(8,128)(2,1)S(1)} %get-tuple-element.35.refs_1_), channel_id=1, source_target_pairs={{0,24},{8,16},{16,8},{24,0},{1,25},{9,17},{17,9},{25,1},{2,26},{10... | collective-permute-start | bytes 98312 | tf_op jit(solution)/shard_map/ppermute | solution.py:55
  33.7 4.3 %collective-permute-start.18 = (bf16[128,128]{1,0:T(8,128)(2,1)S(1)}, bf16[128,128]{1,0:T(8,128)(2,1)S(1)}, u32[]{:S(2)}, u32[]{:S(2)}) collective-permute-start(bf16[128,128]{1,0:T(8,128)(2,1)S(1)} %get-tuple-element.35.refs_1_), channel_id=1, source_target_pairs={{0,16},{8,24},{16,0},{24,8},{1,17},{9,25},{17,1},{25,9},{2,18},{10... | collective-permute-start | bytes 98312 | tf_op jit(solution)/shard_map/ppermute | solution.py:55
  35.1 2.9 %collective-permute-start.17 = (bf16[128,128]{1,0:T(8,128)(2,1)S(1)}, bf16[128,128]{1,0:T(8,128)(2,1)S(1)}, u32[]{:S(2)}, u32[]{:S(2)}) collective-permute-start(bf16[128,128]{1,0:T(8,128)(2,1)S(1)} %get-tuple-element.35.refs_1_), channel_id=1, source_target_pairs={{0,8},{8,0},{16,24},{24,16},{1,9},{9,1},{17,25},{25,17},{2,10},{10... | collective-permute-start | bytes 98312 | tf_op jit(solution)/shard_map/ppermute | solution.py:55
  38.4 4.1 %collective-permute-start.20 = (f32[96,128]{1,0:T(8,128)S(1)}, f32[96,128]{1,0:T(8,128)S(1)}, u32[]{:S(2)}, u32[]{:S(2)}) collective-permute-start(f32[96,128]{1,0:T(8,128)S(1)} %shard_map.117.mine_ref), channel_id=1, source_target_pairs={{0,1},{1,0},{2,3},{3,2},{4,5},{5,4},{6,7},{7,6},{8,9},{9,8},{10,11... | collective-permute-start | bytes 147464 | tf_op jit(solution)/shard_map/ppermute | solution.py:36

commit v5 on v4

--- a/solution.py
+++ b/solution.py
@@ -102,14 +102,31 @@
                 dense_ref[start : start + block, col * block : (col + 1) * block] = dense
 
 
-def join_kernel(mine_ref, theirs_ref, *outs):
+def join_kernel(mine_ref, theirs_ref, joined_ref):
     half = mine_ref.shape[1] // 2
-    side = lax.axis_index("src") % 2
+    side = lax.axis_index("src") % PAIR
     theirs = pltpu.roll(theirs_ref[...], half, 1)
-    joined = jnp.where(lane_side(theirs.shape, half) == side, mine_ref[...], theirs)
-    each = joined.shape[0] // len(outs)
+    joined_ref[...] = jnp.where(lane_side(theirs.shape, half) == side, mine_ref[...], theirs)
+
+
+def fold(value, side):
+    rows, half = value.shape[0] // 2, value.shape[1] // 2
+    moved = pltpu.roll(value, half, 1)
+    left = jnp.where(side == 0, value[:rows], moved[:rows])
+    right = jnp.where(side == 0, moved[rows:], value[rows:])
+    return jnp.where(lane_side(left.shape, half) == 0, left, right)
+
+
+def finish_kernel(mine_ref, theirs_ref, *outs):
+    half = mine_ref.shape[1] // 2
+    side = lax.axis_index("src") % PAIR
+    theirs = theirs_ref[...]
+    moved = pltpu.roll(theirs, half, 1)
+    theirs = jnp.concatenate([jnp.where(side == 1, theirs, moved), jnp.where(side == 1, moved, theirs)])
+    done = jnp.where(lane_side(theirs.shape, half) == side, mine_ref[...], theirs)
+    own = done.shape[0] // len(outs)
     for i, out in enumerate(outs):
-        out[...] = joined[i * each : (i + 1) * each]
+        out[...] = done[i * own : (i + 1) * own]
 
 
 def unpack_kernel(count, *refs):
@@ -183,8 +200,9 @@
         moved = tuple(0.75 * first + 0.25 * value for first, value in zip(begin, moved))
     elif stage == 2:
         moved = tuple(first / 3.0 + (2.0 / 3.0) * value for first, value in zip(begin, moved))
-        for i, value in enumerate(moved):
-            outs[0][i * own : (i + 1) * own] = value
+        done = jnp.concatenate(moved)
+        outs[0][...] = done
+        outs[1][...] = fold(done, 1 - lax.axis_index("src") % PAIR)
         return
     for out, value in zip(outs, moved):
         out[...] = value
@@ -242,7 +260,7 @@
     matrix_type = jax.ShapeDtypeStruct((2 * rows, sources * leaf_cols * block), jnp.bfloat16)
     for stage in range(3):
         given = (*dense_blocks, *gather_target(dev), *begin, all_a, all_h, *now)
-        outs = ((wide,) * 3 + (dev_type,)) if stage < 2 else (floats(3 * own),)
+        outs = ((wide,) * 3 + (dev_type,)) if stage < 2 else (floats(3 * own), floats(3 * own // 2))
         outs = outs + ((matrix_type,) if stage == 0 else ())
         results = call(
             functools.partial(stage_kernel, stage, own, len(dense_blocks), targets),
@@ -255,7 +273,7 @@
             dev = results[3]
         if stage == 0:
             dense_blocks = [results[4]]
-    return call(join_kernel, (floats(own),) * 3, (results[0], across_pair(results[0])))
+    return call(finish_kernel, (floats(own),) * 3, (results[0], across_pair(results[1])))
 
 
 def solution(mesh):

time: 43.4 us -> 43.2 us (level)
  no operation moved by 1% of the time
where the time goes in v5:
time: 43.2 us; the launch traced here: 43 us
  starting transfers between devices  23.6 us (55%)
  waiting for transfers between devices  14.6 us (34%)
  Pallas kernels  4.08 us (9%)
  between operations  0.72 us (2%)
    ppermute x6, starting transfers between devices, along_line(): return lax.ppermute(block, 'src', moves)  9.48 us
    ppermute x6, starting transfers between devices, across_pair(): lax.ppermute(block, 'src', [(i, i ^ 1) for i in range(lax.axis_size('src'...  8.19 us
    ppermute x9, waiting for transfers between devices, gather_target(): lax.ppermute(block, 'tgt', [(i, partner(i, step, targets)) for i in range...  7.6 us
    ppermute x9, starting transfers between devices, gather_target(): lax.ppermute(block, 'tgt', [(i, partner(i, step, targets)) for i in range...  5.9 us
    ppermute x6, waiting for transfers between devices, along_line(): return lax.ppermute(block, 'src', moves)  4.11 us
    pallas_call x7, Pallas kernels, call(): pl.pallas_call(kernel, out_shape=tuple(outs), in_specs=[space] * len(give...  4.08 us
    ppermute x6, waiting for transfers between devices, across_pair(): lax.ppermute(block, 'src', [(i, i ^ 1) for i in range(lax.axis_size('src'...  2.85 us
  transfers between devices with their start and end apart: 21, of which 9 were waited for; matrix products, arithmetic and copies ran while one was open for 0% of the time, Pallas kernels for 0%

profile of v5, /device:TPU:0, one launch (start us, length us, event | category | flops | bytes accessed | tf_op | source)
XLA Modules:
  0.0 43.0 jit_solution(8189076786109735391)
XLA Ops:
  0.6 1.3 %shard_map.112 = (f32[160,128]{1,0:T(8,128)S(1)}, bf16[512,128]{1,0:T(8,128)(2,1)S(1)}) custom-call(s32[1,2]{1,0:T(1,128)} %bitcast.2, s32[1,2]{1,0:T(1,128)} %bitcast.3, bf16[2,1,128,128]{3,2,1,0:T(8,128)(2,1)} %refs_2_.1, bf16[2,1,128,128]{3,2,1,0:T(8,128)(2,1)} %refs_3_.1, f32[32,128]{1,0:T(8,128)} %refs_4_.1, f32[32,128]{1,0:T(8,128)} %refs_5_.1, ...), custom_call_target="tpu_custom_call" | custom-call | tf_op jit(solution)/shard_map/pallas_call | solution.py:213
  1.9 3.0 %collective-permute-start.7 = (f32[160,128]{1,0:T(8,128)S(1)}, f32[160,128]{1,0:T(8,128)S(1)}, u32[]{:S(2)}, u32[]{:S(2)}) collective-permute-start(f32[160,128]{1,0:T(8,128)S(1)} %get-tuple-element.25.mine_ref), channel_id=1, source_target_pairs={{0,1},{1,0},{2,3},{3,2},{4,5},{5,4},{6,7},{7,6},{8,9},{9,8},{10,11... | collective-permute-start | bytes 245768 | tf_op jit(solution)/shard_map/ppermute | solution.py:36
  5.0 3.0 %collective-permute-start.1 = (bf16[512,128]{1,0:T(8,128)(2,1)S(1)}, bf16[512,128]{1,0:T(8,128)(2,1)S(1)}, u32[]{:S(2)}, u32[]{:S(2)}) collective-permute-start(bf16[512,128]{1,0:T(8,128)(2,1)S(1)} %get-tuple-element.23.refs_0_), channel_id=1, source_target_pairs={{0,4},{1,5},{2,6},{3,7},{4,0},{5,1},{6,2},{7,3},{8,12},{9,13},{10,... | collective-permute-start | bytes 393224 | tf_op jit(solution)/shard_map/ppermute | solution.py:32
  8.0 1.6 %collective-permute-start = (bf16[512,128]{1,0:T(8,128)(2,1)S(1)}, bf16[512,128]{1,0:T(8,128)(2,1)S(1)}, u32[]{:S(2)}, u32[]{:S(2)}) collective-permute-start(bf16[512,128]{1,0:T(8,128)(2,1)S(1)} %get-tuple-element.23.refs_0_), channel_id=1, source_target_pairs={{0,2},{1,3},{2,0},{3,1},{4,6},{5,7},{6,4},{7,5},{8,10},{9,11},{10,... | collective-permute-start | bytes 393224 | tf_op jit(solution)/shard_map/ppermute | solution.py:32
  9.7 1.7 %collective-permute-start.9 = (f32[160,128]{1,0:T(8,128)S(1)}, f32[160,128]{1,0:T(8,128)S(1)}, u32[]{:S(2)}, u32[]{:S(2)}) collective-permute-start(f32[160,128]{1,0:T(8,128)S(1)} %shard_map.113.refs_0_), channel_id=1, source_target_pairs={{0,4},{1,5},{2,6},{3,7},{4,0},{5,1},{6,2},{7,3},{8,12},{9,13},{10,... | collective-permute-start | bytes 245768 | tf_op jit(solution)/shard_map/ppermute | solution.py:32
  11.4 1.6 %collective-permute-start.8 = (f32[160,128]{1,0:T(8,128)S(1)}, f32[160,128]{1,0:T(8,128)S(1)}, u32[]{:S(2)}, u32[]{:S(2)}) collective-permute-start(f32[160,128]{1,0:T(8,128)S(1)} %shard_map.113.refs_0_), channel_id=1, source_target_pairs={{0,2},{1,3},{2,0},{3,1},{4,6},{5,7},{6,4},{7,5},{8,10},{9,11},{10,... | collective-permute-start | bytes 245768 | tf_op jit(solution)/shard_map/ppermute | solution.py:32
  13.1 2.5 %collective-permute-done.1.refs_2_ = bf16[512,128]{1,0:T(8,128)(2,1)S(1)} collective-permute-done((bf16[512,128]{1,0:T(8,128)(2,1)S(1)}, bf16[512,128]{1,0:T(8,128)(2,1)S(1)}, u32[]{:S(2)}, u32[]{:S(2)}) %collective-permute-start.1) | collective-permute-done | bytes 131104 | tf_op jit(solution)/shard_map/ppermute | solution.py:32
  15.6 0.3 collective-permute-start.3
  15.9 1.5 %collective-permute-start.5 = (bf16[512,128]{1,0:T(8,128)(2,1)S(1)}, bf16[512,128]{1,0:T(8,128)(2,1)S(1)}, u32[]{:S(2)}, u32[]{:S(2)}) collective-permute-start(bf16[512,128]{1,0:T(8,128)(2,1)S(1)} %collective-permute-done.1.refs_2_), channel_id=1, source_target_pairs={{0,1},{1,0},{2,3},{3,2},{4,5},{5,4},{6,7},{7,6},{8,9},{9,8},{10,11... | collective-permute-start | bytes 393224 | tf_op jit(solution)/shard_map/ppermute | solution.py:36
  17.4 1.0 %collective-permute-start.4 = (bf16[512,128]{1,0:T(8,128)(2,1)S(1)}, bf16[512,128]{1,0:T(8,128)(2,1)S(1)}, u32[]{:S(2)}, u32[]{:S(2)}) collective-permute-start(bf16[512,128]{1,0:T(8,128)(2,1)S(1)} %collective-permute-done.refs_1_), channel_id=1, source_target_pairs={{0,1},{1,0},{2,3},{3,2},{4,5},{5,4},{6,7},{7,6},{8,9},{9,8},{10,11... | collective-permute-start | bytes 393224 | tf_op jit(solution)/shard_map/ppermute | solution.py:36
  18.4 1.2 %collective-permute-start.10 = (f32[160,128]{1,0:T(8,128)S(1)}, f32[160,128]{1,0:T(8,128)S(1)}, u32[]{:S(2)}, u32[]{:S(2)}) collective-permute-start(f32[160,128]{1,0:T(8,128)S(1)} %collective-permute-done.9.refs_2_), channel_id=1, source_target_pairs={{0,2},{1,3},{2,0},{3,1},{4,6},{5,7},{6,4},{7,5},{8,10},{9,11},{10,... | collective-permute-start | bytes 245768 | tf_op jit(solution)/shard_map/ppermute | solution.py:32
  19.7 1.6 %collective-permute-done.3.refs_3_ = bf16[512,128]{1,0:T(8,128)(2,1)S(1)} collective-permute-done((bf16[512,128]{1,0:T(8,128)(2,1)S(1)}, bf16[512,128]{1,0:T(8,128)(2,1)S(1)}, u32[]{:S(2)}, u32[]{:S(2)}) %collective-permute-start.3) | collective-permute-done | bytes 131104 | tf_op jit(solution)/shard_map/ppermute | solution.py:32
  21.3 1.5 %collective-permute-start.6 = (bf16[512,128]{1,0:T(8,128)(2,1)S(1)}, bf16[512,128]{1,0:T(8,128)(2,1)S(1)}, u32[]{:S(2)}, u32[]{:S(2)}) collective-permute-start(bf16[512,128]{1,0:T(8,128)(2,1)S(1)} %collective-permute-done.3.refs_3_), channel_id=1, source_target_pairs={{0,1},{1,0},{2,3},{3,2},{4,5},{5,4},{6,7},{7,6},{8,9},{9,8},{10,11... | collective-permute-start | bytes 393224 | tf_op jit(solution)/shard_map/ppermute | solution.py:36
  23.0 1.6 %collective-permute-start.12 = (bf16[128,128]{1,0:T(8,128)(2,1)S(1)}, bf16[128,128]{1,0:T(8,128)(2,1)S(1)}, u32[]{:S(2)}, u32[]{:S(2)}) collective-permute-start(bf16[128,128]{1,0:T(8,128)(2,1)S(1)} %get-tuple-element.26.refs_8_), channel_id=1, source_target_pairs={{0,16},{8,24},{16,0},{24,8},{1,17},{9,25},{17,1},{25,9},{2,18},{10... | collective-permute-start | bytes 98312 | tf_op jit(solution)/shard_map/ppermute | solution.py:55
  24.6 0.3 collective-permute-start.11
  24.9 1.7 %collective-permute-done.13.refs_11_ = bf16[128,128]{1,0:T(8,128)(2,1)S(1)} collective-permute-done((bf16[128,128]{1,0:T(8,128)(2,1)S(1)}, bf16[128,128]{1,0:T(8,128)(2,1)S(1)}, u32[]{:S(2)}, u32[]{:S(2)}) %collective-permute-start.13) | collective-permute-done | bytes 32800 | tf_op jit(solution)/shard_map/ppermute | solution.py:55
  26.6 0.4 collective-permute-done.12.refs_10_
  27.1 0.9 %shard_map.115 = (f32[128,128]{1,0:T(8,128)S(1)}, f32[128,128]{1,0:T(8,128)S(1)}, f32[128,128]{1,0:T(8,128)S(1)}, bf16[128,128]{1,0:T(8,128)(2,1)S(1)}, bf16[512,1024]{1,0:T(8,128)(2,1)S(1)}) custom-call(bf16[512,128]{1,0:T(8,128)(2,1)S(1)} %get-tuple-element.23.refs_0_, bf16[512,128]{1,0:T(8,128)(2,1)S(1)} %collective-permute-done.refs_1_, ...), custom_call_target="tpu_custom_call" | custom-call | tf_op jit(solution)/shard_map/pallas_call | solution.py:213
  27.9 1.0 %collective-permute-start.16 = (bf16[128,128]{1,0:T(8,128)(2,1)S(1)}, bf16[128,128]{1,0:T(8,128)(2,1)S(1)}, u32[]{:S(2)}, u32[]{:S(2)}) collective-permute-start(bf16[128,128]{1,0:T(8,128)(2,1)S(1)} %get-tuple-element.33.refs_1_), channel_id=1, source_target_pairs={{0,24},{8,16},{16,8},{24,0},{1,25},{9,17},{17,9},{25,1},{2,26},{10... | collective-permute-start | bytes 98312 | tf_op jit(solution)/shard_map/ppermute | solution.py:55
  29.0 1.0 %collective-permute-start.15 = (bf16[128,128]{1,0:T(8,128)(2,1)S(1)}, bf16[128,128]{1,0:T(8,128)(2,1)S(1)}, u32[]{:S(2)}, u32[]{:S(2)}) collective-permute-start(bf16[128,128]{1,0:T(8,128)(2,1)S(1)} %get-tuple-element.33.refs_1_), channel_id=1, source_target_pairs={{0,16},{8,24},{16,0},{24,8},{1,17},{9,25},{17,1},{25,9},{2,18},{10... | collective-permute-start | bytes 98312 | tf_op jit(solution)/shard_map/ppermute | solution.py:55
  30.0 1.4 %collective-permute-done.16.refs_4_ = bf16[128,128]{1,0:T(8,128)(2,1)S(1)} collective-permute-done((bf16[128,128]{1,0:T(8,128)(2,1)S(1)}, bf16[128,128]{1,0:T(8,128)(2,1)S(1)}, u32[]{:S(2)}, u32[]{:S(2)}) %collective-permute-start.16) | collective-permute-done | bytes 32800 | tf_op jit(solution)/shard_map/ppermute | solution.py:55
  31.4 1.6 %collective-permute-done.15.refs_3_ = bf16[128,128]{1,0:T(8,128)(2,1)S(1)} collective-permute-done((bf16[128,128]{1,0:T(8,128)(2,1)S(1)}, bf16[128,128]{1,0:T(8,128)(2,1)S(1)}, u32[]{:S(2)}, u32[]{:S(2)}) %collective-permute-start.15) | collective-permute-done | bytes 32800 | tf_op jit(solution)/shard_map/ppermute | solution.py:55
  32.9 0.6 %shard_map.116 = (f32[128,128]{1,0:T(8,128)S(1)}, f32[128,128]{1,0:T(8,128)S(1)}, f32[128,128]{1,0:T(8,128)S(1)}, bf16[128,128]{1,0:T(8,128)(2,1)S(1)}) custom-call(bf16[512,1024]{1,0:T(8,128)(2,1)S(1)} %get-tuple-element.32.refs_0_, bf16[128,128]{1,0:T(8,128)(2,1)S(1)} %get-tuple-element.33.refs_1_, bf16[128,128]{1,0:T(8,128)(2,1)S(1)} %collective-permute-done.14.refs_2_, ...), custom_call_target="tpu_custom_call" | custom-call | tf_op jit(solution)/shard_map/pallas_call | solution.py:213
  33.6 0.1 collective-permute-start.19
  33.7 1.4 %collective-permute-start.18 = (bf16[128,128]{1,0:T(8,128)(2,1)S(1)}, bf16[128,128]{1,0:T(8,128)(2,1)S(1)}, u32[]{:S(2)}, u32[]{:S(2)}) collective-permute-start(bf16[128,128]{1,0:T(8,128)(2,1)S(1)} %get-tuple-element.37.refs_1_), channel_id=1, source_target_pairs={{0,16},{8,24},{16,0},{24,8},{1,17},{9,25},{17,1},{25,9},{2,18},{10... | collective-permute-start | bytes 98312 | tf_op jit(solution)/shard_map/ppermute | solution.py:55
  35.1 0.4 %collective-permute-start.17 = (bf16[128,128]{1,0:T(8,128)(2,1)S(1)}, bf16[128,128]{1,0:T(8,128)(2,1)S(1)}, u32[]{:S(2)}, u32[]{:S(2)}) collective-permute-start(bf16[128,128]{1,0:T(8,128)(2,1)S(1)} %get-tuple-element.37.refs_1_), channel_id=1, source_target_pairs={{0,8},{8,0},{16,24},{24,16},{1,9},{9,1},{17,25},{25,17},{2,10},{10... | collective-permute-start | bytes 98312 | tf_op jit(solution)/shard_map/ppermute | solution.py:55
  35.5 1.8 %collective-permute-done.19.refs_4_ = bf16[128,128]{1,0:T(8,128)(2,1)S(1)} collective-permute-done((bf16[128,128]{1,0:T(8,128)(2,1)S(1)}, bf16[128,128]{1,0:T(8,128)(2,1)S(1)}, u32[]{:S(2)}, u32[]{:S(2)}) %collective-permute-start.19) | collective-permute-done | bytes 32800 | tf_op jit(solution)/shard_map/ppermute | solution.py:55
  37.3 0.7 %collective-permute-done.18.refs_3_ = bf16[128,128]{1,0:T(8,128)(2,1)S(1)} collective-permute-done((bf16[128,128]{1,0:T(8,128)(2,1)S(1)}, bf16[128,128]{1,0:T(8,128)(2,1)S(1)}, u32[]{:S(2)}, u32[]{:S(2)}) %collective-permute-start.18) | collective-permute-done | bytes 32800 | tf_op jit(solution)/shard_map/ppermute | solution.py:55
  38.0 0.5 %shard_map.117 = (f32[96,128]{1,0:T(8,128)S(1)}, f32[48,128]{1,0:T(8,128)S(1)}) custom-call(bf16[512,1024]{1,0:T(8,128)(2,1)S(1)} %get-tuple-element.32.refs_0_, bf16[128,128]{1,0:T(8,128)(2,1)S(1)} %get-tuple-element.37.refs_1_, bf16[128,128]{1,0:T(8,128)(2,1)S(1)} %collective-permute-done.17.refs_2_, bf16[128,128]{1,0:T(8,128)(2,1)S(1)} %collective-permute-done.18.refs_3_, ...), custom_call_target="tpu_custom_call" | custom-call | tf_op jit(solution)/shard_map/pallas_call | solution.py:213
  38.5 1.0 %collective-permute-start.20 = (f32[48,128]{1,0:T(8,128)S(1)}, f32[48,128]{1,0:T(8,128)S(1)}, u32[]{:S(2)}, u32[]{:S(2)}) collective-permute-start(f32[48,128]{1,0:T(8,128)S(1)} %get-tuple-element.42), channel_id=1, source_target_pairs={{0,1},{1,0},{2,3},{3,2},{4,5},{5,4},{6,7},{7,6},{8,9},{9,8},{10,11... | collective-permute-start | bytes 73736 | tf_op jit(solution)/shard_map/ppermute | solution.py:36
  39.5 2.8 %collective-permute-done.20.theirs_ref = f32[48,128]{1,0:T(8,128)S(1)} collective-permute-done((f32[48,128]{1,0:T(8,128)S(1)}, f32[48,128]{1,0:T(8,128)S(1)}, u32[]{:S(2)}, u32[]{:S(2)}) %collective-permute-start.20) | collective-permute-done | bytes 24608 | tf_op jit(solution)/shard_map/ppermute | solution.py:36
  42.3 0.7 %shard_map.118 = (f32[32,128]{1,0:T(8,128)}, f32[32,128]{1,0:T(8,128)}, f32[32,128]{1,0:T(8,128)}) custom-call(f32[96,128]{1,0:T(8,128)S(1)} %get-tuple-element.41.mine_ref, f32[48,128]{1,0:T(8,128)S(1)} %collective-permute-done.20.theirs_ref), custom_call_target="tpu_custom_call" | custom-call | tf_op jit(solution)/shard_map/pallas_call | solution.py:213
  (21 shorter events, 0.4 us)
Async XLA Ops:
  1.9 7.7 %collective-permute-start.7 = (f32[160,128]{1,0:T(8,128)S(1)}, f32[160,128]{1,0:T(8,128)S(1)}, u32[]{:S(2)}, u32[]{:S(2)}) collective-permute-start(f32[160,128]{1,0:T(8,128)S(1)} %get-tuple-element.25.mine_ref), channel_id=1, source_target_pairs={{0,1},{1,0},{2,3},{3,2},{4,5},{5,4},{6,7},{7,6},{8,9},{9,8},{10,11... | collective-permute-start | bytes 245768 | tf_op jit(solution)/shard_map/ppermute | solution.py:36
  4.9 8.2 %collective-permute-start.2 = (bf16[512,128]{1,0:T(8,128)(2,1)S(1)}, bf16[512,128]{1,0:T(8,128)(2,1)S(1)}, u32[]{:S(2)}, u32[]{:S(2)}) collective-permute-start(bf16[512,128]{1,0:T(8,128)(2,1)S(1)} %get-tuple-element.23.refs_0_), channel_id=1, source_target_pairs={{0,1},{1,0},{2,3},{3,2},{4,5},{5,4},{6,7},{7,6},{8,9},{9,8},{10,11... | collective-permute-start | bytes 393224 | tf_op jit(solution)/shard_map/ppermute | solution.py:36
  5.0 10.6 %collective-permute-start.1 = (bf16[512,128]{1,0:T(8,128)(2,1)S(1)}, bf16[512,128]{1,0:T(8,128)(2,1)S(1)}, u32[]{:S(2)}, u32[]{:S(2)}) collective-permute-start(bf16[512,128]{1,0:T(8,128)(2,1)S(1)} %get-tuple-element.23.refs_0_), channel_id=1, source_target_pairs={{0,4},{1,5},{2,6},{3,7},{4,0},{5,1},{6,2},{7,3},{8,12},{9,13},{10,... | collective-permute-start | bytes 393224 | tf_op jit(solution)/shard_map/ppermute | solution.py:32
  8.0 9.3 %collective-permute-start = (bf16[512,128]{1,0:T(8,128)(2,1)S(1)}, bf16[512,128]{1,0:T(8,128)(2,1)S(1)}, u32[]{:S(2)}, u32[]{:S(2)}) collective-permute-start(bf16[512,128]{1,0:T(8,128)(2,1)S(1)} %get-tuple-element.23.refs_0_), channel_id=1, source_target_pairs={{0,2},{1,3},{2,0},{3,1},{4,6},{5,7},{6,4},{7,5},{8,10},{9,11},{10,... | collective-permute-start | bytes 393224 | tf_op jit(solution)/shard_map/ppermute | solution.py:32
  9.7 8.7 %collective-permute-start.9 = (f32[160,128]{1,0:T(8,128)S(1)}, f32[160,128]{1,0:T(8,128)S(1)}, u32[]{:S(2)}, u32[]{:S(2)}) collective-permute-start(f32[160,128]{1,0:T(8,128)S(1)} %shard_map.113.refs_0_), channel_id=1, source_target_pairs={{0,4},{1,5},{2,6},{3,7},{4,0},{5,1},{6,2},{7,3},{8,12},{9,13},{10,... | collective-permute-start | bytes 245768 | tf_op jit(solution)/shard_map/ppermute | solution.py:32
  11.4 8.2 %collective-permute-start.8 = (f32[160,128]{1,0:T(8,128)S(1)}, f32[160,128]{1,0:T(8,128)S(1)}, u32[]{:S(2)}, u32[]{:S(2)}) collective-permute-start(f32[160,128]{1,0:T(8,128)S(1)} %shard_map.113.refs_0_), channel_id=1, source_target_pairs={{0,2},{1,3},{2,0},{3,1},{4,6},{5,7},{6,4},{7,5},{8,10},{9,11},{10,... | collective-permute-start | bytes 245768 | tf_op jit(solution)/shard_map/ppermute | solution.py:32
  15.6 5.7 %collective-permute-start.3 = (bf16[512,128]{1,0:T(8,128)(2,1)S(1)}, bf16[512,128]{1,0:T(8,128)(2,1)S(1)}, u32[]{:S(2)}, u32[]{:S(2)}) collective-permute-start(bf16[512,128]{1,0:T(8,128)(2,1)S(1)} %collective-permute-done.1.refs_2_), channel_id=1, source_target_pairs={{0,2},{1,3},{2,0},{3,1},{4,6},{5,7},{6,4},{7,5},{8,10},{9,11},{10,... | collective-permute-start | bytes 393224 | tf_op jit(solution)/shard_map/ppermute | solution.py:32
  15.9 8.7 %collective-permute-start.5 = (bf16[512,128]{1,0:T(8,128)(2,1)S(1)}, bf16[512,128]{1,0:T(8,128)(2,1)S(1)}, u32[]{:S(2)}, u32[]{:S(2)}) collective-permute-start(bf16[512,128]{1,0:T(8,128)(2,1)S(1)} %collective-permute-done.1.refs_2_), channel_id=1, source_target_pairs={{0,1},{1,0},{2,3},{3,2},{4,5},{5,4},{6,7},{7,6},{8,9},{9,8},{10,11... | collective-permute-start | bytes 393224 | tf_op jit(solution)/shard_map/ppermute | solution.py:36
  17.4 7.5 %collective-permute-start.4 = (bf16[512,128]{1,0:T(8,128)(2,1)S(1)}, bf16[512,128]{1,0:T(8,128)(2,1)S(1)}, u32[]{:S(2)}, u32[]{:S(2)}) collective-permute-start(bf16[512,128]{1,0:T(8,128)(2,1)S(1)} %collective-permute-done.refs_1_), channel_id=1, source_target_pairs={{0,1},{1,0},{2,3},{3,2},{4,5},{5,4},{6,7},{7,6},{8,9},{9,8},{10,11... | collective-permute-start | bytes 393224 | tf_op jit(solution)/shard_map/ppermute | solution.py:36
  18.4 4.4 %collective-permute-start.10 = (f32[160,128]{1,0:T(8,128)S(1)}, f32[160,128]{1,0:T(8,128)S(1)}, u32[]{:S(2)}, u32[]{:S(2)}) collective-permute-start(f32[160,128]{1,0:T(8,128)S(1)} %collective-permute-done.9.refs_2_), channel_id=1, source_target_pairs={{0,2},{1,3},{2,0},{3,1},{4,6},{5,7},{6,4},{7,5},{8,10},{9,11},{10,... | collective-permute-start | bytes 245768 | tf_op jit(solution)/shard_map/ppermute | solution.py:32
  21.3 5.8 %collective-permute-start.6 = (bf16[512,128]{1,0:T(8,128)(2,1)S(1)}, bf16[512,128]{1,0:T(8,128)(2,1)S(1)}, u32[]{:S(2)}, u32[]{:S(2)}) collective-permute-start(bf16[512,128]{1,0:T(8,128)(2,1)S(1)} %collective-permute-done.3.refs_3_), channel_id=1, source_target_pairs={{0,1},{1,0},{2,3},{3,2},{4,5},{5,4},{6,7},{7,6},{8,9},{9,8},{10,11... | collective-permute-start | bytes 393224 | tf_op jit(solution)/shard_map/ppermute | solution.py:36
  22.9 3.7 %collective-permute-start.13 = (bf16[128,128]{1,0:T(8,128)(2,1)S(1)}, bf16[128,128]{1,0:T(8,128)(2,1)S(1)}, u32[]{:S(2)}, u32[]{:S(2)}) collective-permute-start(bf16[128,128]{1,0:T(8,128)(2,1)S(1)} %get-tuple-element.26.refs_8_), channel_id=1, source_target_pairs={{0,24},{8,16},{16,8},{24,0},{1,25},{9,17},{17,9},{25,1},{2,26},{10... | collective-permute-start | bytes 98312 | tf_op jit(solution)/shard_map/ppermute | solution.py:55
  23.0 4.0 %collective-permute-start.12 = (bf16[128,128]{1,0:T(8,128)(2,1)S(1)}, bf16[128,128]{1,0:T(8,128)(2,1)S(1)}, u32[]{:S(2)}, u32[]{:S(2)}) collective-permute-start(bf16[128,128]{1,0:T(8,128)(2,1)S(1)} %get-tuple-element.26.refs_8_), channel_id=1, source_target_pairs={{0,16},{8,24},{16,0},{24,8},{1,17},{9,25},{17,1},{25,9},{2,18},{10... | collective-permute-start | bytes 98312 | tf_op jit(solution)/shard_map/ppermute | solution.py:55
  24.6 2.4 %collective-permute-start.11 = (bf16[128,128]{1,0:T(8,128)(2,1)S(1)}, bf16[128,128]{1,0:T(8,128)(2,1)S(1)}, u32[]{:S(2)}, u32[]{:S(2)}) collective-permute-start(bf16[128,128]{1,0:T(8,128)(2,1)S(1)} %get-tuple-element.26.refs_8_), channel_id=1, source_target_pairs={{0,8},{8,0},{16,24},{24,16},{1,9},{9,1},{17,25},{25,17},{2,10},{10... | collective-permute-start | bytes 98312 | tf_op jit(solution)/shard_map/ppermute | solution.py:55
  27.9 3.4 %collective-permute-start.16 = (bf16[128,128]{1,0:T(8,128)(2,1)S(1)}, bf16[128,128]{1,0:T(8,128)(2,1)S(1)}, u32[]{:S(2)}, u32[]{:S(2)}) collective-permute-start(bf16[128,128]{1,0:T(8,128)(2,1)S(1)} %get-tuple-element.33.refs_1_), channel_id=1, source_target_pairs={{0,24},{8,16},{16,8},{24,0},{1,25},{9,17},{17,9},{25,1},{2,26},{10... | collective-permute-start | bytes 98312 | tf_op jit(solution)/shard_map/ppermute | solution.py:55
  29.0 3.9 %collective-permute-start.15 = (bf16[128,128]{1,0:T(8,128)(2,1)S(1)}, bf16[128,128]{1,0:T(8,128)(2,1)S(1)}, u32[]{:S(2)}, u32[]{:S(2)}) collective-permute-start(bf16[128,128]{1,0:T(8,128)(2,1)S(1)} %get-tuple-element.33.refs_1_), channel_id=1, source_target_pairs={{0,16},{8,24},{16,0},{24,8},{1,17},{9,25},{17,1},{25,9},{2,18},{10... | collective-permute-start | bytes 98312 | tf_op jit(solution)/shard_map/ppermute | solution.py:55
  30.0 2.9 %collective-permute-start.14 = (bf16[128,128]{1,0:T(8,128)(2,1)S(1)}, bf16[128,128]{1,0:T(8,128)(2,1)S(1)}, u32[]{:S(2)}, u32[]{:S(2)}) collective-permute-start(bf16[128,128]{1,0:T(8,128)(2,1)S(1)} %get-tuple-element.33.refs_1_), channel_id=1, source_target_pairs={{0,8},{8,0},{16,24},{24,16},{1,9},{9,1},{17,25},{25,17},{2,10},{10... | collective-permute-start | bytes 98312 | tf_op jit(solution)/shard_map/ppermute | solution.py:55
  33.6 3.8 %collective-permute-start.19 = (bf16[128,128]{1,0:T(8,128)(2,1)S(1)}, bf16[128,128]{1,0:T(8,128)(2,1)S(1)}, u32[]{:S(2)}, u32[]{:S(2)}) collective-permute-start(bf16[128,128]{1,0:T(8,128)(2,1)S(1)} %get-tuple-element.37.refs_1_), channel_id=1, source_target_pairs={{0,24},{8,16},{16,8},{24,0},{1,25},{9,17},{17,9},{25,1},{2,26},{10... | collective-permute-start | bytes 98312 | tf_op jit(solution)/shard_map/ppermute | solution.py:55
  33.7 4.3 %collective-permute-start.18 = (bf16[128,128]{1,0:T(8,128)(2,1)S(1)}, bf16[128,128]{1,0:T(8,128)(2,1)S(1)}, u32[]{:S(2)}, u32[]{:S(2)}) collective-permute-start(bf16[128,128]{1,0:T(8,128)(2,1)S(1)} %get-tuple-element.37.refs_1_), channel_id=1, source_target_pairs={{0,16},{8,24},{16,0},{24,8},{1,17},{9,25},{17,1},{25,9},{2,18},{10... | collective-permute-start | bytes 98312 | tf_op jit(solution)/shard_map/ppermute | solution.py:55
  35.1 2.9 %collective-permute-start.17 = (bf16[128,128]{1,0:T(8,128)(2,1)S(1)}, bf16[128,128]{1,0:T(8,128)(2,1)S(1)}, u32[]{:S(2)}, u32[]{:S(2)}) collective-permute-start(bf16[128,128]{1,0:T(8,128)(2,1)S(1)} %get-tuple-element.37.refs_1_), channel_id=1, source_target_pairs={{0,8},{8,0},{16,24},{24,16},{1,9},{9,1},{17,25},{25,17},{2,10},{10... | collective-permute-start | bytes 98312 | tf_op jit(solution)/shard_map/ppermute | solution.py:55
  38.5 3.9 %collective-permute-start.20 = (f32[48,128]{1,0:T(8,128)S(1)}, f32[48,128]{1,0:T(8,128)S(1)}, u32[]{:S(2)}, u32[]{:S(2)}) collective-permute-start(f32[48,128]{1,0:T(8,128)S(1)} %get-tuple-element.42), channel_id=1, source_target_pairs={{0,1},{1,0},{2,3},{3,2},{4,5},{5,4},{6,7},{7,6},{8,9},{9,8},{10,11... | collective-permute-start | bytes 73736 | tf_op jit(solution)/shard_map/ppermute | solution.py:36

commit v6 on v5

--- a/solution.py
+++ b/solution.py
@@ -9,6 +9,7 @@
 
 time_step = 0.25
 PAIR = 2
+EARLY = 1
 VMEM = pl.BlockSpec(memory_space=pltpu.VMEM)
 HBM = pl.BlockSpec(memory_space=pltpu.HBM)
 
@@ -142,25 +143,53 @@
     dev_ref[...] = deviation_of(slips[...])
 
 
+def place_deviations(dev_ref, place, own, scratch):
+    dev = dev_ref[...].astype(jnp.float32)
+    half = dev.shape[1] // 2
+    for side, part in enumerate((dev, pltpu.roll(dev, half, 1))):
+        for far in range(dev.shape[0] // own):
+            start = pl.multiple_of(place + (2 * far + side) * own, own)
+            scratch[pl.ds(start, own)] = part[far * own : (far + 1) * own]
+
+
+def product(stage, own, steps, targets, dense_ref, dev_refs, scratch):
+    rows = 2 * dev_refs[0].shape[0]
+    start = pl.multiple_of(lax.axis_index("src") // PAIR * 2 * own, 2 * own)
+    total = 0.0
+    for i, (step, dev_ref) in enumerate(zip(steps, dev_refs)):
+        place_deviations(dev_ref, i * rows, own, scratch)
+        columns = pl.ds(pl.multiple_of(origin(lax.axis_index("tgt"), step, targets) * rows, rows), rows)
+        block = scratch[i * rows : (i + 1) * rows].astype(jnp.bfloat16)
+        if stage < 2:
+            dense = dense_ref[:, columns]
+        else:
+            dense = jnp.concatenate([dense_ref[pl.ds(first + start, 2 * own), columns] for first in (0, rows)])
+        total += jnp.dot(dense, block, preferred_element_type=jnp.float32)
+    return total
+
+
+def early_kernel(stage, own, targets, dense_ref, *refs):
+    refs, total_ref, scratch = refs[:-2], refs[-2], refs[-1]
+    total_ref[...] = product(stage, own, range(len(refs)), targets, dense_ref, refs, scratch)
+
+
 def stage_kernel(stage, own, dense_count, targets, *refs):
     refs, all_dev = refs[:-1], refs[-1]
     dense_in, refs = refs[:dense_count], refs[dense_count:]
-    dev_in, refs = refs[:targets], refs[targets:]
+    late = targets - EARLY if stage else targets
+    dev_in, refs = refs[:late], refs[late:]
+    if stage:
+        early_ref, refs = refs[0], refs[1:]
     begin_in, (a_ref, h_ref), refs = refs[:3], refs[3:5], refs[5:]
     now_in, outs = (refs[:3], refs[3:]) if stage else (begin_in, refs)
 
     joined, members = dev_in[0].shape
     half = members // 2
     rows, line = 2 * joined, joined // own
-    for step, dev_ref in enumerate(dev_in):
-        place = origin(lax.axis_index("tgt"), step, targets) * rows
-        dev = dev_ref[...].astype(jnp.float32)
-        for side, part in enumerate((dev, pltpu.roll(dev, half, 1))):
-            for far in range(line):
-                start = pl.multiple_of(place + (2 * far + side) * own, own)
-                all_dev[pl.ds(start, own)] = part[far * own : (far + 1) * own]
-    deviations = all_dev[...].astype(jnp.bfloat16)
     if stage == 0:
+        for step, dev_ref in enumerate(dev_in):
+            place_deviations(dev_ref, origin(lax.axis_index("tgt"), step, targets) * rows, own, all_dev)
+        deviations = all_dev[...].astype(jnp.bfloat16)
         dense_ref, outs = outs[-1], outs[:-1]
         width = dense_in[0].shape[1]
         for place, dense in zip(block_order(lax.axis_index("src"), dense_count), dense_in):
@@ -168,19 +197,16 @@
     else:
         dense_ref = dense_in[0]
 
+    if stage == 0:
+        total = jnp.dot(dense_ref[...], deviations, preferred_element_type=jnp.float32)
+    else:
+        total = early_ref[...] + product(stage, own, range(EARLY, targets), targets, dense_ref, dev_in, all_dev)
+    totals = [total[: total.shape[0] // 2], total[total.shape[0] // 2 :]]
     if stage < 2:
         mine, kept = slice(None), line
-        total = jnp.dot(dense_ref[...], deviations, preferred_element_type=jnp.float32)
-        totals = [total[:rows], total[rows:]]
     else:
         kept = 1
-        far = lax.axis_index("src") // 2
-        mine = pl.ds(pl.multiple_of(far * own, own), own)
-        start = pl.multiple_of(far * 2 * own, 2 * own)
-        totals = [
-            jnp.dot(dense_ref[pl.ds(first + start, 2 * own)], deviations, preferred_element_type=jnp.float32)
-            for first in (0, rows)
-        ]
+        mine = pl.ds(pl.multiple_of(lax.axis_index("src") // PAIR * own, own), own)
     change = []
     for total in totals:
         sides = [
@@ -259,7 +285,17 @@
     now = ()
     matrix_type = jax.ShapeDtypeStruct((2 * rows, sources * leaf_cols * block), jnp.bfloat16)
     for stage in range(3):
-        given = (*dense_blocks, *gather_target(dev), *begin, all_a, all_h, *now)
+        dev_blocks = gather_target(dev)
+        if stage:
+            product_rows = 2 * rows if stage < 2 else 4 * own
+            early = call(
+                functools.partial(early_kernel, stage, own, targets),
+                (floats(product_rows),),
+                (*dense_blocks, *dev_blocks[:EARLY]),
+                [pltpu.VMEM((rows * EARLY, members), jnp.float32)],
+            )
+            dev_blocks = (*dev_blocks[EARLY:], *early)
+        given = (*dense_blocks, *dev_blocks, *begin, all_a, all_h, *now)
         outs = ((wide,) * 3 + (dev_type,)) if stage < 2 else (floats(3 * own), floats(3 * own // 2))
         outs = outs + ((matrix_type,) if stage == 0 else ())
         results = call(

time: 43.2 us -> 43 us (level)
  waiting for transfers between devices: 14.6 us -> 14.1 us
    ppermute x9, waiting for transfers between devices: 7.6 us -> 7.1 us  [gather_target(): lax.ppermute(block, 'tgt', [(i, partner(i, step, targets)) for i in range...]
    pallas_call x7 -> x9, Pallas kernels: 4.08 us -> 4.4 us  [call(): pl.pallas_call(kernel, out_shape=tuple(outs), in_specs=[space] * len(give...]
  transfers between devices with their start and end apart: 21 -> 21, of which waited for: 9 -> 9; matrix products, arithmetic and copies ran while one was open for 0% -> 0% of each run, Pallas kernels for 0% -> 1%
where the time goes in v6:
time: 43 us; the launch traced here: 42.9 us
  starting transfers between devices  23.6 us (55%)
  waiting for transfers between devices  14.1 us (33%)
  Pallas kernels  4.4 us (10%)
  between operations  0.74 us (2%)
    ppermute x6, starting transfers between devices, along_line(): return lax.ppermute(block, 'src', moves)  9.48 us
    ppermute x6, starting transfers between devices, across_pair(): lax.ppermute(block, 'src', [(i, i ^ 1) for i in range(lax.axis_size('src'...  8.2 us
    ppermute x9, waiting for transfers between devices, gather_target(): lax.ppermute(block, 'tgt', [(i, partner(i, step, targets)) for i in range...  7.1 us
    ppermute x9, starting transfers between devices, gather_target(): lax.ppermute(block, 'tgt', [(i, partner(i, step, targets)) for i in range...  5.9 us
    pallas_call x9, Pallas kernels, call(): pl.pallas_call(kernel, out_shape=tuple(outs), in_specs=[space] * len(give...  4.4 us
    ppermute x6, waiting for transfers between devices, along_line(): return lax.ppermute(block, 'src', moves)  4.11 us
    ppermute x6, waiting for transfers between devices, across_pair(): lax.ppermute(block, 'src', [(i, i ^ 1) for i in range(lax.axis_size('src'...  2.86 us
  transfers between devices with their start and end apart: 21, of which 9 were waited for; matrix products, arithmetic and copies ran while one was open for 0% of the time, Pallas kernels for 1%

profile of v6, /device:TPU:0, one launch (start us, length us, event | category | flops | bytes accessed | tf_op | source)
XLA Modules:
  0.0 42.9 jit_solution(15084513406720641181)
XLA Ops:
  0.6 1.3 %shard_map.112 = (f32[160,128]{1,0:T(8,128)S(1)}, bf16[512,128]{1,0:T(8,128)(2,1)S(1)}) custom-call(s32[1,2]{1,0:T(1,128)} %bitcast.2, s32[1,2]{1,0:T(1,128)} %bitcast.3, bf16[2,1,128,128]{3,2,1,0:T(8,128)(2,1)} %refs_2_.1, bf16[2,1,128,128]{3,2,1,0:T(8,128)(2,1)} %refs_3_.1, f32[32,128]{1,0:T(8,128)} %refs_4_.1, f32[32,128]{1,0:T(8,128)} %refs_5_.1, ...), custom_call_target="tpu_custom_call" | custom-call | tf_op jit(solution)/shard_map/pallas_call | solution.py:239
  1.9 3.0 %collective-permute-start.7 = (f32[160,128]{1,0:T(8,128)S(1)}, f32[160,128]{1,0:T(8,128)S(1)}, u32[]{:S(2)}, u32[]{:S(2)}) collective-permute-start(f32[160,128]{1,0:T(8,128)S(1)} %get-tuple-element.25.mine_ref), channel_id=1, source_target_pairs={{0,1},{1,0},{2,3},{3,2},{4,5},{5,4},{6,7},{7,6},{8,9},{9,8},{10,11... | collective-permute-start | bytes 245768 | tf_op jit(solution)/shard_map/ppermute | solution.py:37
  5.0 3.0 %collective-permute-start.1 = (bf16[512,128]{1,0:T(8,128)(2,1)S(1)}, bf16[512,128]{1,0:T(8,128)(2,1)S(1)}, u32[]{:S(2)}, u32[]{:S(2)}) collective-permute-start(bf16[512,128]{1,0:T(8,128)(2,1)S(1)} %get-tuple-element.23.refs_0_), channel_id=1, source_target_pairs={{0,4},{1,5},{2,6},{3,7},{4,0},{5,1},{6,2},{7,3},{8,12},{9,13},{10,... | collective-permute-start | bytes 393224 | tf_op jit(solution)/shard_map/ppermute | solution.py:33
  8.0 1.6 %collective-permute-start = (bf16[512,128]{1,0:T(8,128)(2,1)S(1)}, bf16[512,128]{1,0:T(8,128)(2,1)S(1)}, u32[]{:S(2)}, u32[]{:S(2)}) collective-permute-start(bf16[512,128]{1,0:T(8,128)(2,1)S(1)} %get-tuple-element.23.refs_0_), channel_id=1, source_target_pairs={{0,2},{1,3},{2,0},{3,1},{4,6},{5,7},{6,4},{7,5},{8,10},{9,11},{10,... | collective-permute-start | bytes 393224 | tf_op jit(solution)/shard_map/ppermute | solution.py:33
  9.7 1.7 %collective-permute-start.9 = (f32[160,128]{1,0:T(8,128)S(1)}, f32[160,128]{1,0:T(8,128)S(1)}, u32[]{:S(2)}, u32[]{:S(2)}) collective-permute-start(f32[160,128]{1,0:T(8,128)S(1)} %shard_map.113.refs_0_), channel_id=1, source_target_pairs={{0,4},{1,5},{2,6},{3,7},{4,0},{5,1},{6,2},{7,3},{8,12},{9,13},{10,... | collective-permute-start | bytes 245768 | tf_op jit(solution)/shard_map/ppermute | solution.py:33
  11.4 1.6 %collective-permute-start.8 = (f32[160,128]{1,0:T(8,128)S(1)}, f32[160,128]{1,0:T(8,128)S(1)}, u32[]{:S(2)}, u32[]{:S(2)}) collective-permute-start(f32[160,128]{1,0:T(8,128)S(1)} %shard_map.113.refs_0_), channel_id=1, source_target_pairs={{0,2},{1,3},{2,0},{3,1},{4,6},{5,7},{6,4},{7,5},{8,10},{9,11},{10,... | collective-permute-start | bytes 245768 | tf_op jit(solution)/shard_map/ppermute | solution.py:33
  13.1 2.5 %collective-permute-done.1.refs_2_ = bf16[512,128]{1,0:T(8,128)(2,1)S(1)} collective-permute-done((bf16[512,128]{1,0:T(8,128)(2,1)S(1)}, bf16[512,128]{1,0:T(8,128)(2,1)S(1)}, u32[]{:S(2)}, u32[]{:S(2)}) %collective-permute-start.1) | collective-permute-done | bytes 131104 | tf_op jit(solution)/shard_map/ppermute | solution.py:33
  15.6 0.3 collective-permute-start.3
  15.9 1.5 %collective-permute-start.5 = (bf16[512,128]{1,0:T(8,128)(2,1)S(1)}, bf16[512,128]{1,0:T(8,128)(2,1)S(1)}, u32[]{:S(2)}, u32[]{:S(2)}) collective-permute-start(bf16[512,128]{1,0:T(8,128)(2,1)S(1)} %collective-permute-done.1.refs_2_), channel_id=1, source_target_pairs={{0,1},{1,0},{2,3},{3,2},{4,5},{5,4},{6,7},{7,6},{8,9},{9,8},{10,11... | collective-permute-start | bytes 393224 | tf_op jit(solution)/shard_map/ppermute | solution.py:37
  17.4 1.0 %collective-permute-start.4 = (bf16[512,128]{1,0:T(8,128)(2,1)S(1)}, bf16[512,128]{1,0:T(8,128)(2,1)S(1)}, u32[]{:S(2)}, u32[]{:S(2)}) collective-permute-start(bf16[512,128]{1,0:T(8,128)(2,1)S(1)} %collective-permute-done.refs_1_), channel_id=1, source_target_pairs={{0,1},{1,0},{2,3},{3,2},{4,5},{5,4},{6,7},{7,6},{8,9},{9,8},{10,11... | collective-permute-start | bytes 393224 | tf_op jit(solution)/shard_map/ppermute | solution.py:37
  18.4 1.2 %collective-permute-start.10 = (f32[160,128]{1,0:T(8,128)S(1)}, f32[160,128]{1,0:T(8,128)S(1)}, u32[]{:S(2)}, u32[]{:S(2)}) collective-permute-start(f32[160,128]{1,0:T(8,128)S(1)} %collective-permute-done.9.refs_2_), channel_id=1, source_target_pairs={{0,2},{1,3},{2,0},{3,1},{4,6},{5,7},{6,4},{7,5},{8,10},{9,11},{10,... | collective-permute-start | bytes 245768 | tf_op jit(solution)/shard_map/ppermute | solution.py:33
  19.7 1.6 %collective-permute-done.3.refs_3_ = bf16[512,128]{1,0:T(8,128)(2,1)S(1)} collective-permute-done((bf16[512,128]{1,0:T(8,128)(2,1)S(1)}, bf16[512,128]{1,0:T(8,128)(2,1)S(1)}, u32[]{:S(2)}, u32[]{:S(2)}) %collective-permute-start.3) | collective-permute-done | bytes 131104 | tf_op jit(solution)/shard_map/ppermute | solution.py:33
  21.3 1.5 %collective-permute-start.6 = (bf16[512,128]{1,0:T(8,128)(2,1)S(1)}, bf16[512,128]{1,0:T(8,128)(2,1)S(1)}, u32[]{:S(2)}, u32[]{:S(2)}) collective-permute-start(bf16[512,128]{1,0:T(8,128)(2,1)S(1)} %collective-permute-done.3.refs_3_), channel_id=1, source_target_pairs={{0,1},{1,0},{2,3},{3,2},{4,5},{5,4},{6,7},{7,6},{8,9},{9,8},{10,11... | collective-permute-start | bytes 393224 | tf_op jit(solution)/shard_map/ppermute | solution.py:37
  23.0 1.6 %collective-permute-start.12 = (bf16[128,128]{1,0:T(8,128)(2,1)S(1)}, bf16[128,128]{1,0:T(8,128)(2,1)S(1)}, u32[]{:S(2)}, u32[]{:S(2)}) collective-permute-start(bf16[128,128]{1,0:T(8,128)(2,1)S(1)} %get-tuple-element.26.refs_8_), channel_id=1, source_target_pairs={{0,16},{8,24},{16,0},{24,8},{1,17},{9,25},{17,1},{25,9},{2,18},{10... | collective-permute-start | bytes 98312 | tf_op jit(solution)/shard_map/ppermute | solution.py:56
  24.6 0.3 collective-permute-start.11
  24.9 1.7 %collective-permute-done.13.refs_11_ = bf16[128,128]{1,0:T(8,128)(2,1)S(1)} collective-permute-done((bf16[128,128]{1,0:T(8,128)(2,1)S(1)}, bf16[128,128]{1,0:T(8,128)(2,1)S(1)}, u32[]{:S(2)}, u32[]{:S(2)}) %collective-permute-start.13) | collective-permute-done | bytes 32800 | tf_op jit(solution)/shard_map/ppermute | solution.py:56
  26.6 0.4 collective-permute-done.12.refs_10_
  27.1 0.9 %shard_map.115 = (f32[128,128]{1,0:T(8,128)S(1)}, f32[128,128]{1,0:T(8,128)S(1)}, f32[128,128]{1,0:T(8,128)S(1)}, bf16[128,128]{1,0:T(8,128)(2,1)S(1)}, bf16[512,1024]{1,0:T(8,128)(2,1)S(1)}) custom-call(bf16[512,128]{1,0:T(8,128)(2,1)S(1)} %get-tuple-element.23.refs_0_, bf16[512,128]{1,0:T(8,128)(2,1)S(1)} %collective-permute-done.refs_1_, ...), custom_call_target="tpu_custom_call" | custom-call | tf_op jit(solution)/shard_map/pallas_call | solution.py:239
  27.9 1.0 %collective-permute-start.16 = (bf16[128,128]{1,0:T(8,128)(2,1)S(1)}, bf16[128,128]{1,0:T(8,128)(2,1)S(1)}, u32[]{:S(2)}, u32[]{:S(2)}) collective-permute-start(bf16[128,128]{1,0:T(8,128)(2,1)S(1)} %get-tuple-element.33.refs_0_), channel_id=1, source_target_pairs={{0,24},{8,16},{16,8},{24,0},{1,25},{9,17},{17,9},{25,1},{2,26},{10... | collective-permute-start | bytes 98312 | tf_op jit(solution)/shard_map/ppermute | solution.py:56
  29.0 1.0 %collective-permute-start.15 = (bf16[128,128]{1,0:T(8,128)(2,1)S(1)}, bf16[128,128]{1,0:T(8,128)(2,1)S(1)}, u32[]{:S(2)}, u32[]{:S(2)}) collective-permute-start(bf16[128,128]{1,0:T(8,128)(2,1)S(1)} %get-tuple-element.33.refs_0_), channel_id=1, source_target_pairs={{0,16},{8,24},{16,0},{24,8},{1,17},{9,25},{17,1},{25,9},{2,18},{10... | collective-permute-start | bytes 98312 | tf_op jit(solution)/shard_map/ppermute | solution.py:56
  30.0 0.3 shard_map.116.refs_4_
  30.3 1.1 %collective-permute-done.16.refs_3_ = bf16[128,128]{1,0:T(8,128)(2,1)S(1)} collective-permute-done((bf16[128,128]{1,0:T(8,128)(2,1)S(1)}, bf16[128,128]{1,0:T(8,128)(2,1)S(1)}, u32[]{:S(2)}, u32[]{:S(2)}) %collective-permute-start.16) | collective-permute-done | bytes 32800 | tf_op jit(solution)/shard_map/ppermute | solution.py:56
  31.4 1.6 %collective-permute-done.15.refs_2_ = bf16[128,128]{1,0:T(8,128)(2,1)S(1)} collective-permute-done((bf16[128,128]{1,0:T(8,128)(2,1)S(1)}, bf16[128,128]{1,0:T(8,128)(2,1)S(1)}, u32[]{:S(2)}, u32[]{:S(2)}) %collective-permute-start.15) | collective-permute-done | bytes 32800 | tf_op jit(solution)/shard_map/ppermute | solution.py:56
  32.9 0.5 %shard_map.117 = (f32[128,128]{1,0:T(8,128)S(1)}, f32[128,128]{1,0:T(8,128)S(1)}, f32[128,128]{1,0:T(8,128)S(1)}, bf16[128,128]{1,0:T(8,128)(2,1)S(1)}) custom-call(bf16[512,1024]{1,0:T(8,128)(2,1)S(1)} %get-tuple-element.32.dense_ref.refs_0_, bf16[128,128]{1,0:T(8,128)(2,1)S(1)} %collective-permute-done.14.refs_1_, ...), custom_call_target="tpu_custom_call" | custom-call | tf_op jit(solution)/shard_map/pallas_call | solution.py:239
  33.6 1.4 %collective-permute-start.18 = (bf16[128,128]{1,0:T(8,128)(2,1)S(1)}, bf16[128,128]{1,0:T(8,128)(2,1)S(1)}, u32[]{:S(2)}, u32[]{:S(2)}) collective-permute-start(bf16[128,128]{1,0:T(8,128)(2,1)S(1)} %get-tuple-element.37.refs_0_), channel_id=1, source_target_pairs={{0,16},{8,24},{16,0},{24,8},{1,17},{9,25},{17,1},{25,9},{2,18},{10... | collective-permute-start | bytes 98312 | tf_op jit(solution)/shard_map/ppermute | solution.py:56
  35.0 0.4 %collective-permute-start.17 = (bf16[128,128]{1,0:T(8,128)(2,1)S(1)}, bf16[128,128]{1,0:T(8,128)(2,1)S(1)}, u32[]{:S(2)}, u32[]{:S(2)}) collective-permute-start(bf16[128,128]{1,0:T(8,128)(2,1)S(1)} %get-tuple-element.37.refs_0_), channel_id=1, source_target_pairs={{0,8},{8,0},{16,24},{24,16},{1,9},{9,1},{17,25},{25,17},{2,10},{10... | collective-permute-start | bytes 98312 | tf_op jit(solution)/shard_map/ppermute | solution.py:56
  35.6 1.6 %collective-permute-done.19.refs_3_ = bf16[128,128]{1,0:T(8,128)(2,1)S(1)} collective-permute-done((bf16[128,128]{1,0:T(8,128)(2,1)S(1)}, bf16[128,128]{1,0:T(8,128)(2,1)S(1)}, u32[]{:S(2)}, u32[]{:S(2)}) %collective-permute-start.19) | collective-permute-done | bytes 32800 | tf_op jit(solution)/shard_map/ppermute | solution.py:56
  37.2 0.7 %collective-permute-done.18.refs_2_ = bf16[128,128]{1,0:T(8,128)(2,1)S(1)} collective-permute-done((bf16[128,128]{1,0:T(8,128)(2,1)S(1)}, bf16[128,128]{1,0:T(8,128)(2,1)S(1)}, u32[]{:S(2)}, u32[]{:S(2)}) %collective-permute-start.18) | collective-permute-done | bytes 32800 | tf_op jit(solution)/shard_map/ppermute | solution.py:56
  37.9 0.4 shard_map.119
  38.3 1.0 %collective-permute-start.20 = (f32[48,128]{1,0:T(8,128)S(1)}, f32[48,128]{1,0:T(8,128)S(1)}, u32[]{:S(2)}, u32[]{:S(2)}) collective-permute-start(f32[48,128]{1,0:T(8,128)S(1)} %get-tuple-element.42), channel_id=1, source_target_pairs={{0,1},{1,0},{2,3},{3,2},{4,5},{5,4},{6,7},{7,6},{8,9},{9,8},{10,11... | collective-permute-start | bytes 73736 | tf_op jit(solution)/shard_map/ppermute | solution.py:37
  39.3 2.8 %collective-permute-done.20.theirs_ref = f32[48,128]{1,0:T(8,128)S(1)} collective-permute-done((f32[48,128]{1,0:T(8,128)S(1)}, f32[48,128]{1,0:T(8,128)S(1)}, u32[]{:S(2)}, u32[]{:S(2)}) %collective-permute-start.20) | collective-permute-done | bytes 24608 | tf_op jit(solution)/shard_map/ppermute | solution.py:37
  42.2 0.7 %shard_map.120 = (f32[32,128]{1,0:T(8,128)}, f32[32,128]{1,0:T(8,128)}, f32[32,128]{1,0:T(8,128)}) custom-call(f32[96,128]{1,0:T(8,128)S(1)} %get-tuple-element.41.mine_ref, f32[48,128]{1,0:T(8,128)S(1)} %collective-permute-done.20.theirs_ref), custom_call_target="tpu_custom_call" | custom-call | tf_op jit(solution)/shard_map/pallas_call | solution.py:239
  (23 shorter events, 0.8 us)
Async XLA Ops:
  1.9 7.7 %collective-permute-start.7 = (f32[160,128]{1,0:T(8,128)S(1)}, f32[160,128]{1,0:T(8,128)S(1)}, u32[]{:S(2)}, u32[]{:S(2)}) collective-permute-start(f32[160,128]{1,0:T(8,128)S(1)} %get-tuple-element.25.mine_ref), channel_id=1, source_target_pairs={{0,1},{1,0},{2,3},{3,2},{4,5},{5,4},{6,7},{7,6},{8,9},{9,8},{10,11... | collective-permute-start | bytes 245768 | tf_op jit(solution)/shard_map/ppermute | solution.py:37
  4.9 8.2 %collective-permute-start.2 = (bf16[512,128]{1,0:T(8,128)(2,1)S(1)}, bf16[512,128]{1,0:T(8,128)(2,1)S(1)}, u32[]{:S(2)}, u32[]{:S(2)}) collective-permute-start(bf16[512,128]{1,0:T(8,128)(2,1)S(1)} %get-tuple-element.23.refs_0_), channel_id=1, source_target_pairs={{0,1},{1,0},{2,3},{3,2},{4,5},{5,4},{6,7},{7,6},{8,9},{9,8},{10,11... | collective-permute-start | bytes 393224 | tf_op jit(solution)/shard_map/ppermute | solution.py:37
  5.0 10.6 %collective-permute-start.1 = (bf16[512,128]{1,0:T(8,128)(2,1)S(1)}, bf16[512,128]{1,0:T(8,128)(2,1)S(1)}, u32[]{:S(2)}, u32[]{:S(2)}) collective-permute-start(bf16[512,128]{1,0:T(8,128)(2,1)S(1)} %get-tuple-element.23.refs_0_), channel_id=1, source_target_pairs={{0,4},{1,5},{2,6},{3,7},{4,0},{5,1},{6,2},{7,3},{8,12},{9,13},{10,... | collective-permute-start | bytes 393224 | tf_op jit(solution)/shard_map/ppermute | solution.py:33
  8.0 9.3 %collective-permute-start = (bf16[512,128]{1,0:T(8,128)(2,1)S(1)}, bf16[512,128]{1,0:T(8,128)(2,1)S(1)}, u32[]{:S(2)}, u32[]{:S(2)}) collective-permute-start(bf16[512,128]{1,0:T(8,128)(2,1)S(1)} %get-tuple-element.23.refs_0_), channel_id=1, source_target_pairs={{0,2},{1,3},{2,0},{3,1},{4,6},{5,7},{6,4},{7,5},{8,10},{9,11},{10,... | collective-permute-start | bytes 393224 | tf_op jit(solution)/shard_map/ppermute | solution.py:33
  9.7 8.7 %collective-permute-start.9 = (f32[160,128]{1,0:T(8,128)S(1)}, f32[160,128]{1,0:T(8,128)S(1)}, u32[]{:S(2)}, u32[]{:S(2)}) collective-permute-start(f32[160,128]{1,0:T(8,128)S(1)} %shard_map.113.refs_0_), channel_id=1, source_target_pairs={{0,4},{1,5},{2,6},{3,7},{4,0},{5,1},{6,2},{7,3},{8,12},{9,13},{10,... | collective-permute-start | bytes 245768 | tf_op jit(solution)/shard_map/ppermute | solution.py:33
  11.4 8.2 %collective-permute-start.8 = (f32[160,128]{1,0:T(8,128)S(1)}, f32[160,128]{1,0:T(8,128)S(1)}, u32[]{:S(2)}, u32[]{:S(2)}) collective-permute-start(f32[160,128]{1,0:T(8,128)S(1)} %shard_map.113.refs_0_), channel_id=1, source_target_pairs={{0,2},{1,3},{2,0},{3,1},{4,6},{5,7},{6,4},{7,5},{8,10},{9,11},{10,... | collective-permute-start | bytes 245768 | tf_op jit(solution)/shard_map/ppermute | solution.py:33
  15.6 5.7 %collective-permute-start.3 = (bf16[512,128]{1,0:T(8,128)(2,1)S(1)}, bf16[512,128]{1,0:T(8,128)(2,1)S(1)}, u32[]{:S(2)}, u32[]{:S(2)}) collective-permute-start(bf16[512,128]{1,0:T(8,128)(2,1)S(1)} %collective-permute-done.1.refs_2_), channel_id=1, source_target_pairs={{0,2},{1,3},{2,0},{3,1},{4,6},{5,7},{6,4},{7,5},{8,10},{9,11},{10,... | collective-permute-start | bytes 393224 | tf_op jit(solution)/shard_map/ppermute | solution.py:33
  15.9 8.7 %collective-permute-start.5 = (bf16[512,128]{1,0:T(8,128)(2,1)S(1)}, bf16[512,128]{1,0:T(8,128)(2,1)S(1)}, u32[]{:S(2)}, u32[]{:S(2)}) collective-permute-start(bf16[512,128]{1,0:T(8,128)(2,1)S(1)} %collective-permute-done.1.refs_2_), channel_id=1, source_target_pairs={{0,1},{1,0},{2,3},{3,2},{4,5},{5,4},{6,7},{7,6},{8,9},{9,8},{10,11... | collective-permute-start | bytes 393224 | tf_op jit(solution)/shard_map/ppermute | solution.py:37
  17.4 7.5 %collective-permute-start.4 = (bf16[512,128]{1,0:T(8,128)(2,1)S(1)}, bf16[512,128]{1,0:T(8,128)(2,1)S(1)}, u32[]{:S(2)}, u32[]{:S(2)}) collective-permute-start(bf16[512,128]{1,0:T(8,128)(2,1)S(1)} %collective-permute-done.refs_1_), channel_id=1, source_target_pairs={{0,1},{1,0},{2,3},{3,2},{4,5},{5,4},{6,7},{7,6},{8,9},{9,8},{10,11... | collective-permute-start | bytes 393224 | tf_op jit(solution)/shard_map/ppermute | solution.py:37
  18.4 4.4 %collective-permute-start.10 = (f32[160,128]{1,0:T(8,128)S(1)}, f32[160,128]{1,0:T(8,128)S(1)}, u32[]{:S(2)}, u32[]{:S(2)}) collective-permute-start(f32[160,128]{1,0:T(8,128)S(1)} %collective-permute-done.9.refs_2_), channel_id=1, source_target_pairs={{0,2},{1,3},{2,0},{3,1},{4,6},{5,7},{6,4},{7,5},{8,10},{9,11},{10,... | collective-permute-start | bytes 245768 | tf_op jit(solution)/shard_map/ppermute | solution.py:33
  21.3 5.8 %collective-permute-start.6 = (bf16[512,128]{1,0:T(8,128)(2,1)S(1)}, bf16[512,128]{1,0:T(8,128)(2,1)S(1)}, u32[]{:S(2)}, u32[]{:S(2)}) collective-permute-start(bf16[512,128]{1,0:T(8,128)(2,1)S(1)} %collective-permute-done.3.refs_3_), channel_id=1, source_target_pairs={{0,1},{1,0},{2,3},{3,2},{4,5},{5,4},{6,7},{7,6},{8,9},{9,8},{10,11... | collective-permute-start | bytes 393224 | tf_op jit(solution)/shard_map/ppermute | solution.py:37
  22.9 3.7 %collective-permute-start.13 = (bf16[128,128]{1,0:T(8,128)(2,1)S(1)}, bf16[128,128]{1,0:T(8,128)(2,1)S(1)}, u32[]{:S(2)}, u32[]{:S(2)}) collective-permute-start(bf16[128,128]{1,0:T(8,128)(2,1)S(1)} %get-tuple-element.26.refs_8_), channel_id=1, source_target_pairs={{0,24},{8,16},{16,8},{24,0},{1,25},{9,17},{17,9},{25,1},{2,26},{10... | collective-permute-start | bytes 98312 | tf_op jit(solution)/shard_map/ppermute | solution.py:56
  23.0 4.0 %collective-permute-start.12 = (bf16[128,128]{1,0:T(8,128)(2,1)S(1)}, bf16[128,128]{1,0:T(8,128)(2,1)S(1)}, u32[]{:S(2)}, u32[]{:S(2)}) collective-permute-start(bf16[128,128]{1,0:T(8,128)(2,1)S(1)} %get-tuple-element.26.refs_8_), channel_id=1, source_target_pairs={{0,16},{8,24},{16,0},{24,8},{1,17},{9,25},{17,1},{25,9},{2,18},{10... | collective-permute-start | bytes 98312 | tf_op jit(solution)/shard_map/ppermute | solution.py:56
  24.6 2.4 %collective-permute-start.11 = (bf16[128,128]{1,0:T(8,128)(2,1)S(1)}, bf16[128,128]{1,0:T(8,128)(2,1)S(1)}, u32[]{:S(2)}, u32[]{:S(2)}) collective-permute-start(bf16[128,128]{1,0:T(8,128)(2,1)S(1)} %get-tuple-element.26.refs_8_), channel_id=1, source_target_pairs={{0,8},{8,0},{16,24},{24,16},{1,9},{9,1},{17,25},{25,17},{2,10},{10... | collective-permute-start | bytes 98312 | tf_op jit(solution)/shard_map/ppermute | solution.py:56
  27.9 3.4 %collective-permute-start.16 = (bf16[128,128]{1,0:T(8,128)(2,1)S(1)}, bf16[128,128]{1,0:T(8,128)(2,1)S(1)}, u32[]{:S(2)}, u32[]{:S(2)}) collective-permute-start(bf16[128,128]{1,0:T(8,128)(2,1)S(1)} %get-tuple-element.33.refs_0_), channel_id=1, source_target_pairs={{0,24},{8,16},{16,8},{24,0},{1,25},{9,17},{17,9},{25,1},{2,26},{10... | collective-permute-start | bytes 98312 | tf_op jit(solution)/shard_map/ppermute | solution.py:56
  29.0 3.9 %collective-permute-start.15 = (bf16[128,128]{1,0:T(8,128)(2,1)S(1)}, bf16[128,128]{1,0:T(8,128)(2,1)S(1)}, u32[]{:S(2)}, u32[]{:S(2)}) collective-permute-start(bf16[128,128]{1,0:T(8,128)(2,1)S(1)} %get-tuple-element.33.refs_0_), channel_id=1, source_target_pairs={{0,16},{8,24},{16,0},{24,8},{1,17},{9,25},{17,1},{25,9},{2,18},{10... | collective-permute-start | bytes 98312 | tf_op jit(solution)/shard_map/ppermute | solution.py:56
  30.0 2.9 %collective-permute-start.14 = (bf16[128,128]{1,0:T(8,128)(2,1)S(1)}, bf16[128,128]{1,0:T(8,128)(2,1)S(1)}, u32[]{:S(2)}, u32[]{:S(2)}) collective-permute-start(bf16[128,128]{1,0:T(8,128)(2,1)S(1)} %get-tuple-element.33.refs_0_), channel_id=1, source_target_pairs={{0,8},{8,0},{16,24},{24,16},{1,9},{9,1},{17,25},{25,17},{2,10},{10... | collective-permute-start | bytes 98312 | tf_op jit(solution)/shard_map/ppermute | solution.py:56
  33.5 3.8 %collective-permute-start.19 = (bf16[128,128]{1,0:T(8,128)(2,1)S(1)}, bf16[128,128]{1,0:T(8,128)(2,1)S(1)}, u32[]{:S(2)}, u32[]{:S(2)}) collective-permute-start(bf16[128,128]{1,0:T(8,128)(2,1)S(1)} %get-tuple-element.37.refs_0_), channel_id=1, source_target_pairs={{0,24},{8,16},{16,8},{24,0},{1,25},{9,17},{17,9},{25,1},{2,26},{10... | collective-permute-start | bytes 98312 | tf_op jit(solution)/shard_map/ppermute | solution.py:56
  33.6 4.3 %collective-permute-start.18 = (bf16[128,128]{1,0:T(8,128)(2,1)S(1)}, bf16[128,128]{1,0:T(8,128)(2,1)S(1)}, u32[]{:S(2)}, u32[]{:S(2)}) collective-permute-start(bf16[128,128]{1,0:T(8,128)(2,1)S(1)} %get-tuple-element.37.refs_0_), channel_id=1, source_target_pairs={{0,16},{8,24},{16,0},{24,8},{1,17},{9,25},{17,1},{25,9},{2,18},{10... | collective-permute-start | bytes 98312 | tf_op jit(solution)/shard_map/ppermute | solution.py:56
  35.0 2.9 %collective-permute-start.17 = (bf16[128,128]{1,0:T(8,128)(2,1)S(1)}, bf16[128,128]{1,0:T(8,128)(2,1)S(1)}, u32[]{:S(2)}, u32[]{:S(2)}) collective-permute-start(bf16[128,128]{1,0:T(8,128)(2,1)S(1)} %get-tuple-element.37.refs_0_), channel_id=1, source_target_pairs={{0,8},{8,0},{16,24},{24,16},{1,9},{9,1},{17,25},{25,17},{2,10},{10... | collective-permute-start | bytes 98312 | tf_op jit(solution)/shard_map/ppermute | solution.py:56
  38.3 3.9 %collective-permute-start.20 = (f32[48,128]{1,0:T(8,128)S(1)}, f32[48,128]{1,0:T(8,128)S(1)}, u32[]{:S(2)}, u32[]{:S(2)}) collective-permute-start(f32[48,128]{1,0:T(8,128)S(1)} %get-tuple-element.42), channel_id=1, source_target_pairs={{0,1},{1,0},{2,3},{3,2},{4,5},{5,4},{6,7},{7,6},{8,9},{9,8},{10,11... | collective-permute-start | bytes 73736 | tf_op jit(solution)/shard_map/ppermute | solution.py:37
